TPU v7x, 256 devices: a whole 4x4x8 slice. The times are simulated.
256 devices in a mesh: band: 16 (over x, y), mesh: 8 (over z), rep: 2 (over core).
Axes of the slice: x: 4, y: 4, z: 8, core: 2. Of those that a mesh axis runs over, the one named last changes fastest.
Arguments:
- grid_latent: bfloat16 [2, 65536, 512], P('rep', ('band', 'mesh')), may hold values from -6 to 6
- mesh_latent: bfloat16 [2, 16384, 512], P('rep', ('band', 'mesh')), may hold values from -6 to 6
- edge_latent: bfloat16 [2, 131072, 512], P('rep', ('band', 'mesh')), may hold values from -6 to 6
- mesh_cotangent: bfloat16 [2, 16384, 512], P('rep', ('band', 'mesh')), may hold values from -6 to 6
- w_first: bfloat16 [1536, 512], replicated, may hold values from -0.15625 to 0.15625
- w_second: bfloat16 [512, 512], replicated, may hold values from -0.25 to 0.25
- norm_gain: float32 [512], replicated, may hold values from 0.1 to 1.9
- senders: int32 [131072], P(('band', 'mesh')), may hold values from 0 to 65535, as said below
- receivers: int32 [131072], P(('band', 'mesh')), may hold values from 0 to 16383, as said below
- live_counts: int32 [128], P(('band', 'mesh')), may hold values from 512 to 1024, as said below
Outputs:
- grid_grad: bfloat16 [2, 65536, 512], P('rep', ('band', 'mesh'))
- mesh_grad: float32 [2, 16384, 512], P('rep', ('band', 'mesh'))
- edge_grad: bfloat16 [2, 131072, 512], P('rep', ('band', 'mesh'))
- first_grad: float32 [1536, 512], replicated
- second_grad: float32 [512, 512], replicated
- gain_grad: float32 [512], replicated
Inputs may be any that keep to these rules, and one draw needn't show every extreme that they name: `senders`: A slot of sub-band k (slots k * 1024 to (k + 1) * 1024 - 1) names a grid node of that sub-band, k * 512 to (k + 1) * 512 - 1. `receivers`: A slot of sub-band k names a mesh node of sub-bands k - 1, k or k + 1, that is (k - 1) * 128 to (k + 2) * 128 - 1, within the mesh. `live_counts`: some sub-band has all its 1024 slots live.
All inputs are finite; a program needn't handle non-finite values.
Results may differ from a plain program's by a relative error of at most 0.012.
Values may be sent and summed in bfloat16 or wider, within the bound.
No kernel may reach another device: no remote copies, remote signals or barrier semaphores. Data moves between devices by JAX's collectives and lax.ppermute only.
A program may use at most 64 MiB of HBM per device.

v0:
```python
import math

import jax
import jax.numpy as jnp
from jax import lax
from jax.sharding import PartitionSpec as P

NORM_EPS = 1e-05


def passed_along(value, axis, steps):
    count = lax.axis_size(axis)
    leading, last = (max(0, -steps), min(count, count - steps))
    return lax.ppermute(value, axis, [(source, source + steps) for source in range(leading, last)])


def padded(shard, sides, width):
    for axis, dim in sides:
        peers, length = (lax.axis_size(axis), shard.shape[dim])
        up = [(i, (i + 1) % peers) for i in range(peers - 1)]
        down = [(j, i) for i, j in up]
        last = lax.slice_in_dim(shard, length - width, length, axis=dim)
        leading = lax.slice_in_dim(shard, 0, width, axis=dim)
        before = lax.ppermute(last, axis, up)
        after = lax.ppermute(leading, axis, down)
        shard = jnp.concatenate([before, shard, after], axis=dim)
    return shard


def contract_rows(left, right):
    return lax.dot_general(
        left, right, (((0,), (0,)), ((), ())), preferred_element_type=jnp.float32
    )


def contract_cols(left, right, accuracy=None):
    return lax.dot_general(
        left,
        right,
        (((1,), (1,)), ((), ())),
        precision=accuracy,
        preferred_element_type=jnp.float32,
    )


def onehot_table(indices, width):
    return (indices[:, None] == lax.iota(jnp.int32, width)[None, :]).astype(jnp.bfloat16)


def pick_rows(table, rows):
    return jnp.dot(table, rows, preferred_element_type=jnp.float32).astype(jnp.bfloat16)


def gather_sums(table, terms):
    upper = terms.astype(jnp.bfloat16)
    lower = (terms - upper.astype(jnp.float32)).astype(jnp.bfloat16)
    return contract_rows(table, upper) + contract_rows(table, lower)


def edge_backward(features, cotangent, live_mask, w_first, w_second, norm_gain):
    pre_act = jnp.dot(features, w_first, preferred_element_type=jnp.float32)
    hidden = jax.nn.silu(pre_act).astype(jnp.bfloat16)
    output = jnp.dot(hidden, w_second, preferred_element_type=jnp.float32)
    centered = output - jnp.mean(output, axis=1, keepdims=True)
    inverse = lax.rsqrt(jnp.mean(centered * centered, axis=1, keepdims=True) + NORM_EPS)
    normed = centered * inverse
    upstream = jnp.where(live_mask[:, None], cotangent.astype(jnp.float32), jnp.float32(0.0))
    gain_term = jnp.sum(upstream * normed, axis=0)
    scaled = upstream * norm_gain
    grad_output = (
        inverse
        * (
            scaled
            - jnp.mean(scaled, axis=1, keepdims=True)
            - normed * jnp.mean(scaled * normed, axis=1, keepdims=True)
        )
    ).astype(jnp.bfloat16)
    second_term = contract_rows(hidden, grad_output)
    grad_hidden = contract_cols(grad_output, w_second)
    sigmoid = jax.nn.sigmoid(pre_act)
    grad_pre = (grad_hidden * sigmoid * (1.0 + pre_act * (1.0 - sigmoid))).astype(jnp.bfloat16)
    first_term = contract_rows(features, grad_pre)
    return (grad_pre, first_term, second_term, gain_term)


def return_rims(terms, rows_mesh):
    from_above = passed_along(terms[:rows_mesh].astype(jnp.bfloat16), ("band", "mesh"), -1).astype(
        jnp.float32
    )
    from_below = passed_along(
        terms[2 * rows_mesh :].astype(jnp.bfloat16), ("band", "mesh"), 1
    ).astype(jnp.float32)
    return terms[rows_mesh : 2 * rows_mesh] + from_above + from_below


def per_device(
    grid_latent,
    mesh_latent,
    edge_latent,
    mesh_cotangent,
    w_first,
    w_second,
    norm_gain,
    senders,
    receivers,
    live_counts,
):
    model_width = w_second.shape[0]
    rows_grid = grid_latent.shape[1]
    rows_mesh = mesh_latent.shape[1]
    slot_count = senders.shape[0]
    shard_index = lax.axis_index(("band", "mesh"))
    stacked = jnp.concatenate([mesh_latent, mesh_cotangent], axis=2)
    nearby = padded(stacked, ((("band", "mesh"), 1),), rows_mesh)[0]
    send_table = onehot_table(senders - shard_index * rows_grid, rows_grid)
    recv_table = onehot_table(receivers - (shard_index - 1) * rows_mesh, 3 * rows_mesh)
    picked = pick_rows(recv_table, nearby)
    features = jnp.concatenate(
        [edge_latent[0], pick_rows(send_table, grid_latent[0]), picked[:, :model_width]], axis=1
    )
    live_mask = lax.iota(jnp.int32, slot_count) < live_counts[0]
    grad_pre, first_term, second_term, gain_term = edge_backward(
        features, picked[:, model_width:], live_mask, w_first, w_second, norm_gain
    )
    devices = lax.axis_size("band") * lax.axis_size("mesh") * lax.axis_size("rep")
    factor = 1.0 / math.sqrt(slot_count * devices)
    first_total, second_total, gain_total = lax.psum(
        (first_term, second_term, gain_term), ("band", "mesh", "rep")
    )
    grad_features = contract_cols(grad_pre, w_first)
    grad_front = grad_features[:, : 2 * model_width]
    mesh_terms = gather_sums(recv_table, grad_features[:, 2 * model_width :])
    mesh_grad = return_rims(mesh_terms, rows_mesh)
    edge_grad = grad_front[:, :model_width].astype(jnp.bfloat16)
    grid_grad = gather_sums(send_table, grad_front[:, model_width:]).astype(jnp.bfloat16)
    return (
        grid_grad[None],
        mesh_grad[None],
        edge_grad[None],
        first_total * factor,
        second_total * factor,
        gain_total * factor,
    )


def solution(mesh):
    in_specs = (
        P("rep", ("band", "mesh"), None),
        P("rep", ("band", "mesh"), None),
        P("rep", ("band", "mesh"), None),
        P("rep", ("band", "mesh"), None),
        P(),
        P(),
        P(),
        P(("band", "mesh")),
        P(("band", "mesh")),
        P(("band", "mesh")),
    )
    out_specs = (
        P("rep", ("band", "mesh"), None),
        P("rep", ("band", "mesh"), None),
        P("rep", ("band", "mesh"), None),
        P(),
        P(),
        P(),
    )
    return jax.shard_map(
        per_device, mesh=mesh, in_specs=in_specs, out_specs=out_specs, check_vma=False
    )
```

profile of v0, /device:TPU:1, one launch (start us, length us, event | category | flops | bytes accessed | tf_op | source)
XLA Modules:
  0.0 328.2 jit_solution(12541836803715100547)
XLA Ops:
  7.3 1.0 constant_dynamic-update-slice_fusion.1
  8.3 0.9 constant_dynamic-update-slice_fusion
  9.2 1.3 collective-permute-start.1
  10.5 5.7 %collective-permute-start = (bf16[1,128,1024]{2,1,0:T(8,128)(2,1)S(1)}, bf16[1,128,1024]{2,1,0:T(8,128)(2,1)}, u32[]{:S(2)}, u32[]{:S(2)}) collective-permute-start(bf16[1,128,1024]{2,1,0:T(8,128)(2,1)S(1)} %constant_dynamic-update-slice_fusion), channel_id=1, source_target_pairs={{0,2},{2,4},{4,6},{6,8},{8,10},{10,12},{12,14},{14,16},{16,18},{18... | collective-permute-start | bytes 786440 | tf_op jit(solution)/shard_map/ppermute | solution.py:24
  16.9 1.5 copy.16
  18.5 0.9 fusion.7
  19.4 2.5 convolution_convert_fusion
  22.0 2.1 multiply_convert_fusion.2
  26.8 1.7 fusion.35
  28.5 1.3 multiply_convert_fusion
  29.9 1.0 copy-done.7
  30.8 3.5 %fusion.11 = f32[1536,512]{1,0:T(8,128)} fusion(bf16[1024,512]{1,0:T(8,128)(2,1)S(1)} %multiply_convert_fusion, bf16[1024,512]{0,1:T(8,128)(2,1)S(1)} %slice.38, bf16[1024,512]{0,1:T(8,128)(2,1)S(1)} %fusion.7, bf16[1024,512]{0,1:T(8,128)(2,1)S(1)} %bitcast.26), kind=kOutput, calls=%fused_computation.30 | convolution fusion | flops 1620049920 | bytes 7340032 | tf_op jit(solution)/shard_map/dot_general | solution.py:31
  34.3 5.7 %fusion.34 = f32[1024,1536]{1,0:T(8,128)} fusion(bf16[1024,512]{1,0:T(8,128)(2,1)} %copy-done.7, bf16[1536,512]{1,0:T(8,128)(2,1)S(1)} %copy-done), kind=kOutput, calls=%fused_computation.66 | convolution fusion | flops 1610612736 | bytes 8912896 | tf_op jit(solution)/shard_map/dot_general | solution.py:37
  40.0 2.7 fusion.5
  42.7 2.5 fusion.33
  45.3 1.3 collective-permute-start.2
  46.6 5.2 %collective-permute-start.3 = (bf16[128,512]{1,0:T(8,128)(2,1)S(1)}, bf16[128,512]{1,0:T(8,128)(2,1)S(1)}, u32[]{:S(2)}, u32[]{:S(2)}) collective-permute-start(bf16[128,512]{1,0:T(8,128)(2,1)S(1)} %get-tuple-element.12), channel_id=1, source_target_pairs={{0,2},{2,4},{4,6},{6,8},{8,10},{10,12},{12,14},{14,16},{16,18},{18... | collective-permute-start | bytes 393224 | tf_op jit(solution)/shard_map/ppermute | solution.py:14
  51.8 90.0 %psum.23 = f32[512]{0:T(512)S(1)} all-reduce(f32[512]{0:T(512)S(1)} %get-tuple-element.6), channel_id=1, replica_groups=mesh['band'=16,'mesh'=8,'rep'=2] {'band','mesh','rep'}, use_global_device_ids=true, to_apply=%region_7.8 | all-reduce | flops 512 | bytes 4096 | tf_op jit(solution)/shard_map/psum | solution.py:127
  141.7 2.6 fusion.2
  144.3 3.4 %fusion.13 = bf16[1,512,512]{2,1,0:T(8,128)(2,1)} fusion(f32[512,512]{1,0:T(8,128)S(1)} %fusion.2, s32[1024]{0:T(1024)S(1)} %broadcast_subtract_fusion.1, f32[1024,1536]{1,0:T(8,128)} %fusion.34), kind=kOutput, calls=%fused_computation.32 | convolution fusion | flops 537919488 | bytes 2625536 | tf_op jit(solution)/shard_map/dot_general | solution.py:31
  147.7 2.7 fusion.14
  151.8 164.5 %all-reduce.3.cloned.1.call-done = (f32[1536,512]{1,0:T(8,128)}, f32[512,512]{1,0:T(8,128)}) async-done(((f32[1536,512]{1,0:T(8,128)}, f32[512,512]{1,0:T(8,128)}), (f32[1536,512]{1,0:T(8,128)}, f32[512,512]{1,0:T(8,128)})) %all-reduce.3.cloned.1.call-update) | async-done | bytes 4194320 | tf_op jit(solution)/shard_map/psum | solution.py:127
  316.3 4.0 %broadcast_multiply_fusion = f32[1536,512]{1,0:T(8,128)} fusion(f32[1536,512]{1,0:T(8,128)} %get-tuple-element.9), kind=kLoop, calls=%fused_computation.22 | loop fusion | flops 786432 | bytes 6291456 | tf_op jit(solution)/shard_map/mul | solution.py:140
  320.3 1.1 broadcast_multiply_fusion.1
  (35 shorter events, 4.2 us)
Async XLA Ops:
  7.2 14.8 %copy-start = (bf16[1536,512]{1,0:T(8,128)(2,1)S(1)}, bf16[1536,512]{1,0:T(8,128)(2,1)}, u32[]{:S(2)}) copy-start(bf16[1536,512]{1,0:T(8,128)(2,1)} %param.14) | copy-start | bytes 4718596
  7.2 11.2 %copy-start.4 = (s32[1024]{0:T(1024)S(1)}, s32[1024]{0:T(1024)}, u32[]{:S(2)}) copy-start(s32[1024]{0:T(1024)} %param.17) | copy-start | bytes 12292
  7.2 11.2 %copy-start.5 = (s32[1024]{0:T(1024)S(1)}, s32[1024]{0:T(1024)}, u32[]{:S(2)}) copy-start(s32[1024]{0:T(1024)} %param.18) | copy-start | bytes 12292
  7.2 11.3 %copy-start.6 = (bf16[1,512,512]{2,1,0:T(8,128)(2,1)S(1)}, bf16[1,512,512]{2,1,0:T(8,128)(2,1)}, u32[]{:S(2)}) copy-start(bf16[1,512,512]{2,1,0:T(8,128)(2,1)} %param.10) | copy-start | bytes 1572868
  7.2 309.1 %all-reduce.3.cloned.1.call-start = ((), (), s32[]{:S(2)}) async-start(), calls=%async_computation | async-start | bytes 8388608 | tf_op jit(solution)/shard_map/psum | solution.py:127
  9.2 10.2 %collective-permute-start.1 = (bf16[1,128,1024]{2,1,0:T(8,128)(2,1)S(1)}, bf16[1,128,1024]{2,1,0:T(8,128)(2,1)}, u32[]{:S(2)}, u32[]{:S(2)}) collective-permute-start(bf16[1,128,1024]{2,1,0:T(8,128)(2,1)S(1)} %constant_dynamic-update-slice_fusion), channel_id=1, source_target_pairs={{2,0},{4,2},{6,4},{8,6},{10,8},{12,10},{14,12},{16,14},{18,16},{20... | collective-permute-start | bytes 786440 | tf_op jit(solution)/shard_map/ppermute | solution.py:25
  10.5 8.9 %collective-permute-start = (bf16[1,128,1024]{2,1,0:T(8,128)(2,1)S(1)}, bf16[1,128,1024]{2,1,0:T(8,128)(2,1)}, u32[]{:S(2)}, u32[]{:S(2)}) collective-permute-start(bf16[1,128,1024]{2,1,0:T(8,128)(2,1)S(1)} %constant_dynamic-update-slice_fusion), channel_id=1, source_target_pairs={{0,2},{2,4},{4,6},{6,8},{8,10},{10,12},{12,14},{14,16},{16,18},{18... | collective-permute-start | bytes 786440 | tf_op jit(solution)/shard_map/ppermute | solution.py:24
  22.0 2.2 copy-start.2
  24.1 1.1 copy-start.3
  29.8 1.0 copy-start.7
  45.3 105.7 %collective-permute-start.2 = (bf16[128,512]{1,0:T(8,128)(2,1)S(1)}, bf16[128,512]{1,0:T(8,128)(2,1)S(1)}, u32[]{:S(2)}, u32[]{:S(2)}) collective-permute-start(bf16[128,512]{1,0:T(8,128)(2,1)S(1)} %get-tuple-element.11), channel_id=1, source_target_pairs={{2,0},{4,2},{6,4},{8,6},{10,8},{12,10},{14,12},{16,14},{18,16},{20... | collective-permute-start | bytes 393224 | tf_op jit(solution)/shard_map/ppermute | solution.py:14
  46.6 104.4 %collective-permute-start.3 = (bf16[128,512]{1,0:T(8,128)(2,1)S(1)}, bf16[128,512]{1,0:T(8,128)(2,1)S(1)}, u32[]{:S(2)}, u32[]{:S(2)}) collective-permute-start(bf16[128,512]{1,0:T(8,128)(2,1)S(1)} %get-tuple-element.12), channel_id=1, source_target_pairs={{0,2},{2,4},{4,6},{6,8},{8,10},{10,12},{12,14},{14,16},{16,18},{18... | collective-permute-start | bytes 393224 | tf_op jit(solution)/shard_map/ppermute | solution.py:14
  316.3 4.0 %copy-start.1 = (f32[512,512]{1,0:T(8,128)S(1)}, f32[512,512]{1,0:T(8,128)}, u32[]{:S(2)}) copy-start(f32[512,512]{1,0:T(8,128)} %get-tuple-element.10) | copy-start | bytes 3145732
Sparse Core Ops, SparseCore 0:
  40.1 276.1 all-reduce.2
where the time goes:
time: 330 us; the launch traced here: 328 us
  waiting for transfers between devices  165 us (50%)
  blocking collectives  90 us (27%)
  matrix products  29.7 us (9%)
  between operations  14.9 us (5%)
  starting transfers between devices  13.5 us (4%)
  other arithmetic  8.28 us (3%)
  local copies, waits for them, and re-layouts  7.24 us (2%)
    psum x1, waiting for transfers between devices, per_device(): lax.psum((first_term, second_term, gain_term), ('band', 'mesh', 'rep'))  165 us
    psum x1, blocking collectives, per_device(): lax.psum((first_term, second_term, gain_term), ('band', 'mesh', 'rep'))  90 us
    dot_general x6, matrix products, contract_rows(): lax.dot_general(left, right, (((0,), (0,)), ((), ())), preferred_element_...  16.4 us
    dot_general x2, matrix products, contract_cols(): lax.dot_general(left, right, (((1,), (1,)), ((), ())), precision=accuracy...  6.99 us
  transfers between devices with their start and end apart: 5, of which 1 were waited for; matrix products, arithmetic and copies ran while one was open for 5% of the time, Pallas kernels for 0%

commit v1 on v0

--- a/solution.py
+++ b/solution.py
@@ -93,6 +93,55 @@
     return terms[rows_mesh : 2 * rows_mesh] + from_above + from_below
 
 
+def swapped(value):
+    return lax.ppermute(value, "rep", [(0, 1), (1, 0)])
+
+
+def summed_shares(shares):
+    return jnp.sum(shares.astype(jnp.float32), axis=0)
+
+
+def total_over_devices(terms, gain_term, factor):
+    rows, width = terms.shape
+    bands, meshes = lax.axis_size("band"), lax.axis_size("mesh")
+    half = rows // 2
+    part = half // bands
+    piece = part // meshes
+    core = lax.axis_index("rep")
+    blocks = terms.reshape(2, half, width)
+    kept = lax.dynamic_index_in_dim(blocks, core, 0, False)
+    sent = lax.dynamic_index_in_dim(blocks, 1 - core, 0, False)
+
+    def with_gain(shares, gain):
+        upper = gain.astype(jnp.bfloat16)
+        lower = (gain - upper.astype(jnp.float32)).astype(jnp.bfloat16)
+        extra = jnp.concatenate(
+            [upper[None], lower[None], jnp.zeros((6, width), jnp.bfloat16)], axis=0
+        )
+        extra = jnp.broadcast_to(extra[None], (shares.shape[0], 8, width))
+        return jnp.concatenate([shares.astype(jnp.bfloat16), extra], axis=1)
+
+    def split_gain(total, rows_here):
+        return total[:rows_here], total[rows_here] + total[rows_here + 1]
+
+    got = swapped(with_gain(sent[None], gain_term)[0]).astype(jnp.float32)
+    got, gain_got = split_gain(got, half)
+    total, gain = kept + got, gain_term + gain_got
+    got = lax.all_to_all(with_gain(total.reshape(bands, part, width), gain), "band", 0, 0)
+    total, gain = split_gain(summed_shares(got), part)
+    got = lax.all_to_all(with_gain(total.reshape(meshes, piece, width), gain), "mesh", 0, 0)
+    total, gain = split_gain(summed_shares(got), piece)
+    total = (total * factor).astype(jnp.bfloat16)
+    total = lax.all_to_all(jnp.broadcast_to(total[None], (meshes, piece, width)), "mesh", 0, 0)
+    total = total.reshape(part, width)
+    total = lax.all_to_all(jnp.broadcast_to(total[None], (bands, part, width)), "band", 0, 0)
+    total = total.reshape(half, width)
+    other = swapped(total)
+    low = jnp.where(core == 0, total, other)
+    high = jnp.where(core == 0, other, total)
+    return jnp.concatenate([low, high], axis=0).astype(jnp.float32), gain * factor
+
+
 def per_device(
     grid_latent,
     mesh_latent,
@@ -124,8 +173,8 @@
     )
     devices = lax.axis_size("band") * lax.axis_size("mesh") * lax.axis_size("rep")
     factor = 1.0 / math.sqrt(slot_count * devices)
-    first_total, second_total, gain_total = lax.psum(
-        (first_term, second_term, gain_term), ("band", "mesh", "rep")
+    weight_total, gain_total = total_over_devices(
+        jnp.concatenate([first_term, second_term], axis=0), gain_term, factor
     )
     grad_features = contract_cols(grad_pre, w_first)
     grad_front = grad_features[:, : 2 * model_width]
@@ -137,9 +186,9 @@
         grid_grad[None],
         mesh_grad[None],
         edge_grad[None],
-        first_total * factor,
-        second_total * factor,
-        gain_total * factor,
+        weight_total[: 3 * model_width],
+        weight_total[3 * model_width :],
+        gain_total,
     )
 
 

time: 330 us -> 133 us (0.40)
  waiting for transfers between devices: 165 us -> 12.9 us
  blocking collectives: 90 us -> 33.3 us
  starting transfers between devices: 13.5 us -> 30.7 us
  between operations: 14.9 us -> 1.68 us
  local copies, waits for them, and re-layouts: 7.24 us -> 14.1 us
  other arithmetic: 8.28 us -> 11.9 us
    psum x1 -> x0, waiting for transfers between devices: 165 us -> none  [per_device(): lax.psum((first_term, second_term, gain_term), ('band', 'mesh', 'rep'))]
    psum x1 -> x0, blocking collectives: 90 us -> none  [per_device(): lax.psum((first_term, second_term, gain_term), ('band', 'mesh', 'rep'))]
    all_to_all x0 -> x1, blocking collectives: none -> 33.3 us  [total_over_devices(): lax.all_to_all(with_gain(total.reshape(bands, part, width), gain), 'band'...]
    all_to_all x0 -> x3, waiting for transfers between devices: none -> 10.5 us  [the longest x1 7.83 us: total_over_devices(): lax.all_to_all(with_gain(total.reshape(meshes, piece, width), gain), 'mes...]
    all_to_all x0 -> x3, starting transfers between devices: none -> 10.4 us  [the longest x1 3.66 us: total_over_devices(): lax.all_to_all(jnp.broadcast_to(total[None], (bands, part, width)), 'band...]
    ppermute x0 -> x2, starting transfers between devices: none -> 7.37 us  [swapped(): return lax.ppermute(value, 'rep', [(0, 1), (1, 0)])]
    mul x3 -> x1, other arithmetic: 5.65 us -> 1.37 us  [total_over_devices(): gain * factor]
    convert_element_type x0 -> x9, other arithmetic: none -> 4.08 us  [the longest x1 1.95 us: with_gain(): return jnp.concatenate([shares.astype(jnp.bfloat16), extra], axis=1)]
  transfers between devices with their start and end apart: 5 -> 9, of which waited for: 1 -> 3; matrix products, arithmetic and copies ran while one was open for 5% -> 20% of each run, Pallas kernels for 0% -> 0%
where the time goes in v1:
time: 133 us; the launch traced here: 132 us
  blocking collectives  33.3 us (25%)
  starting transfers between devices  30.7 us (23%)
  matrix products  27.7 us (21%)
  local copies, waits for them, and re-layouts  14.1 us (11%)
  waiting for transfers between devices  12.9 us (10%)
  other arithmetic  11.9 us (9%)
  between operations  1.68 us (1%)
    all_to_all x1, blocking collectives, total_over_devices(): lax.all_to_all(with_gain(total.reshape(bands, part, width), gain), 'band'...  33.3 us
    dot_general x6, matrix products, contract_rows(): lax.dot_general(left, right, (((0,), (0,)), ((), ())), preferred_element_...  14.6 us
    all_to_all x1, waiting for transfers between devices, total_over_devices(): lax.all_to_all(with_gain(total.reshape(meshes, piece, width), gain), 'mes...  7.83 us
    ppermute x2, starting transfers between devices, swapped(): return lax.ppermute(value, 'rep', [(0, 1), (1, 0)])  7.37 us
    ppermute x2, starting transfers between devices, passed_along(): lax.ppermute(value, axis, [(source, source + steps) for source in range(l...  5.93 us
    dot_general x2, matrix products, contract_cols(): lax.dot_general(left, right, (((1,), (1,)), ((), ())), precision=accuracy...  5.79 us
    unnamed x22, local copies, waits for them, and re-layouts  5.76 us
    ppermute x1, starting transfers between devices, padded(): before = lax.ppermute(last, axis, up)  5.72 us
  transfers between devices with their start and end apart: 9, of which 3 were waited for; matrix products, arithmetic and copies ran while one was open for 20% of the time, Pallas kernels for 0%

profile of v1, /device:TPU:1, one launch (start us, length us, event | category | flops | bytes accessed | tf_op | source)
XLA Modules:
  0.0 132.3 jit_solution(5464826145448355554)
XLA Ops:
  3.9 5.7 %collective-permute-start = (bf16[1,128,1024]{2,1,0:T(8,128)(2,1)S(1)}, bf16[1,128,1024]{2,1,0:T(8,128)(2,1)}, u32[]{:S(2)}, u32[]{:S(2)}) collective-permute-start(bf16[1,128,1024]{2,1,0:T(8,128)(2,1)S(1)} %constant_dynamic-update-slice_fusion), channel_id=1, source_target_pairs={{0,2},{2,4},{4,6},{6,8},{8,10},{10,12},{12,14},{14,16},{16,18},{18... | collective-permute-start | bytes 786440 | tf_op jit(solution)/shard_map/ppermute | solution.py:24
  11.9 2.0 %fusion.8 = bf16[1024,512]{0,1:T(8,128)(2,1)S(1)} fusion(s32[1024]{0:T(1024)S(1)} %broadcast_subtract_fusion.1, bf16[1,512,512]{2,1,0:T(8,128)(2,1)} %param.10), kind=kOutput, calls=%fused_computation.31 | convolution fusion | flops 537919488 | bytes 1576960 | tf_op jit(solution)/shard_map/dot_general | solution.py:51
  13.9 2.4 %convolution_convert_fusion = bf16[1024,1024]{0,1:T(8,128)(2,1)S(1)} fusion(bf16[1,128,1024]{2,1,0:T(8,128)(2,1)S(1)} %collective-permute-done.1, bf16[1,128,1024]{2,1,0:T(8,128)(2,1)S(1)} %constant_dynamic-update-slice_fusion, bf16[1,128,1024]{2,1,0:T(8,128)(2,1)} %collective-permute-done, s32[1024]{0:T(1024)S(1)} %broadcast_subtract_fusion), kind=kOutput, calls=%fused_computation.27 | convolution fusion | flops 809107456 | bytes 2887680 | tf_op jit(solution)/shard_map/dot_general | solution.py:51
  16.4 2.1 %multiply_convert_fusion.2 = (bf16[1024,512]{1,0:T(8,128)(2,1)S(1)}, f32[1024,512]{1,0:T(8,128)S(1)}) fusion(bf16[1536,512]{1,0:T(8,128)(2,1)S(1)} %copy-done, bf16[1024,512]{0,1:T(8,128)(2,1)S(1)} %slice.83, bf16[1024,512]{0,1:T(8,128)(2,1)S(1)} %fusion.8, bf16[1024,512]{0,1:T(8,128)(2,1)S(1)} %bitcast.45), kind=kOutput, calls=%fused_computation.18 | convolution fusion | flops 1622671360 | bytes 7864320 | tf_op jit(solution)/shard_map/dot_general | solution.py:61
  24.3 1.8 %fusion.12 = f32[1536,512]{1,0:T(8,128)S(1)} fusion(bf16[1024,512]{1,0:T(8,128)(2,1)S(1)} %multiply_convert_fusion, bf16[1024,512]{0,1:T(8,128)(2,1)S(1)} %slice.83, bf16[1024,512]{0,1:T(8,128)(2,1)S(1)} %fusion.8, bf16[1024,512]{0,1:T(8,128)(2,1)S(1)} %bitcast.46), kind=kOutput, calls=%fused_computation.35 | convolution fusion | flops 1620049920 | bytes 7340032 | tf_op jit(solution)/shard_map/dot_general | solution.py:31
  28.5 2.8 %collective-permute-start.4 = (bf16[1032,512]{1,0:T(8,128)(2,1)S(1)}, bf16[1032,512]{1,0:T(8,128)(2,1)}, u32[]{:S(2)}, u32[]{:S(2)}) collective-permute-start(bf16[1032,512]{1,0:T(8,128)(2,1)S(1)} %maximum_bitcast_fusion), channel_id=1, source_target_pairs={{0,1},{1,0},{2,3},{3,2},{4,5},{5,4},{6,7},{7,6},{8,9},{9,8},{10,11... | collective-permute-start | bytes 3170312 | tf_op jit(solution)/shard_map/ppermute | solution.py:97
  31.3 2.4 %collective-permute-done.4 = bf16[1032,512]{1,0:T(8,128)(2,1)} collective-permute-done((bf16[1032,512]{1,0:T(8,128)(2,1)S(1)}, bf16[1032,512]{1,0:T(8,128)(2,1)}, u32[]{:S(2)}, u32[]{:S(2)}) %collective-permute-start.4) | collective-permute-done | bytes 1056800 | tf_op jit(solution)/shard_map/ppermute | solution.py:97
  35.3 1.9 %fusion = bf16[1024,512]{1,0:T(8,128)(2,1)S(1)} fusion(f32[1032,512]{1,0:T(8,128)S(1)} %convert_element_type.157, f32[2,1024,512]{2,1,0:T(8,128)} %bitcast.42, s32[]{:T(128)S(6)} %select_n.25), kind=kLoop, calls=%fused_computation.4 | loop fusion | flops 1048576 | bytes 5242884 | tf_op jit(solution)/shard_map/convert_element_type | solution.py:122
  37.4 33.3 %all_to_all.20 = bf16[16,72,512]{2,1,0:T(8,128)(2,1)S(1)} all-to-all(bf16[16,72,512]{2,1,0:T(8,128)(2,1)S(1)} %pad_maximum_fusion.4), channel_id=1, replica_groups=mesh['band'=16,'mesh'=8,'rep'=2] {'band'}, dimensions={0} | all-to-all | bytes 2359296 | tf_op jit(solution)/shard_map/all_to_all | solution.py:130
  71.7 3.4 %all-to-all-start.1 = ((bf16[8,16,512]{2,1,0:T(8,128)(2,1)}), bf16[8,16,512]{2,1,0:T(8,128)(2,1)S(1)}, u32[]{:S(2)}, u32[]{:S(2)}) async-start(bf16[8,16,512]{2,1,0:T(8,128)(2,1)} %pad_maximum_fusion.5), calls=%async_computation.1 | async-start | bytes 262144 | tf_op jit(solution)/shard_map/all_to_all | solution.py:132
  75.1 7.8 %all-to-all-done.1 = bf16[8,16,512]{2,1,0:T(8,128)(2,1)S(1)} async-done(((bf16[8,16,512]{2,1,0:T(8,128)(2,1)}), bf16[8,16,512]{2,1,0:T(8,128)(2,1)S(1)}, u32[]{:S(2)}, u32[]{:S(2)}) %all-to-all-start.1) | async-done | bytes 131104 | tf_op jit(solution)/shard_map/all_to_all | solution.py:132
  84.2 3.4 %all-to-all-start.2 = ((bf16[8,8,512]{2,1,0:T(8,128)(2,1)}), bf16[8,8,512]{2,1,0:T(8,128)(2,1)S(1)}, u32[]{:S(2)}, u32[]{:S(2)}) async-start(bf16[8,8,512]{2,1,0:T(8,128)(2,1)} %broadcast_in_dim.38), calls=%async_computation.2 | async-start | bytes 131072 | tf_op jit(solution)/shard_map/all_to_all | solution.py:135
  87.5 4.5 %fusion.42 = f32[1024,1536]{1,0:T(8,128)} fusion(bf16[1024,512]{1,0:T(8,128)(2,1)S(1)} %copy-done.9, bf16[1536,512]{1,0:T(8,128)(2,1)S(1)} %copy-done), kind=kOutput, calls=%fused_computation.93 | convolution fusion | flops 1610612736 | bytes 8912896 | tf_op jit(solution)/shard_map/dot_general | solution.py:37
  92.0 2.6 %all-to-all-done.2 = bf16[8,8,512]{2,1,0:T(8,128)(2,1)S(1)} async-done(((bf16[8,8,512]{2,1,0:T(8,128)(2,1)}), bf16[8,8,512]{2,1,0:T(8,128)(2,1)S(1)}, u32[]{:S(2)}, u32[]{:S(2)}) %all-to-all-start.2) | async-done | bytes 65568 | tf_op jit(solution)/shard_map/all_to_all | solution.py:135
  95.7 3.7 %all-to-all-start.3 = ((bf16[16,64,512]{2,1,0:T(8,128)(2,1)}), bf16[16,64,512]{2,1,0:T(8,128)(2,1)S(1)}, u32[]{:S(2)}, u32[]{:S(2)}) async-start(bf16[16,64,512]{2,1,0:T(8,128)(2,1)} %broadcast_in_dim.40), calls=%async_computation.3 | async-start | bytes 2097152 | tf_op jit(solution)/shard_map/all_to_all | solution.py:137
  99.4 2.5 %fusion.6 = f32[384,512]{1,0:T(8,128)S(1)} fusion(f32[1024,1536]{1,0:T(8,128)} %fusion.42, s32[1024]{0:T(1024)S(1)} %broadcast_subtract_fusion), kind=kOutput, calls=%fused_computation.29 | convolution fusion | flops 405143552 | bytes 2887680 | tf_op jit(solution)/shard_map/dot_general | solution.py:31
  101.9 2.5 %fusion.41 = (bf16[384,512]{1,0:T(8,128)(2,1)S(1)}, f32[384,512]{1,0:T(8,128)S(1)}) fusion(f32[384,512]{1,0:T(8,128)S(1)} %fusion.6, f32[1024,1536]{1,0:T(8,128)} %fusion.42, s32[1024]{0:T(1024)S(1)} %broadcast_subtract_fusion), kind=kOutput, calls=%fused_computation.92 | convolution fusion | flops 403439616 | bytes 3018752 | tf_op jit(solution)/shard_map/dot_general | solution.py:31
  106.5 4.6 %collective-permute-start.3 = (bf16[128,512]{1,0:T(8,128)(2,1)}, bf16[128,512]{1,0:T(8,128)(2,1)}, u32[]{:S(2)}, u32[]{:S(2)}) collective-permute-start(bf16[128,512]{1,0:T(8,128)(2,1)} %get-tuple-element.14), channel_id=1, source_target_pairs={{0,2},{2,4},{4,6},{6,8},{8,10},{10,12},{12,14},{14,16},{16,18},{18... | collective-permute-start | bytes 393224 | tf_op jit(solution)/shard_map/ppermute | solution.py:14
  111.1 3.6 %fusion.3 = f32[512,512]{1,0:T(8,128)} fusion(f32[1024,1536]{1,0:T(8,128)} %fusion.42, s32[1024]{0:T(1024)S(1)} %broadcast_subtract_fusion.1), kind=kOutput, calls=%fused_computation.21 | convolution fusion | flops 539492352 | bytes 3149824 | tf_op jit(solution)/shard_map/dot_general | solution.py:31
  114.7 4.6 %collective-permute-start.5 = (bf16[1024,512]{1,0:T(8,128)(2,1)S(1)}, bf16[1024,512]{1,0:T(8,128)(2,1)S(1)}, u32[]{:S(2)}, u32[]{:S(2)}) collective-permute-start(bf16[1024,512]{1,0:T(8,128)(2,1)S(1)} %bitcast.43), channel_id=1, source_target_pairs={{0,1},{1,0},{2,3},{3,2},{4,5},{5,4},{6,7},{7,6},{8,9},{9,8},{10,11... | collective-permute-start | bytes 3145736 | tf_op jit(solution)/shard_map/ppermute | solution.py:97
  119.3 2.7 %fusion.15 = bf16[1,1024,512]{2,1,0:T(8,128)(2,1)} fusion(f32[1024,1536]{1,0:T(8,128)} %fusion.42), kind=kLoop, calls=%fused_computation.40 | loop fusion | bytes 2097152 | tf_op jit(solution)/shard_map/broadcast_in_dim | solution.py:188
  122.0 3.4 %fusion.14 = bf16[1,512,512]{2,1,0:T(8,128)(2,1)} fusion(f32[512,512]{1,0:T(8,128)S(1)} %copy-done.7, s32[1024]{0:T(1024)S(1)} %broadcast_subtract_fusion.1, f32[1024,1536]{1,0:T(8,128)} %fusion.42), kind=kOutput, calls=%fused_computation.37 | convolution fusion | flops 537919488 | bytes 2625536 | tf_op jit(solution)/shard_map/dot_general | solution.py:31
  125.4 1.6 %fusion.28 = f32[1,128,512]{2,1,0:T(8,128)} fusion(f32[384,512]{1,0:T(8,128)S(1)} %get-tuple-element.22, bf16[128,512]{1,0:T(8,128)(2,1)} %collective-permute-done.3, bf16[128,512]{1,0:T(8,128)(2,1)S(1)} %collective-permute-done.2), kind=kLoop, calls=%fused_computation.58 | loop fusion | flops 262144 | bytes 786432 | tf_op jit(solution)/shard_map/broadcast_in_dim | solution.py:187
  130.3 2.0 %slice.98 = f32[1536,512]{1,0:T(8,128)} slice(f32[2048,512]{1,0:T(8,128)S(1)} %maximum_convert_fusion), slice={[0:1536], [0:512]} | slice | bytes 6291456 | tf_op jit(solution)/shard_map/slice | solution.py:189
  (73 shorter events, 23.2 us)
Async XLA Ops:
  0.6 15.7 %copy-start = (bf16[1536,512]{1,0:T(8,128)(2,1)S(1)}, bf16[1536,512]{1,0:T(8,128)(2,1)}, u32[]{:S(2)}) copy-start(bf16[1536,512]{1,0:T(8,128)(2,1)} %param.14) | copy-start | bytes 4718596
  0.6 11.2 %copy-start.5 = (s32[1024]{0:T(1024)S(1)}, s32[1024]{0:T(1024)}, u32[]{:S(2)}) copy-start(s32[1024]{0:T(1024)} %param.17) | copy-start | bytes 12292
  0.7 11.2 %copy-start.6 = (s32[1024]{0:T(1024)S(1)}, s32[1024]{0:T(1024)}, u32[]{:S(2)}) copy-start(s32[1024]{0:T(1024)} %param.18) | copy-start | bytes 12292
  2.6 11.2 %collective-permute-start.1 = (bf16[1,128,1024]{2,1,0:T(8,128)(2,1)S(1)}, bf16[1,128,1024]{2,1,0:T(8,128)(2,1)S(1)}, u32[]{:S(2)}, u32[]{:S(2)}) collective-permute-start(bf16[1,128,1024]{2,1,0:T(8,128)(2,1)S(1)} %constant_dynamic-update-slice_fusion), channel_id=1, source_target_pairs={{2,0},{4,2},{6,4},{8,6},{10,8},{12,10},{14,12},{16,14},{18,16},{20... | collective-permute-start | bytes 786440 | tf_op jit(solution)/shard_map/ppermute | solution.py:25
  3.9 10.0 %collective-permute-start = (bf16[1,128,1024]{2,1,0:T(8,128)(2,1)S(1)}, bf16[1,128,1024]{2,1,0:T(8,128)(2,1)}, u32[]{:S(2)}, u32[]{:S(2)}) collective-permute-start(bf16[1,128,1024]{2,1,0:T(8,128)(2,1)S(1)} %constant_dynamic-update-slice_fusion), channel_id=1, source_target_pairs={{0,2},{2,4},{4,6},{6,8},{8,10},{10,12},{12,14},{14,16},{16,18},{18... | collective-permute-start | bytes 786440 | tf_op jit(solution)/shard_map/ppermute | solution.py:24
  16.4 2.2 %copy-start.2 = (bf16[512,512]{1,0:T(8,128)(2,1)S(1)}, bf16[512,512]{1,0:T(8,128)(2,1)}, u32[]{:S(2)}) copy-start(bf16[512,512]{1,0:T(8,128)(2,1)} %param.15) | copy-start | bytes 1572868
  18.5 1.1 copy-start.4
  23.3 1.0 copy-start.8
  26.6 1.9 %copy-start.1 = (f32[2048,512]{1,0:T(8,128)}, f32[2048,512]{1,0:T(8,128)S(1)}, u32[]{:S(2)}) copy-start(f32[2048,512]{1,0:T(8,128)S(1)} %pad_maximum_fusion) | copy-start | bytes 12582916
  28.5 5.2 %collective-permute-start.4 = (bf16[1032,512]{1,0:T(8,128)(2,1)S(1)}, bf16[1032,512]{1,0:T(8,128)(2,1)}, u32[]{:S(2)}, u32[]{:S(2)}) collective-permute-start(bf16[1032,512]{1,0:T(8,128)(2,1)S(1)} %maximum_bitcast_fusion), channel_id=1, source_target_pairs={{0,1},{1,0},{2,3},{3,2},{4,5},{5,4},{6,7},{7,6},{8,9},{9,8},{10,11... | collective-permute-start | bytes 3170312 | tf_op jit(solution)/shard_map/ppermute | solution.py:97
  37.4 50.1 %copy-start.9 = (bf16[1024,512]{1,0:T(8,128)(2,1)S(1)}, bf16[1024,512]{1,0:T(8,128)(2,1)}, u32[]{:S(2)}) copy-start(bf16[1024,512]{1,0:T(8,128)(2,1)} %copy-done.8) | copy-start | bytes 3145732
  71.7 11.2 %all-to-all-start.1 = ((bf16[8,16,512]{2,1,0:T(8,128)(2,1)}), bf16[8,16,512]{2,1,0:T(8,128)(2,1)S(1)}, u32[]{:S(2)}, u32[]{:S(2)}) async-start(bf16[8,16,512]{2,1,0:T(8,128)(2,1)} %pad_maximum_fusion.5), calls=%async_computation.1 | async-start | bytes 262144 | tf_op jit(solution)/shard_map/all_to_all | solution.py:132
  82.9 0.6 copy-start.3
  84.2 10.5 %all-to-all-start.2 = ((bf16[8,8,512]{2,1,0:T(8,128)(2,1)}), bf16[8,8,512]{2,1,0:T(8,128)(2,1)S(1)}, u32[]{:S(2)}, u32[]{:S(2)}) async-start(bf16[8,8,512]{2,1,0:T(8,128)(2,1)} %broadcast_in_dim.38), calls=%async_computation.2 | async-start | bytes 131072 | tf_op jit(solution)/shard_map/all_to_all | solution.py:135
  95.7 19.0 %all-to-all-start.3 = ((bf16[16,64,512]{2,1,0:T(8,128)(2,1)}), bf16[16,64,512]{2,1,0:T(8,128)(2,1)S(1)}, u32[]{:S(2)}, u32[]{:S(2)}) async-start(bf16[16,64,512]{2,1,0:T(8,128)(2,1)} %broadcast_in_dim.40), calls=%async_computation.3 | async-start | bytes 2097152 | tf_op jit(solution)/shard_map/all_to_all | solution.py:137
  105.2 20.2 %collective-permute-start.2 = (bf16[128,512]{1,0:T(8,128)(2,1)}, bf16[128,512]{1,0:T(8,128)(2,1)S(1)}, u32[]{:S(2)}, u32[]{:S(2)}) collective-permute-start(bf16[128,512]{1,0:T(8,128)(2,1)} %get-tuple-element.13), channel_id=1, source_target_pairs={{2,0},{4,2},{6,4},{8,6},{10,8},{12,10},{14,12},{16,14},{18,16},{20... | collective-permute-start | bytes 393224 | tf_op jit(solution)/shard_map/ppermute | solution.py:14
  106.5 18.9 %collective-permute-start.3 = (bf16[128,512]{1,0:T(8,128)(2,1)}, bf16[128,512]{1,0:T(8,128)(2,1)}, u32[]{:S(2)}, u32[]{:S(2)}) collective-permute-start(bf16[128,512]{1,0:T(8,128)(2,1)} %get-tuple-element.14), channel_id=1, source_target_pairs={{0,2},{2,4},{4,6},{6,8},{8,10},{10,12},{12,14},{14,16},{16,18},{18... | collective-permute-start | bytes 393224 | tf_op jit(solution)/shard_map/ppermute | solution.py:14
  114.7 7.3 %copy-start.7 = (f32[512,512]{1,0:T(8,128)S(1)}, f32[512,512]{1,0:T(8,128)}, u32[]{:S(2)}) copy-start(f32[512,512]{1,0:T(8,128)} %fusion.3) | copy-start | bytes 3145732
  114.7 13.7 %collective-permute-start.5 = (bf16[1024,512]{1,0:T(8,128)(2,1)S(1)}, bf16[1024,512]{1,0:T(8,128)(2,1)S(1)}, u32[]{:S(2)}, u32[]{:S(2)}) collective-permute-start(bf16[1024,512]{1,0:T(8,128)(2,1)S(1)} %bitcast.43), channel_id=1, source_target_pairs={{0,1},{1,0},{2,3},{3,2},{4,5},{5,4},{6,7},{7,6},{8,9},{9,8},{10,11... | collective-permute-start | bytes 3145736 | tf_op jit(solution)/shard_map/ppermute | solution.py:97

commit v2 on v0

v2 whole, which is shorter than its diff:
```python
import functools
import math

import jax
import jax.numpy as jnp
from jax import lax
from jax.experimental import pallas as pl
from jax.experimental.pallas import tpu as pltpu
from jax.sharding import PartitionSpec as P

NORM_EPS = 1e-05
TILE = 256
LANES = 128
MIB = 1 << 20


def dot(left, right, left_dim=1, right_dim=0):
    return lax.dot_general(
        left,
        right,
        (((left_dim,), (right_dim,)), ((), ())),
        preferred_element_type=jnp.float32,
    )


def picks(row, width):
    edges = row.shape[1]
    column = jnp.transpose(jnp.broadcast_to(row, (LANES, edges)))
    lane = lax.broadcasted_iota(jnp.int32, (edges, LANES), 1)
    return jnp.concatenate(
        [(column == lane + start).astype(jnp.float32).astype(jnp.bfloat16) for start in range(0, width, LANES)],
        axis=1,
    )


def spreads(row, width):
    edges = row.shape[1]
    place = lax.broadcasted_iota(jnp.int32, (width, edges), 0)
    return (place == row).astype(jnp.float32).astype(jnp.bfloat16)


def upper_lower(value):
    upper = value.astype(jnp.bfloat16)
    return upper, (value - upper.astype(jnp.float32)).astype(jnp.bfloat16)


def gain_rows(gain):
    upper, lower = upper_lower(gain)
    place = lax.broadcasted_iota(jnp.int32, (8, gain.shape[1]), 0)
    return jnp.where(
        place == 0, upper.astype(jnp.float32), jnp.where(place == 1, lower.astype(jnp.float32), 0.0)
    )


def anywhere():
    return pl.BlockSpec(memory_space=pl.ANY)


def in_vmem():
    return pl.BlockSpec(memory_space=pltpu.VMEM)


def in_smem():
    return pl.BlockSpec(memory_space=pltpu.SMEM)


def call(kernel, name, specs, outs, operands, flops, scratch=(), limit=40 * MIB):
    size = sum(math.prod(o.shape) * o.dtype.itemsize for o in outs)
    size += sum(math.prod(o.shape) * o.dtype.itemsize for o in operands)
    return pl.pallas_call(
        kernel,
        out_shape=outs,
        in_specs=specs,
        out_specs=[in_vmem()] * len(outs),
        scratch_shapes=list(scratch),
        compiler_params=pltpu.CompilerParams(vmem_limit_bytes=limit),
        cost_estimate=pl.CostEstimate(flops=int(flops), bytes_accessed=size, transcendentals=0),
        name=name,
    )(*operands)


def near_kernel(scalars, senders, grid, edge, w_first, partial, grid_picked):
    rows_grid, width = grid.shape
    for start in range(0, edge.shape[0], TILE):
        rows = pl.ds(start, TILE)
        table = picks(senders[:, rows] - scalars[0], rows_grid)
        picked = dot(table, grid[...]).astype(jnp.bfloat16)
        grid_picked[rows, :] = picked
        partial[rows, :] = dot(edge[rows, :], w_first[0:width, :]) + dot(
            picked, w_first[width : 2 * width, :]
        )


def live_receivers(scalars, receivers, start):
    row = receivers[:, pl.ds(start, TILE)] - scalars[1]
    slot = start + lax.broadcasted_iota(jnp.int32, (1, TILE), 1)
    return jnp.where(slot < scalars[2], row, -1)


def edge_kernel(
    scalars,
    receivers,
    partial,
    grid_picked,
    edge,
    mesh_before,
    mesh_own,
    mesh_after,
    cot_before,
    cot_own,
    cot_after,
    w_first,
    w_second,
    norm_gain,
    sent,
    gain_term,
    grad_pre,
    grad_output,
    hidden,
    mesh_picked,
):
    width = w_second.shape[0]
    rows_mesh = mesh_own.shape[0]
    gain_sum = jnp.zeros((1, width), jnp.float32)
    for start in range(0, edge.shape[0], TILE):
        rows = pl.ds(start, TILE)
        table = picks(live_receivers(scalars, receivers, start), 3 * rows_mesh)

        def picked_rows(before, own, after):
            near = jnp.concatenate([before[...], own[...], after[...]], axis=0)
            return dot(table, near)

        latents = picked_rows(mesh_before, mesh_own, mesh_after).astype(jnp.bfloat16)
        upstream = picked_rows(cot_before, cot_own, cot_after)
        mesh_picked[rows, :] = latents
        pre_act = partial[rows, :] + dot(latents, w_first[2 * width : 3 * width, :])
        sigmoid = jax.nn.sigmoid(pre_act)
        hid = (pre_act * sigmoid).astype(jnp.bfloat16)
        hidden[rows, :] = hid
        output = dot(hid, w_second[...])
        centered = output - jnp.mean(output, axis=1, keepdims=True)
        inverse = lax.rsqrt(jnp.mean(centered * centered, axis=1, keepdims=True) + NORM_EPS)
        normed = centered * inverse
        gain_sum = gain_sum + jnp.sum(upstream * normed, axis=0, keepdims=True)
        scaled = upstream * norm_gain[...]
        grad_out = (
            inverse
            * (
                scaled
                - jnp.mean(scaled, axis=1, keepdims=True)
                - normed * jnp.mean(scaled * normed, axis=1, keepdims=True)
            )
        ).astype(jnp.bfloat16)
        grad_output[rows, :] = grad_out
        grad_hidden = dot(grad_out, w_second[...], 1, 1)
        grad_pre[rows, :] = (grad_hidden * sigmoid * (1.0 + pre_act * (1.0 - sigmoid))).astype(
            jnp.bfloat16
        )
    gain_term[...] = jnp.broadcast_to(gain_sum, gain_term.shape)
    sent[2 * width : 2 * width + 16, :] = jnp.concatenate(
        [gain_rows(gain_sum), jnp.zeros((8, width), jnp.float32)], axis=0
    ).astype(jnp.bfloat16)

    @pl.when(scalars[3] == 0)
    def _():
        sent[0:width, :] = dot(mesh_picked[...], grad_pre[...], 0, 0).astype(jnp.bfloat16)
        sent[width : 2 * width, :] = dot(hidden[...], grad_output[...], 0, 0).astype(jnp.bfloat16)

    @pl.when(scalars[3] != 0)
    def _():
        sent[0:width, :] = dot(edge[...], grad_pre[...], 0, 0).astype(jnp.bfloat16)
        sent[width : 2 * width, :] = dot(grid_picked[...], grad_pre[...], 0, 0).astype(jnp.bfloat16)


def kept_kernel(scalars, edge, grid_picked, mesh_picked, hidden, grad_pre, grad_output, kept):
    width = grad_pre.shape[1]

    @pl.when(scalars[3] != 0)
    def _():
        kept[0:width, :] = dot(mesh_picked[...], grad_pre[...], 0, 0)
        kept[width : 2 * width, :] = dot(hidden[...], grad_output[...], 0, 0)

    @pl.when(scalars[3] == 0)
    def _():
        kept[0:width, :] = dot(edge[...], grad_pre[...], 0, 0)
        kept[width : 2 * width, :] = dot(grid_picked[...], grad_pre[...], 0, 0)


def pack_kernel(kept, got, gain_term, packed):
    bands = packed.shape[0]
    half, width = kept.shape
    part = half // bands
    tail = got[half : half + 16, :].astype(jnp.float32)
    gain = gain_rows(gain_term[0:1, :] + tail[0:1] + tail[1:2])
    for band in range(bands):
        rows = pl.ds(band * part, part)
        data = kept[rows, :] + got[rows, :].astype(jnp.float32)
        packed[band] = jnp.concatenate([data, gain], axis=0).astype(jnp.bfloat16)


def band_sum_kernel(shares, after, packed):
    meshes, rows = packed.shape[0], packed.shape[1] - 8
    total = shares[0].astype(jnp.float32)
    for band in range(1, shares.shape[0]):
        total = total + shares[band].astype(jnp.float32)
    part = rows * meshes
    gain = gain_rows(total[part : part + 1] + total[part + 1 : part + 2])
    for place in range(meshes):
        data = total[place * rows : (place + 1) * rows]
        packed[place] = jnp.concatenate([data, gain], axis=0).astype(jnp.bfloat16)


def mesh_sum_kernel(factor, shares, copies, gain_grad):
    total = shares[0].astype(jnp.float32)
    for place in range(1, shares.shape[0]):
        total = total + shares[place].astype(jnp.float32)
    total = total * factor
    rows = copies.shape[1]
    gain_grad[...] = jnp.broadcast_to(total[rows : rows + 1] + total[rows + 1 : rows + 2], gain_grad.shape)
    data = total[0:rows].astype(jnp.bfloat16)
    for place in range(copies.shape[0]):
        copies[place] = data


def node_kernel(
    scalars,
    senders,
    receivers,
    grad_pre,
    w_first,
    after,
    edge_grad,
    grid_grad,
    mesh_own,
    to_below,
    to_above,
    done,
):
    edges, width = grad_pre.shape
    rows_grid, rows_mesh = grid_grad.shape[0], mesh_own.shape[0]

    def through(sums, first):
        upper, lower = upper_lower(sums)
        weights = w_first[first : first + width, :]
        return dot(upper, weights, 1, 1) + dot(lower, weights, 1, 1)

    near = jnp.zeros((3 * rows_mesh, width), jnp.float32)
    here = jnp.zeros((rows_grid, width), jnp.float32)
    for start in range(0, edges, TILE):
        rows = pl.ds(start, TILE)
        terms = grad_pre[rows, :]
        near = near + dot(spreads(live_receivers(scalars, receivers, start), 3 * rows_mesh), terms)
        here = here + dot(spreads(senders[:, rows] - scalars[0], rows_grid), terms)
        edge_grad[rows, :] = dot(terms, w_first[0:width, :], 1, 1).astype(jnp.bfloat16)
    mesh_terms = through(near, 2 * width)
    to_below[...] = mesh_terms[0:rows_mesh].astype(jnp.bfloat16)
    mesh_own[...] = mesh_terms[rows_mesh : 2 * rows_mesh]
    to_above[...] = mesh_terms[2 * rows_mesh : 3 * rows_mesh].astype(jnp.bfloat16)
    grid_grad[...] = through(here, width).astype(jnp.bfloat16)
    done[...] = jnp.zeros(done.shape, jnp.float32)


def final_kernel(scalars, own, other, first, second):
    step = pl.program_id(0)
    rows = pl.ds(pl.multiple_of((step % 2) * 512, 512), 512)
    mine = (step // 2) == scalars[3]

    def put(into):
        @pl.when(mine)
        def _():
            into[...] = own[rows, :].astype(jnp.float32)

        @pl.when(jnp.logical_not(mine))
        def _():
            into[...] = other[rows, :].astype(jnp.float32)

    @pl.when(step < 3)
    def _():
        put(first)

    @pl.when(step == 3)
    def _():
        put(second)


def passed_along(value, steps):
    count = lax.axis_size("band") * lax.axis_size("mesh")
    leading, last = (max(0, -steps), min(count, count - steps))
    return lax.ppermute(value, ("band", "mesh"), [(s, s + steps) for s in range(leading, last)])


def swapped(value):
    return lax.ppermute(value, "rep", [(0, 1), (1, 0)])


def everywhere(value, axis):
    count = lax.axis_size(axis)
    return lax.all_to_all(jnp.broadcast_to(value[None], (count,) + value.shape), axis, 0, 0)


def per_device(
    grid_latent,
    mesh_latent,
    edge_latent,
    mesh_cotangent,
    w_first,
    w_second,
    norm_gain,
    senders,
    receivers,
    live_counts,
):
    width = w_second.shape[0]
    rows_grid = grid_latent.shape[1]
    rows_mesh = mesh_latent.shape[1]
    slots = senders.shape[0]
    bands, meshes = lax.axis_size("band"), lax.axis_size("mesh")
    factor = 1.0 / math.sqrt(slots * bands * meshes * lax.axis_size("rep"))
    shard = lax.axis_index(("band", "mesh"))
    scalars = jnp.stack(
        [
            shard * rows_grid,
            (shard - 1) * rows_mesh,
            live_counts[0],
            lax.axis_index("rep").astype(jnp.int32),
        ]
    ).astype(jnp.int32)
    senders, receivers = senders[None], receivers[None]
    gain = norm_gain[None]
    grid, mesh, edge, cot = grid_latent[0], mesh_latent[0], edge_latent[0], mesh_cotangent[0]
    matrix = functools.partial(jax.ShapeDtypeStruct, dtype=jnp.bfloat16)
    floats = functools.partial(jax.ShapeDtypeStruct, dtype=jnp.float32)
    unit = 2.0 * slots * width * width

    mesh_before, mesh_after = passed_along(mesh, 1), passed_along(mesh, -1)
    cot_before, cot_after = passed_along(cot, 1), passed_along(cot, -1)
    partial, grid_picked = call(
        near_kernel,
        "near",
        [in_smem()] + [in_vmem()] * 4,
        [floats((slots, width)), matrix((slots, width))],
        (scalars, senders, grid, edge, w_first),
        3 * unit,
    )
    sent, gain_term, grad_pre, grad_output, hidden, mesh_picked = call(
        edge_kernel,
        "edges",
        [in_smem()] + [in_vmem()] * 13,
        [matrix((2 * width + 16, width)), floats((8, width))] + [matrix((slots, width))] * 4,
        (
            scalars,
            receivers,
            partial,
            grid_picked,
            edge,
            mesh_before,
            mesh,
            mesh_after,
            cot_before,
            cot,
            cot_after,
            w_first,
            w_second,
            gain,
        ),
        7 * unit,
    )
    got = swapped(sent)
    (kept,) = call(
        kept_kernel,
        "kept",
        [in_smem()] + [in_vmem()] * 6,
        [floats((2 * width, width))],
        (scalars, edge, grid_picked, mesh_picked, hidden, grad_pre, grad_output),
        2 * unit,
    )
    part, piece = 2 * width // bands, 2 * width // (bands * meshes)
    (packed,) = call(
        pack_kernel,
        "pack",
        [in_vmem()] * 3,
        [matrix((bands, part + 8, width))],
        (kept, got, gain_term),
        0,
    )
    edge_grad, grid_grad, mesh_own, to_below, to_above, done = call(
        node_kernel,
        "nodes",
        [in_smem()] + [in_vmem()] * 4 + [anywhere()],
        [
            matrix((slots, width)),
            matrix((rows_grid, width)),
            floats((rows_mesh, width)),
            matrix((rows_mesh, width)),
            matrix((rows_mesh, width)),
            floats((8, LANES)),
        ],
        (scalars, senders, receivers, grad_pre, w_first, packed),
        4 * unit,
    )
    shares = lax.all_to_all(packed, "band", 0, 0)
    (packed,) = call(
        band_sum_kernel,
        "band_sum",
        [in_vmem(), anywhere()],
        [matrix((meshes, piece + 8, width))],
        (shares, done),
        0,
    )
    shares = lax.all_to_all(packed, "mesh", 0, 0)
    copies, gain_grad = call(
        functools.partial(mesh_sum_kernel, factor),
        "mesh_sum",
        [in_vmem()],
        [matrix((meshes, piece, width)), floats((8, width))],
        (shares,),
        0,
    )
    total = lax.all_to_all(copies, "mesh", 0, 0).reshape(part, width)
    total = everywhere(total, "band").reshape(2 * width, width)
    other = swapped(total)
    first_grad, second_grad = pl.pallas_call(
        final_kernel,
        grid=(4,),
        out_shape=[floats((3 * width, width)), floats((width, width))],
        in_specs=[in_smem()] + [in_vmem()] * 2,
        out_specs=[
            pl.BlockSpec((width, width), lambda i: (jnp.minimum(i, 2), 0)),
            pl.BlockSpec((width, width), lambda i: (0, 0)),
        ],
        compiler_params=pltpu.CompilerParams(vmem_limit_bytes=24 * MIB),
        name="final",
    )(scalars, total, other)

    from_above = passed_along(to_below, -1).astype(jnp.float32)
    from_below = passed_along(to_above, 1).astype(jnp.float32)
    mesh_grad = mesh_own + from_above + from_below
    return (
        grid_grad[None],
        mesh_grad[None],
        edge_grad[None],
        first_grad,
        second_grad,
        gain_grad[0],
    )


def solution(mesh):
    in_specs = (
        P("rep", ("band", "mesh"), None),
        P("rep", ("band", "mesh"), None),
        P("rep", ("band", "mesh"), None),
        P("rep", ("band", "mesh"), None),
        P(),
        P(),
        P(),
        P(("band", "mesh")),
        P(("band", "mesh")),
        P(("band", "mesh")),
    )
    out_specs = (
        P("rep", ("band", "mesh"), None),
        P("rep", ("band", "mesh"), None),
        P("rep", ("band", "mesh"), None),
        P(),
        P(),
        P(),
    )
    return jax.shard_map(
        per_device, mesh=mesh, in_specs=in_specs, out_specs=out_specs, check_vma=False
    )
```

time: 330 us -> 129 us (0.39)
  the two profiles are of different devices: /device:TPU:1 before, /device:TPU:2 now
where the time goes in v2:
time: 129 us
  blocking collectives  43.1 us (33%)
  starting transfers between devices  33.1 us (26%)
  waiting for transfers between devices  23.5 us (18%)
  Pallas kernels  20.2 us (16%)
  local copies, waits for them, and re-layouts  6.47 us (5%)
  between operations  1.48 us (1%)
    ppermute x6, starting transfers between devices, passed_along(): lax.ppermute(value, ('band', 'mesh'), [(s, s + steps) for s in range(lead...  28 us
    all_to_all x1, blocking collectives, everywhere(): lax.all_to_all(jnp.broadcast_to(value[None], (count,) + value.shape), axi...  17.4 us
    pallas_call x7, Pallas kernels, call(): pl.pallas_call(kernel, out_shape=outs, in_specs=specs, out_specs=[in_vmem...  16.9 us
    all_to_all x1, blocking collectives, per_device(): shares = lax.all_to_all(packed, 'mesh', 0, 0)  14.9 us
    all_to_all x1, waiting for transfers between devices, per_device(): shares = lax.all_to_all(packed, 'band', 0, 0)  11.5 us
    ppermute x6, waiting for transfers between devices, passed_along(): lax.ppermute(value, ('band', 'mesh'), [(s, s + steps) for s in range(lead...  11.2 us
    all_to_all x1, blocking collectives, per_device(): total = lax.all_to_all(copies, 'mesh', 0, 0).reshape(part, width)  10.8 us
    unnamed x26, local copies, waits for them, and re-layouts  5.8 us
  transfers between devices with their start and end apart: 9, of which 5 were waited for; matrix products, arithmetic and copies ran while one was open for 1% of the time, Pallas kernels for 7%

profile of v2, /device:TPU:2, one launch (start us, length us, event | category | flops | bytes accessed | tf_op | source)
XLA Modules:
  0.0 128.8 jit_solution(14711971801042035032)
XLA Ops:
  0.6 10.2 %collective-permute-start.1 = (bf16[128,512]{1,0:T(8,128)(2,1)}, bf16[128,512]{1,0:T(8,128)(2,1)S(1)}, u32[]{:S(2)}, u32[]{:S(2)}) collective-permute-start(bf16[128,512]{1,0:T(8,128)(2,1)} %bitcast.23), channel_id=1, source_target_pairs={{2,0},{4,2},{6,4},{8,6},{10,8},{12,10},{14,12},{16,14},{18,16},{20... | collective-permute-start | bytes 393224 | tf_op jit(solution)/shard_map/ppermute | solution.py:289
  10.8 1.9 %collective-permute-start = (bf16[128,512]{1,0:T(8,128)(2,1)}, bf16[128,512]{1,0:T(8,128)(2,1)S(1)}, u32[]{:S(2)}, u32[]{:S(2)}) collective-permute-start(bf16[128,512]{1,0:T(8,128)(2,1)} %bitcast.24), channel_id=1, source_target_pairs={{0,2},{2,4},{4,6},{6,8},{8,10},{10,12},{12,14},{14,16},{16,18},{18... | collective-permute-start | bytes 393224 | tf_op jit(solution)/shard_map/ppermute | solution.py:289
  12.8 8.1 %collective-permute-start.3 = (bf16[128,512]{1,0:T(8,128)(2,1)}, bf16[128,512]{1,0:T(8,128)(2,1)S(1)}, u32[]{:S(2)}, u32[]{:S(2)}) collective-permute-start(bf16[128,512]{1,0:T(8,128)(2,1)} %bitcast.26), channel_id=1, source_target_pairs={{2,0},{4,2},{6,4},{8,6},{10,8},{12,10},{14,12},{16,14},{18,16},{20... | collective-permute-start | bytes 393224 | tf_op jit(solution)/shard_map/ppermute | solution.py:289
  20.9 1.9 %collective-permute-start.2 = (bf16[128,512]{1,0:T(8,128)(2,1)}, bf16[128,512]{1,0:T(8,128)(2,1)S(1)}, u32[]{:S(2)}, u32[]{:S(2)}) collective-permute-start(bf16[128,512]{1,0:T(8,128)(2,1)} %bitcast.27), channel_id=1, source_target_pairs={{0,2},{2,4},{4,6},{6,8},{8,10},{10,12},{12,14},{14,16},{16,18},{18... | collective-permute-start | bytes 393224 | tf_op jit(solution)/shard_map/ppermute | solution.py:289
  23.6 1.2 copy-done
  24.8 1.4 %copy-done.2 = bf16[1536,512]{1,0:T(8,128)(2,1)S(1)} copy-done((bf16[1536,512]{1,0:T(8,128)(2,1)S(1)}, bf16[1536,512]{1,0:T(8,128)(2,1)}, u32[]{:S(2)}) %copy-start.2) | copy-done | bytes 1572888
  26.2 1.0 copy-done.5
  28.0 2.7 %near.1 = (f32[1024,512]{1,0:T(8,128)S(1)}, bf16[1024,512]{1,0:T(8,128)(2,1)S(1)}) custom-call(s32[4]{0:T(128)S(1)} %pad_add_fusion.scalars, s32[1,1024]{1,0:T(1,128)S(1)} %bitcast.29, bf16[512,512]{1,0:T(8,128)(2,1)S(1)} %bitcast.22, bf16[1024,512]{1,0:T(8,128)(2,1)S(1)} %bitcast.19, bf16[1536,512]{1,0:T(8,128)(2,1)S(1)} %copy-done.2), custom_call_target="tpu_custom_call" | custom-call | flops 1610612736 | bytes 6295568 | tf_op jit(solution)/shard_map/near/pallas_call | solution.py:70
  30.7 1.5 %collective-permute-done.2.cot_before = bf16[128,512]{1,0:T(8,128)(2,1)S(1)} collective-permute-done((bf16[128,512]{1,0:T(8,128)(2,1)}, bf16[128,512]{1,0:T(8,128)(2,1)S(1)}, u32[]{:S(2)}, u32[]{:S(2)}) %collective-permute-start.2) | collective-permute-done | bytes 131104 | tf_op jit(solution)/shard_map/ppermute | solution.py:289
  32.3 7.0 %edges.1 = (bf16[1040,512]{1,0:T(8,128)(2,1)S(1)}, f32[8,512]{1,0:T(8,128)S(1)}, bf16[1024,512]{1,0:T(8,128)(2,1)S(1)}, bf16[1024,512]{1,0:T(8,128)(2,1)S(1)}, b...) custom-call(s32[4]{0:T(128)S(1)} %pad_add_fusion.scalars, s32[1,1024]{1,0:T(1,128)S(1)} %bitcast.31, ...), custom_call_target="tpu_custom_call" | custom-call | flops 3758096384 | bytes 12359696 | tf_op jit(solution)/shard_map/edges/pallas_call | solution.py:70
  39.4 1.8 %kept.1 = f32[1024,512]{1,0:T(8,128)S(1)} custom-call(s32[4]{0:T(128)S(1)} %pad_add_fusion.scalars, bf16[1024,512]{1,0:T(8,128)(2,1)S(1)} %bitcast.21, bf16[1024,512]{1,0:T(8,128)(2,1)S(1)} %get-tuple-element.25.grid_picked, bf16[1024,512]{1,0:T(8,128)(2,1)S(1)} %get-tuple-element.27.mesh_picked, bf16[1024,512]{1,0:T(8,128)(2,1)S(1)} %get-tuple-element.28.hidden, ...), custom_call_target="tpu_custom_call" | custom-call | flops 1073741824 | bytes 8388624 | tf_op jit(solution)/shard_map/kept/pallas_call | solution.py:70
  42.0 1.2 pack.1.after
  43.2 5.0 %all-to-all-start = ((bf16[16,72,512]{2,1,0:T(8,128)(2,1)}), bf16[16,72,512]{2,1,0:T(8,128)(2,1)S(1)}, u32[]{:S(2)}, u32[]{:S(2)}) async-start(bf16[16,72,512]{2,1,0:T(8,128)(2,1)} %pack.1.after), calls=%async_computation | async-start | bytes 2359296 | tf_op jit(solution)/shard_map/all_to_all | solution.py:401
  48.3 1.4 %copy-done.4 = bf16[1536,512]{1,0:T(8,128)(2,1)S(1)} copy-done((bf16[1536,512]{1,0:T(8,128)(2,1)S(1)}, bf16[1536,512]{1,0:T(8,128)(2,1)}, u32[]{:S(2)}) %copy-start.4) | copy-done | bytes 1572888
  49.7 4.0 %nodes.1 = (bf16[1024,512]{1,0:T(8,128)(2,1)}, bf16[512,512]{1,0:T(8,128)(2,1)}, f32[128,512]{1,0:T(8,128)S(1)}, bf16[128,512]{1,0:T(8,128)(2,1)S(1)}, bf16[128,...) custom-call(s32[4]{0:T(128)S(1)} %pad_add_fusion.scalars, s32[1,1024]{1,0:T(1,128)S(1)} %bitcast.30, s32[1,1024]{1,0:T(1,128)S(1)} %bitcast.32, ...), custom_call_target="tpu_custom_call" | custom-call | flops 2147483648 | bytes 5910544 | tf_op jit(solution)/shard_map/nodes/pallas_call | solution.py:70
  53.6 11.5 %all-to-all-done.shares = bf16[16,72,512]{2,1,0:T(8,128)(2,1)S(1)} async-done(((bf16[16,72,512]{2,1,0:T(8,128)(2,1)}), bf16[16,72,512]{2,1,0:T(8,128)(2,1)S(1)}, u32[]{:S(2)}, u32[]{:S(2)}) %all-to-all-start) | async-done | bytes 1179680 | tf_op jit(solution)/shard_map/all_to_all | solution.py:401
  65.3 14.9 %all_to_all.20.shares = bf16[8,16,512]{2,1,0:T(8,128)(2,1)S(1)} all-to-all(bf16[8,16,512]{2,1,0:T(8,128)(2,1)S(1)} %band_sum.1), channel_id=1, replica_groups=mesh['band'=16,'mesh'=8,'rep'=2] {'mesh'}, dimensions={0} | all-to-all | bytes 262144 | tf_op jit(solution)/shard_map/all_to_all | solution.py:410
  80.2 10.8 %all_to_all.21 = bf16[8,8,512]{2,1,0:T(8,128)(2,1)S(1)} all-to-all(bf16[8,8,512]{2,1,0:T(8,128)(2,1)S(1)} %get-tuple-element.38), channel_id=1, replica_groups=mesh['band'=16,'mesh'=8,'rep'=2] {'mesh'}, dimensions={0} | all-to-all | bytes 131072 | tf_op jit(solution)/shard_map/all_to_all | solution.py:419
  91.1 17.4 %all_to_all.22 = bf16[16,64,512]{2,1,0:T(8,128)(2,1)S(1)} all-to-all(bf16[16,64,512]{2,1,0:T(8,128)(2,1)S(1)} %broadcast_in_dim.32), channel_id=1, replica_groups=mesh['band'=16,'mesh'=8,'rep'=2] {'band'}, dimensions={0} | all-to-all | bytes 2097152 | tf_op jit(solution)/shard_map/all_to_all | solution.py:298
  108.5 3.8 %collective-permute-start.5 = (bf16[128,512]{1,0:T(8,128)(2,1)S(1)}, bf16[128,512]{1,0:T(8,128)(2,1)S(1)}, u32[]{:S(2)}, u32[]{:S(2)}) collective-permute-start(bf16[128,512]{1,0:T(8,128)(2,1)S(1)} %get-tuple-element.34), channel_id=1, source_target_pairs={{2,0},{4,2},{6,4},{8,6},{10,8},{12,10},{14,12},{16,14},{18,16},{20... | collective-permute-start | bytes 393224 | tf_op jit(solution)/shard_map/ppermute | solution.py:289
  112.3 2.0 %collective-permute-start.6 = (bf16[128,512]{1,0:T(8,128)(2,1)S(1)}, bf16[128,512]{1,0:T(8,128)(2,1)S(1)}, u32[]{:S(2)}, u32[]{:S(2)}) collective-permute-start(bf16[128,512]{1,0:T(8,128)(2,1)S(1)} %get-tuple-element.35), channel_id=1, source_target_pairs={{0,2},{2,4},{4,6},{6,8},{8,10},{10,12},{12,14},{14,16},{16,18},{18... | collective-permute-start | bytes 393224 | tf_op jit(solution)/shard_map/ppermute | solution.py:289
  114.3 1.9 %collective-permute-done.5 = bf16[128,512]{1,0:T(8,128)(2,1)S(1)} collective-permute-done((bf16[128,512]{1,0:T(8,128)(2,1)S(1)}, bf16[128,512]{1,0:T(8,128)(2,1)S(1)}, u32[]{:S(2)}, u32[]{:S(2)}) %collective-permute-start.5) | collective-permute-done | bytes 131104 | tf_op jit(solution)/shard_map/ppermute | solution.py:289
  116.3 7.8 %collective-permute-done.6 = bf16[128,512]{1,0:T(8,128)(2,1)S(1)} collective-permute-done((bf16[128,512]{1,0:T(8,128)(2,1)S(1)}, bf16[128,512]{1,0:T(8,128)(2,1)S(1)}, u32[]{:S(2)}, u32[]{:S(2)}) %collective-permute-start.6) | collective-permute-done | bytes 131104 | tf_op jit(solution)/shard_map/ppermute | solution.py:289
  125.4 3.4 %final.1 = (f32[1536,512]{1,0:T(8,128)}, f32[512,512]{1,0:T(8,128)}) custom-call(s32[4]{0:T(128)S(1)} %pad_add_fusion.scalars, bf16[1024,512]{1,0:T(8,128)(2,1)S(1)} %bitcast.18, bf16[1024,512]{1,0:T(8,128)(2,1)S(1)} %collective-permute-done.7.other), custom_call_target="tpu_custom_call" | custom-call | tf_op jit(solution)/shard_map/final/pallas_call | solution.py:422
  (35 shorter events, 3.4 us)
Async XLA Ops:
  0.6 30.0 %collective-permute-start.1 = (bf16[128,512]{1,0:T(8,128)(2,1)}, bf16[128,512]{1,0:T(8,128)(2,1)S(1)}, u32[]{:S(2)}, u32[]{:S(2)}) collective-permute-start(bf16[128,512]{1,0:T(8,128)(2,1)} %bitcast.23), channel_id=1, source_target_pairs={{2,0},{4,2},{6,4},{8,6},{10,8},{12,10},{14,12},{16,14},{18,16},{20... | collective-permute-start | bytes 393224 | tf_op jit(solution)/shard_map/ppermute | solution.py:289
  10.8 19.9 %collective-permute-start = (bf16[128,512]{1,0:T(8,128)(2,1)}, bf16[128,512]{1,0:T(8,128)(2,1)S(1)}, u32[]{:S(2)}, u32[]{:S(2)}) collective-permute-start(bf16[128,512]{1,0:T(8,128)(2,1)} %bitcast.24), channel_id=1, source_target_pairs={{0,2},{2,4},{4,6},{6,8},{8,10},{10,12},{12,14},{14,16},{16,18},{18... | collective-permute-start | bytes 393224 | tf_op jit(solution)/shard_map/ppermute | solution.py:289
  12.8 17.9 %collective-permute-start.3 = (bf16[128,512]{1,0:T(8,128)(2,1)}, bf16[128,512]{1,0:T(8,128)(2,1)S(1)}, u32[]{:S(2)}, u32[]{:S(2)}) collective-permute-start(bf16[128,512]{1,0:T(8,128)(2,1)} %bitcast.26), channel_id=1, source_target_pairs={{2,0},{4,2},{6,4},{8,6},{10,8},{12,10},{14,12},{16,14},{18,16},{20... | collective-permute-start | bytes 393224 | tf_op jit(solution)/shard_map/ppermute | solution.py:289
  20.9 11.3 %collective-permute-start.2 = (bf16[128,512]{1,0:T(8,128)(2,1)}, bf16[128,512]{1,0:T(8,128)(2,1)S(1)}, u32[]{:S(2)}, u32[]{:S(2)}) collective-permute-start(bf16[128,512]{1,0:T(8,128)(2,1)} %bitcast.27), channel_id=1, source_target_pairs={{0,2},{2,4},{4,6},{6,8},{8,10},{10,12},{12,14},{14,16},{16,18},{18... | collective-permute-start | bytes 393224 | tf_op jit(solution)/shard_map/ppermute | solution.py:289
  23.6 1.2 copy-start
  24.8 1.4 %copy-start.2 = (bf16[1536,512]{1,0:T(8,128)(2,1)S(1)}, bf16[1536,512]{1,0:T(8,128)(2,1)}, u32[]{:S(2)}) copy-start(bf16[1536,512]{1,0:T(8,128)(2,1)} %w_first.5) | copy-start | bytes 4718596
  26.2 1.0 copy-start.5
  27.2 0.7 copy-start.9
  27.9 4.3 %copy-start.1 = (bf16[1,1024,512]{2,1,0:T(8,128)(2,1)S(1)}, bf16[1,1024,512]{2,1,0:T(8,128)(2,1)}, u32[]{:S(2)}) copy-start(bf16[1,1024,512]{2,1,0:T(8,128)(2,1)} %param.12) | copy-start | bytes 3145732
  27.9 4.3 %copy-start.3 = (bf16[1536,512]{1,0:T(8,128)(2,1)S(1)}, bf16[1536,512]{1,0:T(8,128)(2,1)}, u32[]{:S(2)}) copy-start(bf16[1536,512]{1,0:T(8,128)(2,1)} %w_first.5) | copy-start | bytes 4718596
  27.9 4.3 %copy-start.6 = (bf16[512,512]{1,0:T(8,128)(2,1)S(1)}, bf16[512,512]{1,0:T(8,128)(2,1)}, u32[]{:S(2)}) copy-start(bf16[512,512]{1,0:T(8,128)(2,1)} %w_second.1) | copy-start | bytes 1572868
  27.9 4.3 %copy-start.7 = (bf16[1,128,512]{2,1,0:T(8,128)(2,1)S(1)}, bf16[1,128,512]{2,1,0:T(8,128)(2,1)}, u32[]{:S(2)}) copy-start(bf16[1,128,512]{2,1,0:T(8,128)(2,1)} %param.11) | copy-start | bytes 393220
  27.9 4.3 %copy-start.8 = (bf16[1,128,512]{2,1,0:T(8,128)(2,1)S(1)}, bf16[1,128,512]{2,1,0:T(8,128)(2,1)}, u32[]{:S(2)}) copy-start(bf16[1,128,512]{2,1,0:T(8,128)(2,1)} %param.13) | copy-start | bytes 393220
  28.0 4.3 %copy-start.11 = (s32[1024]{0:T(1024)S(1)}, s32[1024]{0:T(1024)}, u32[]{:S(2)}) copy-start(s32[1024]{0:T(1024)} %param.18) | copy-start | bytes 12292
  28.0 4.3 %copy-start.12 = (f32[512]{0:T(512)S(1)}, f32[512]{0:T(512)}, u32[]{:S(2)}) copy-start(f32[512]{0:T(512)} %param.16) | copy-start | bytes 6148
  39.3 2.8 %collective-permute-start.4 = (bf16[1040,512]{1,0:T(8,128)(2,1)S(1)}, bf16[1040,512]{1,0:T(8,128)(2,1)S(1)}, u32[]{:S(2)}, u32[]{:S(2)}) collective-permute-start(bf16[1040,512]{1,0:T(8,128)(2,1)S(1)} %get-tuple-element.30), channel_id=1, source_target_pairs={{0,1},{1,0},{2,3},{3,2},{4,5},{5,4},{6,7},{7,6},{8,9},{9,8},{10,11... | collective-permute-start | bytes 3194888 | tf_op jit(solution)/shard_map/ppermute | solution.py:293
  43.2 5.0 %copy-start.10 = (s32[1024]{0:T(1024)S(1)}, s32[1024]{0:T(1024)}, u32[]{:S(2)}) copy-start(s32[1024]{0:T(1024)} %param.17) | copy-start | bytes 12292
  43.2 21.9 %all-to-all-start = ((bf16[16,72,512]{2,1,0:T(8,128)(2,1)}), bf16[16,72,512]{2,1,0:T(8,128)(2,1)S(1)}, u32[]{:S(2)}, u32[]{:S(2)}) async-start(bf16[16,72,512]{2,1,0:T(8,128)(2,1)} %pack.1.after), calls=%async_computation | async-start | bytes 2359296 | tf_op jit(solution)/shard_map/all_to_all | solution.py:401
  48.2 1.4 %copy-start.4 = (bf16[1536,512]{1,0:T(8,128)(2,1)S(1)}, bf16[1536,512]{1,0:T(8,128)(2,1)}, u32[]{:S(2)}) copy-start(bf16[1536,512]{1,0:T(8,128)(2,1)} %w_first.5) | copy-start | bytes 4718596
  108.5 16.9 %collective-permute-start.7 = (bf16[1024,512]{1,0:T(8,128)(2,1)S(1)}, bf16[1024,512]{1,0:T(8,128)(2,1)S(1)}, u32[]{:S(2)}, u32[]{:S(2)}) collective-permute-start(bf16[1024,512]{1,0:T(8,128)(2,1)S(1)} %bitcast.17), channel_id=1, source_target_pairs={{0,1},{1,0},{2,3},{3,2},{4,5},{5,4},{6,7},{7,6},{8,9},{9,8},{10,11... | collective-permute-start | bytes 3145736 | tf_op jit(solution)/shard_map/ppermute | solution.py:293
  108.5 7.8 %collective-permute-start.5 = (bf16[128,512]{1,0:T(8,128)(2,1)S(1)}, bf16[128,512]{1,0:T(8,128)(2,1)S(1)}, u32[]{:S(2)}, u32[]{:S(2)}) collective-permute-start(bf16[128,512]{1,0:T(8,128)(2,1)S(1)} %get-tuple-element.34), channel_id=1, source_target_pairs={{2,0},{4,2},{6,4},{8,6},{10,8},{12,10},{14,12},{16,14},{18,16},{20... | collective-permute-start | bytes 393224 | tf_op jit(solution)/shard_map/ppermute | solution.py:289
  112.3 11.7 %collective-permute-start.6 = (bf16[128,512]{1,0:T(8,128)(2,1)S(1)}, bf16[128,512]{1,0:T(8,128)(2,1)S(1)}, u32[]{:S(2)}, u32[]{:S(2)}) collective-permute-start(bf16[128,512]{1,0:T(8,128)(2,1)S(1)} %get-tuple-element.35), channel_id=1, source_target_pairs={{0,2},{2,4},{4,6},{6,8},{8,10},{10,12},{12,14},{14,16},{16,18},{18... | collective-permute-start | bytes 393224 | tf_op jit(solution)/shard_map/ppermute | solution.py:289

commit v3 on v2

v3 whole, which is shorter than its diff:
```python
import functools
import math

import jax
import jax.numpy as jnp
from jax import lax
from jax.experimental import pallas as pl
from jax.experimental.pallas import tpu as pltpu
from jax.sharding import PartitionSpec as P

NORM_EPS = 1e-05
SHARDS = ("band", "hi", "lo")
GROUP = ("band", "lo")
TILE = 256
LANES = 128
MIB = 1 << 20


def dot(left, right, left_dim=1, right_dim=0):
    return lax.dot_general(
        left,
        right,
        (((left_dim,), (right_dim,)), ((), ())),
        preferred_element_type=jnp.float32,
    )


def picks(row, width):
    edges = row.shape[1]
    column = jnp.transpose(jnp.broadcast_to(row, (LANES, edges)))
    lane = lax.broadcasted_iota(jnp.int32, (edges, LANES), 1)
    return jnp.concatenate(
        [(column == lane + start).astype(jnp.float32).astype(jnp.bfloat16) for start in range(0, width, LANES)],
        axis=1,
    )


def spreads(row, width):
    edges = row.shape[1]
    place = lax.broadcasted_iota(jnp.int32, (width, edges), 0)
    return (place == row).astype(jnp.float32).astype(jnp.bfloat16)


def upper_lower(value):
    upper = value.astype(jnp.bfloat16)
    return upper, (value - upper.astype(jnp.float32)).astype(jnp.bfloat16)


def gain_rows(gain, lanes):
    terms = [term.astype(jnp.float32) for term in upper_lower(gain)]
    count = gain.shape[1] // lanes
    return jnp.concatenate(
        [term[:, g * lanes : (g + 1) * lanes] for term in terms for g in range(count)], axis=0
    )


def gain_of(rows):
    count = rows.shape[0] // 2
    return jnp.concatenate([rows[g : g + 1] + rows[count + g : count + g + 1] for g in range(count)], axis=1)


def narrow(rows):
    return jnp.concatenate(
        [rows[:, g : g + LANES] for g in range(0, rows.shape[1], LANES)], axis=0
    )


def anywhere():
    return pl.BlockSpec(memory_space=pl.ANY)


def in_vmem():
    return pl.BlockSpec(memory_space=pltpu.VMEM)


def in_hbm():
    return pl.BlockSpec(memory_space=pltpu.HBM)


def in_smem():
    return pl.BlockSpec(memory_space=pltpu.SMEM)


def call(kernel, name, specs, outs, operands, flops, scratch=(), limit=24 * MIB):
    operands = [
        pltpu.with_memory_space_constraint(o, pltpu.HBM) if spec.memory_space == pltpu.HBM else o
        for o, spec in zip(operands, specs)
    ]
    size = sum(math.prod(o.shape) * jnp.dtype(o.dtype).itemsize for o in outs)
    size += sum(math.prod(o.shape) * jnp.dtype(o.dtype).itemsize for o in operands)
    return pl.pallas_call(
        kernel,
        out_shape=outs,
        in_specs=specs,
        out_specs=[in_vmem()] * len(outs),
        scratch_shapes=list(scratch),
        compiler_params=pltpu.CompilerParams(vmem_limit_bytes=limit),
        cost_estimate=pl.CostEstimate(flops=int(flops), bytes_accessed=size, transcendentals=0),
        name=name,
    )(*operands)


def stack_kernel(mesh, cot, stacked, sems):
    rows = mesh.shape[0]
    copies = [
        pltpu.make_async_copy(mesh, stacked.at[pl.ds(0, rows)], sems.at[0]),
        pltpu.make_async_copy(cot, stacked.at[pl.ds(rows, rows)], sems.at[1]),
    ]
    for copy in copies:
        copy.start()
    for copy in copies:
        copy.wait()


def near_kernel(
    scalars,
    senders,
    grid,
    edge,
    w_first,
    partial,
    grid_picked,
    senders_here,
    grid_here,
    edge_here,
    w_here,
    sems,
):
    rows_grid, width = grid.shape
    copies = [
        pltpu.make_async_copy(senders, senders_here, sems.at[0]),
        pltpu.make_async_copy(grid, grid_here, sems.at[1]),
        pltpu.make_async_copy(w_first.at[pl.ds(0, 2 * width)], w_here, sems.at[2]),
    ]
    tiles = range(0, edge.shape[0], TILE)
    for place, start in enumerate(tiles):
        rows = pl.ds(start, TILE)
        copies.append(pltpu.make_async_copy(edge.at[rows], edge_here.at[rows], sems.at[place + 3]))
    for copy in copies:
        copy.start()
    for copy in copies[:3]:
        copy.wait()
    for start, copy in zip(tiles, copies[3:]):
        rows = pl.ds(start, TILE)
        table = picks(senders_here[:, rows] - scalars[0], rows_grid)
        picked = dot(table, grid_here[...]).astype(jnp.bfloat16)
        grid_picked[rows, :] = picked
        copy.wait()
        partial[rows, :] = dot(edge_here[rows, :], w_here[0:width, :]) + dot(
            picked, w_here[width : 2 * width, :]
        )


def live_receivers(scalars, receivers, start):
    row = receivers[:, pl.ds(start, TILE)] - scalars[1]
    slot = start + lax.broadcasted_iota(jnp.int32, (1, TILE), 1)
    return jnp.where(slot < scalars[2], row, -1)


def edge_kernel(
    scalars,
    receivers,
    partial,
    grid_picked,
    edge,
    stack_before,
    stack_own,
    stack_after,
    w_first,
    w_second,
    norm_gain,
    sent,
    gain_term,
    grad_pre,
    grad_output,
    hidden,
    mesh_picked,
):
    width = w_second.shape[0]
    rows_mesh = stack_own.shape[0] // 2
    gain_sum = jnp.zeros((1, width), jnp.float32)
    for start in range(0, edge.shape[0], TILE):
        rows = pl.ds(start, TILE)
        table = picks(live_receivers(scalars, receivers, start), 3 * rows_mesh)

        def picked_rows(first):
            part = pl.ds(first, rows_mesh)
            near = jnp.concatenate([stack_before[part, :], stack_own[part, :], stack_after[part, :]], axis=0)
            return dot(table, near)

        latents = picked_rows(0).astype(jnp.bfloat16)
        upstream = picked_rows(rows_mesh)
        mesh_picked[rows, :] = latents
        pre_act = partial[rows, :] + dot(latents, w_first[2 * width : 3 * width, :])
        sigmoid = jax.nn.sigmoid(pre_act)
        hid = (pre_act * sigmoid).astype(jnp.bfloat16)
        hidden[rows, :] = hid
        output = dot(hid, w_second[...])
        centered = output - jnp.mean(output, axis=1, keepdims=True)
        inverse = lax.rsqrt(jnp.mean(centered * centered, axis=1, keepdims=True) + NORM_EPS)
        normed = centered * inverse
        gain_sum = gain_sum + jnp.sum(upstream * normed, axis=0, keepdims=True)
        scaled = upstream * norm_gain[...]
        grad_out = (
            inverse
            * (
                scaled
                - jnp.mean(scaled, axis=1, keepdims=True)
                - normed * jnp.mean(scaled * normed, axis=1, keepdims=True)
            )
        ).astype(jnp.bfloat16)
        grad_output[rows, :] = grad_out
        grad_hidden = dot(grad_out, w_second[...], 1, 1)
        grad_pre[rows, :] = (grad_hidden * sigmoid * (1.0 + pre_act * (1.0 - sigmoid))).astype(
            jnp.bfloat16
        )
    gain_term[...] = jnp.broadcast_to(gain_sum, gain_term.shape)
    sent[2 * width : 2 * width + 16, :] = jnp.concatenate(
        [gain_rows(gain_sum, width), jnp.zeros((14, width), jnp.float32)], axis=0
    ).astype(jnp.bfloat16)

    @pl.when(scalars[3] == 0)
    def _():
        sent[0:width, :] = dot(mesh_picked[...], grad_pre[...], 0, 0).astype(jnp.bfloat16)
        sent[width : 2 * width, :] = dot(hidden[...], grad_output[...], 0, 0).astype(jnp.bfloat16)

    @pl.when(scalars[3] != 0)
    def _():
        sent[0:width, :] = dot(edge[...], grad_pre[...], 0, 0).astype(jnp.bfloat16)
        sent[width : 2 * width, :] = dot(grid_picked[...], grad_pre[...], 0, 0).astype(jnp.bfloat16)


def kept_kernel(scalars, edge, grid_picked, mesh_picked, hidden, grad_pre, grad_output, kept):
    width = grad_pre.shape[1]

    @pl.when(scalars[3] != 0)
    def _():
        kept[0:width, :] = dot(mesh_picked[...], grad_pre[...], 0, 0)
        kept[width : 2 * width, :] = dot(hidden[...], grad_output[...], 0, 0)

    @pl.when(scalars[3] == 0)
    def _():
        kept[0:width, :] = dot(edge[...], grad_pre[...], 0, 0)
        kept[width : 2 * width, :] = dot(grid_picked[...], grad_pre[...], 0, 0)


def pack_kernel(kept, got, gain_term, packed, done):
    count = packed.shape[0]
    half, width = kept.shape
    part = half // count
    tail = got[half : half + 16, :].astype(jnp.float32)
    gain = gain_rows(gain_term[0:1, :] + gain_of(tail[0:2]), LANES)
    for place in range(count):
        rows = pl.ds(place * part, part)
        data = narrow(kept[rows, :] + got[rows, :].astype(jnp.float32))
        packed[place] = jnp.concatenate([data, gain], axis=0).astype(jnp.bfloat16)
    done[...] = jnp.zeros(done.shape, jnp.float32)


def group_sum_kernel(shares, after, copies):
    total = shares[0].astype(jnp.float32)
    for place in range(1, shares.shape[0]):
        total = total + shares[place].astype(jnp.float32)
    data = total.shape[0] - 8
    gain = gain_rows(gain_of(total[data:]), LANES)
    row = jnp.concatenate([total[:data], gain], axis=0).astype(jnp.bfloat16)
    for place in range(copies.shape[0]):
        copies[place] = row


def whole_sum_kernel(factor, shares, copies, gain_grad):
    total = shares[0].astype(jnp.float32)
    for place in range(1, shares.shape[0]):
        total = total + shares[place].astype(jnp.float32)
    total = total * factor
    data = copies.shape[1]
    gain_grad[...] = jnp.broadcast_to(gain_of(total[data:]), gain_grad.shape)
    share = total[:data].astype(jnp.bfloat16)
    for place in range(copies.shape[0]):
        copies[place] = share


def node_kernel(
    scalars,
    senders,
    receivers,
    grad_pre,
    w_first,
    after,
    edge_grad,
    grid_grad,
    mesh_own,
    to_below,
    to_above,
):
    edges, width = grad_pre.shape
    rows_grid, rows_mesh = grid_grad.shape[0], mesh_own.shape[0]

    def through(sums, first):
        upper, lower = upper_lower(sums)
        weights = w_first[first : first + width, :]
        return dot(upper, weights, 1, 1) + dot(lower, weights, 1, 1)

    near = jnp.zeros((3 * rows_mesh, width), jnp.float32)
    here = jnp.zeros((rows_grid, width), jnp.float32)
    for start in range(0, edges, TILE):
        rows = pl.ds(start, TILE)
        terms = grad_pre[rows, :]
        near = near + dot(spreads(live_receivers(scalars, receivers, start), 3 * rows_mesh), terms)
        here = here + dot(spreads(senders[:, rows] - scalars[0], rows_grid), terms)
        edge_grad[rows, :] = dot(terms, w_first[0:width, :], 1, 1).astype(jnp.bfloat16)
    mesh_terms = through(near, 2 * width)
    to_below[...] = mesh_terms[0:rows_mesh].astype(jnp.bfloat16)
    mesh_own[...] = mesh_terms[rows_mesh : 2 * rows_mesh]
    to_above[...] = mesh_terms[2 * rows_mesh : 3 * rows_mesh].astype(jnp.bfloat16)
    grid_grad[...] = through(here, width).astype(jnp.bfloat16)


def final_kernel(scalars, own, other, first, second):
    step = pl.program_id(0)
    height, width = first.shape
    part = own.shape[1] * LANES // width
    shares = height // part
    blocks = own.shape[0] // shares
    mine = (step // blocks) == scalars[3]

    def put(into):
        def put_from(half):
            for place in range(shares):
                share = half[(step % blocks) * shares + place].astype(jnp.float32)
                for g in range(width // LANES):
                    into[place * part : (place + 1) * part, g * LANES : (g + 1) * LANES] = share[
                        g * part : (g + 1) * part
                    ]

        @pl.when(mine)
        def _():
            put_from(own)

        @pl.when(jnp.logical_not(mine))
        def _():
            put_from(other)

    @pl.when(step * height < 3 * width)
    def _():
        put(first)

    @pl.when(step * height >= 3 * width)
    def _():
        put(second)


def passed_along(value, steps):
    count = lax.axis_size(SHARDS)
    leading, last = (max(0, -steps), min(count, count - steps))
    return lax.ppermute(value, SHARDS, [(s, s + steps) for s in range(leading, last)])


def swapped(value):
    return lax.ppermute(value, "rep", [(0, 1), (1, 0)])


def per_device(
    grid_latent,
    mesh_latent,
    edge_latent,
    mesh_cotangent,
    w_first,
    w_second,
    norm_gain,
    senders,
    receivers,
    live_counts,
):
    width = w_second.shape[0]
    rows_grid = grid_latent.shape[1]
    rows_mesh = mesh_latent.shape[1]
    slots = senders.shape[0]
    group, groups = lax.axis_size(GROUP), lax.axis_size("hi")
    factor = 1.0 / math.sqrt(slots * group * groups * lax.axis_size("rep"))
    shard = lax.axis_index(SHARDS)
    scalars = jnp.stack(
        [
            shard * rows_grid,
            (shard - 1) * rows_mesh,
            live_counts[0],
            lax.axis_index("rep").astype(jnp.int32),
        ]
    ).astype(jnp.int32)
    senders, receivers = senders[None], receivers[None]
    gain = norm_gain[None]
    grid, mesh, edge, cot = grid_latent[0], mesh_latent[0], edge_latent[0], mesh_cotangent[0]
    matrix = functools.partial(jax.ShapeDtypeStruct, dtype=jnp.bfloat16)
    floats = functools.partial(jax.ShapeDtypeStruct, dtype=jnp.float32)
    unit = 2.0 * slots * width * width

    (stacked,) = call(
        stack_kernel,
        "stack",
        [in_hbm()] * 2,
        [matrix((2 * rows_mesh, width))],
        (mesh, cot),
        0,
        [pltpu.SemaphoreType.DMA((2,))],
    )
    stack_before, stack_after = passed_along(stacked, 1), passed_along(stacked, -1)
    partial, grid_picked = call(
        near_kernel,
        "near",
        [in_smem()] + [in_hbm()] * 4,
        [floats((slots, width)), matrix((slots, width))],
        (scalars, senders, grid, edge, w_first),
        3 * unit,
        [
            pltpu.VMEM((1, slots), jnp.int32),
            pltpu.VMEM((rows_grid, width), jnp.bfloat16),
            pltpu.VMEM((slots, width), jnp.bfloat16),
            pltpu.VMEM((2 * width, width), jnp.bfloat16),
            pltpu.SemaphoreType.DMA((3 + slots // TILE,)),
        ],
    )
    sent, gain_term, grad_pre, grad_output, hidden, mesh_picked = call(
        edge_kernel,
        "edges",
        [in_smem()] + [in_vmem()] * 10,
        [
            matrix((2 * width + 16, width)),
            floats((8, width)),
            pltpu.VMEM((slots, width), jnp.bfloat16),
        ]
        + [matrix((slots, width))] * 3,
        (
            scalars,
            receivers,
            partial,
            grid_picked,
            edge,
            stack_before,
            stacked,
            stack_after,
            w_first,
            w_second,
            gain,
        ),
        7 * unit,
    )
    got = swapped(sent)
    (kept,) = call(
        kept_kernel,
        "kept",
        [in_smem()] + [in_vmem()] * 6,
        [floats((2 * width, width))],
        (scalars, edge, grid_picked, mesh_picked, hidden, grad_pre, grad_output),
        2 * unit,
    )
    part = 2 * width // group * width // LANES
    extra = 2 * width // LANES
    packed, done = call(
        pack_kernel,
        "pack",
        [in_vmem()] * 3,
        [matrix((group, part + extra, LANES)), floats((8, LANES))],
        (kept, got, gain_term),
        0,
    )
    edge_grad, grid_grad, mesh_own, to_below, to_above = call(
        node_kernel,
        "nodes",
        [in_smem()] + [in_vmem()] * 4 + [anywhere()],
        [
            matrix((slots, width)),
            matrix((rows_grid, width)),
            floats((rows_mesh, width)),
            matrix((rows_mesh, width)),
            matrix((rows_mesh, width)),
        ],
        (scalars, senders, receivers, grad_pre, w_first, done),
        4 * unit,
    )
    from_above = passed_along(to_below, -1).astype(jnp.float32)
    from_below = passed_along(to_above, 1).astype(jnp.float32)
    mesh_grad = mesh_own + from_above + from_below
    shares = lax.all_to_all(packed, GROUP, 0, 0)
    (copies,) = call(
        group_sum_kernel,
        "group_sum",
        [in_vmem(), anywhere()],
        [matrix((groups, part + extra, LANES))],
        (shares, mesh_grad),
        0,
    )
    shares = lax.all_to_all(copies, "hi", 0, 0)
    copies, gain_grad = call(
        functools.partial(whole_sum_kernel, factor),
        "whole_sum",
        [in_vmem()],
        [matrix((group, part, LANES)), floats((8, width))],
        (shares,),
        0,
    )
    total = lax.all_to_all(copies, GROUP, 0, 0)
    other = swapped(total)
    steps, height = 8, width // 2
    first_grad, second_grad = pl.pallas_call(
        final_kernel,
        grid=(steps,),
        out_shape=[floats((3 * width, width)), floats((width, width))],
        in_specs=[in_smem()] + [in_vmem()] * 2,
        out_specs=[
            pl.BlockSpec((height, width), lambda i: (jnp.minimum(i, 5), 0)),
            pl.BlockSpec((height, width), lambda i: (jnp.maximum(i - 6, 0), 0)),
        ],
        compiler_params=pltpu.CompilerParams(vmem_limit_bytes=24 * MIB),
        name="final",
    )(scalars, total, other)
    return (
        grid_grad[None],
        mesh_grad[None],
        edge_grad[None],
        first_grad,
        second_grad,
        gain_grad[0],
    )


def solution(mesh):
    bands, meshes, cores = mesh.devices.shape
    mesh = jax.sharding.Mesh(
        mesh.devices.reshape(bands, meshes // 2, 2, cores), ("band", "hi", "lo", "rep")
    )
    in_specs = (
        P("rep", SHARDS, None),
        P("rep", SHARDS, None),
        P("rep", SHARDS, None),
        P("rep", SHARDS, None),
        P(),
        P(),
        P(),
        P(SHARDS),
        P(SHARDS),
        P(SHARDS),
    )
    out_specs = (
        P("rep", SHARDS, None),
        P("rep", SHARDS, None),
        P("rep", SHARDS, None),
        P(),
        P(),
        P(),
    )
    return jax.shard_map(
        per_device, mesh=mesh, in_specs=in_specs, out_specs=out_specs, check_vma=False
    )
```

time: 129 us -> 102 us (0.79)
  the two profiles are of different devices: /device:TPU:2 before, /device:TPU:1 now
where the time goes in v3:
time: 102 us
  starting transfers between devices  33.1 us (32%)
  blocking collectives  31.5 us (31%)
  Pallas kernels  24.3 us (24%)
  waiting for transfers between devices  9.35 us (9%)
  local copies, waits for them, and re-layouts  2.01 us (2%)
  between operations  1.47 us (1%)
    all_to_all x1, blocking collectives, per_device(): total = lax.all_to_all(copies, GROUP, 0, 0)  21.8 us
    pallas_call x8, Pallas kernels, call(): pl.pallas_call(kernel, out_shape=outs, in_specs=specs, out_specs=[in_vmem...  20 us
    all_to_all x1, starting transfers between devices, per_device(): shares = lax.all_to_all(packed, GROUP, 0, 0)  15.6 us
    ppermute x4, starting transfers between devices, passed_along(): lax.ppermute(value, SHARDS, [(s, s + steps) for s in range(leading, last)])  11.6 us
    all_to_all x1, blocking collectives, per_device(): shares = lax.all_to_all(copies, 'hi', 0, 0)  9.71 us
    ppermute x2, starting transfers between devices, swapped(): return lax.ppermute(value, 'rep', [(0, 1), (1, 0)])  5.88 us
    ppermute x4, waiting for transfers between devices, passed_along(): lax.ppermute(value, SHARDS, [(s, s + steps) for s in range(leading, last)])  5.37 us
    pallas_call x1, Pallas kernels, per_device(): pl.pallas_call(final_kernel, grid=(steps,), out_shape=[floats((3 * width,...  4.32 us
  transfers between devices with their start and end apart: 7, of which 4 were waited for; matrix products, arithmetic and copies ran while one was open for 1% of the time, Pallas kernels for 10%

profile of v3, /device:TPU:1, one launch (start us, length us, event | category | flops | bytes accessed | tf_op | source)
XLA Modules:
  0.0 101.9 jit_solution(7050095931241948398)
XLA Ops:
  0.6 1.0 stack.17.stack_own
  1.6 1.3 %collective-permute-start.1 = (bf16[256,512]{1,0:T(8,128)(2,1)S(1)}, bf16[256,512]{1,0:T(8,128)(2,1)S(1)}, u32[]{:S(2)}, u32[]{:S(2)}) collective-permute-start(bf16[256,512]{1,0:T(8,128)(2,1)S(1)} %stack.17.stack_own), channel_id=1, source_target_pairs={{2,0},{4,2},{6,4},{8,6},{10,8},{12,10},{14,12},{16,14},{18,16},{20... | collective-permute-start | bytes 786440 | tf_op jit(solution)/shard_map/ppermute | solution.py:356
  2.9 5.0 %collective-permute-start = (bf16[256,512]{1,0:T(8,128)(2,1)S(1)}, bf16[256,512]{1,0:T(8,128)(2,1)S(1)}, u32[]{:S(2)}, u32[]{:S(2)}) collective-permute-start(bf16[256,512]{1,0:T(8,128)(2,1)S(1)} %stack.17.stack_own), channel_id=1, source_target_pairs={{0,2},{2,4},{4,6},{6,8},{8,10},{10,12},{12,14},{14,16},{16,18},{18... | collective-permute-start | bytes 786440 | tf_op jit(solution)/shard_map/ppermute | solution.py:356
  8.7 4.8 %near.1 = (f32[1024,512]{1,0:T(8,128)S(1)}, bf16[1024,512]{1,0:T(8,128)(2,1)S(1)}) custom-call(s32[4]{0:T(128)S(1)} %pad_add_fusion.scalars, s32[1,1024]{1,0:T(1,128)} %bitcast.18, bf16[512,512]{1,0:T(8,128)(2,1)} %bitcast.26, bf16[1024,512]{1,0:T(8,128)(2,1)} %bitcast.14, bf16[1536,512]{1,0:T(8,128)(2,1)} %w_first.5), custom_call_target="tpu_custom_call" | custom-call | flops 1610612736 | bytes 6295568 | tf_op jit(solution)/shard_map/near/pallas_call | solution.py:91
  13.6 7.0 %edges.1 = (bf16[1040,512]{1,0:T(8,128)(2,1)S(1)}, f32[8,512]{1,0:T(8,128)S(1)}, bf16[1024,512]{1,0:T(8,128)(2,1)S(1)}, bf16[1024,512]{1,0:T(8,128)(2,1)S(1)}, b...) custom-call(s32[4]{0:T(128)S(1)} %pad_add_fusion.scalars, s32[1,1024]{1,0:T(1,128)S(1)} %bitcast.20, ...), custom_call_target="tpu_custom_call" | custom-call | flops 3758096384 | bytes 12359696 | tf_op jit(solution)/shard_map/edges/pallas_call | solution.py:91
  20.6 2.9 %collective-permute-start.2 = (bf16[1040,512]{1,0:T(8,128)(2,1)S(1)}, bf16[1040,512]{1,0:T(8,128)(2,1)S(1)}, u32[]{:S(2)}, u32[]{:S(2)}) collective-permute-start(bf16[1040,512]{1,0:T(8,128)(2,1)S(1)} %get-tuple-element.31), channel_id=1, source_target_pairs={{0,1},{1,0},{2,3},{3,2},{4,5},{5,4},{6,7},{7,6},{8,9},{9,8},{10,11... | collective-permute-start | bytes 3194888 | tf_op jit(solution)/shard_map/ppermute | solution.py:360
  23.5 1.8 %kept.1 = f32[1024,512]{1,0:T(8,128)S(1)} custom-call(s32[4]{0:T(128)S(1)} %pad_add_fusion.scalars, bf16[1024,512]{1,0:T(8,128)(2,1)S(1)} %bitcast.16, bf16[1024,512]{1,0:T(8,128)(2,1)S(1)} %get-tuple-element.26.grid_picked, bf16[1024,512]{1,0:T(8,128)(2,1)S(1)} %get-tuple-element.28.mesh_picked, bf16[1024,512]{1,0:T(8,128)(2,1)S(1)} %get-tuple-element.29.hidden, ...), custom_call_target="tpu_custom_call" | custom-call | flops 1073741824 | bytes 8388624 | tf_op jit(solution)/shard_map/kept/pallas_call | solution.py:91
  25.3 0.5 collective-permute-done.2.got
  25.8 1.2 %pack.1 = (bf16[32,136,128]{2,1,0:T(8,128)(2,1)}, f32[8,128]{1,0:T(8,128)S(1)}) custom-call(f32[1024,512]{1,0:T(8,128)S(1)} %kept.1, bf16[1040,512]{1,0:T(8,128)(2,1)S(1)} %collective-permute-done.2.got, f32[8,512]{1,0:T(8,128)S(1)} %get-tuple-element.32.gain_term), custom_call_target="tpu_custom_call" | custom-call | bytes 4296704 | tf_op jit(solution)/shard_map/pack/pallas_call | solution.py:91
  26.9 15.6 %all-to-all-start = ((bf16[32,136,128]{2,1,0:T(8,128)(2,1)}), bf16[32,136,128]{2,1,0:T(8,128)(2,1)S(1)}, u32[]{:S(2)}, u32[]{:S(2)}) async-start(bf16[32,136,128]{2,1,0:T(8,128)(2,1)} %get-tuple-element.39), calls=%async_computation | async-start | bytes 2228224 | tf_op jit(solution)/shard_map/all_to_all | solution.py:483
  42.6 1.4 %copy-done.3 = bf16[1536,512]{1,0:T(8,128)(2,1)S(1)} copy-done((bf16[1536,512]{1,0:T(8,128)(2,1)S(1)}, bf16[1536,512]{1,0:T(8,128)(2,1)}, u32[]{:S(2)}) %copy-start.3) | copy-done | bytes 1572888
  44.0 4.0 %nodes.1 = (bf16[1024,512]{1,0:T(8,128)(2,1)}, bf16[512,512]{1,0:T(8,128)(2,1)}, f32[128,512]{1,0:T(8,128)S(1)}, bf16[128,512]{1,0:T(8,128)(2,1)S(1)}, bf16[128,512]{1,0:T(8,128)(2,1)S(1)}) custom-call(s32[4]{0:T(128)S(1)} %pad_add_fusion.scalars, s32[1,1024]{1,0:T(1,128)S(1)} %bitcast.19, s32[1,1024]{1,0:T(1,128)S(1)} %bitcast.21, ...), custom_call_target="tpu_custom_call" | custom-call | flops 2147483648 | bytes 4730896 | tf_op jit(solution)/shard_map/nodes/pallas_call | solution.py:91
  48.0 1.3 %collective-permute-start.3 = (bf16[128,512]{1,0:T(8,128)(2,1)S(1)}, bf16[128,512]{1,0:T(8,128)(2,1)S(1)}, u32[]{:S(2)}, u32[]{:S(2)}) collective-permute-start(bf16[128,512]{1,0:T(8,128)(2,1)S(1)} %get-tuple-element.36), channel_id=1, source_target_pairs={{2,0},{4,2},{6,4},{8,6},{10,8},{12,10},{14,12},{16,14},{18,16},{20... | collective-permute-start | bytes 393224 | tf_op jit(solution)/shard_map/ppermute | solution.py:356
  49.3 4.0 %collective-permute-start.4 = (bf16[128,512]{1,0:T(8,128)(2,1)S(1)}, bf16[128,512]{1,0:T(8,128)(2,1)S(1)}, u32[]{:S(2)}, u32[]{:S(2)}) collective-permute-start(bf16[128,512]{1,0:T(8,128)(2,1)S(1)} %get-tuple-element.37), channel_id=1, source_target_pairs={{0,2},{2,4},{4,6},{6,8},{8,10},{10,12},{12,14},{14,16},{16,18},{18... | collective-permute-start | bytes 393224 | tf_op jit(solution)/shard_map/ppermute | solution.py:356
  53.3 5.4 %collective-permute-done.3 = bf16[128,512]{1,0:T(8,128)(2,1)S(1)} collective-permute-done((bf16[128,512]{1,0:T(8,128)(2,1)S(1)}, bf16[128,512]{1,0:T(8,128)(2,1)S(1)}, u32[]{:S(2)}, u32[]{:S(2)}) %collective-permute-start.3) | collective-permute-done | bytes 131104 | tf_op jit(solution)/shard_map/ppermute | solution.py:356
  58.7 1.8 %all-to-all-done.shares = bf16[32,136,128]{2,1,0:T(8,128)(2,1)S(1)} async-done(((bf16[32,136,128]{2,1,0:T(8,128)(2,1)}), bf16[32,136,128]{2,1,0:T(8,128)(2,1)S(1)}, u32[]{:S(2)}, u32[]{:S(2)}) %all-to-all-start) | async-done | bytes 1114144 | tf_op jit(solution)/shard_map/all_to_all | solution.py:483
  60.5 0.2 group_sum.1
  60.7 9.7 %all_to_all.15.shares = bf16[4,136,128]{2,1,0:T(8,128)(2,1)S(1)} all-to-all(bf16[4,136,128]{2,1,0:T(8,128)(2,1)S(1)} %group_sum.1), channel_id=1, replica_groups=mesh['band'=16,'hi'=4,'lo'=2,'rep'=2] {'hi'}, dimensions={0} | all-to-all | bytes 278528 | tf_op jit(solution)/shard_map/all_to_all | solution.py:492
  70.4 0.1 whole_sum.1
  70.5 21.8 %all_to_all.16.own = bf16[32,128,128]{2,1,0:T(8,128)(2,1)S(1)} all-to-all(bf16[32,128,128]{2,1,0:T(8,128)(2,1)S(1)} %get-tuple-element.40), channel_id=1, replica_groups=mesh['band'=16,'hi'=4,'lo'=2,'rep'=2] {'band','lo'}, dimensions={0} | all-to-all | bytes 2097152 | tf_op jit(solution)/shard_map/all_to_all | solution.py:501
  92.3 3.0 %collective-permute-start.5 = (bf16[32,128,128]{2,1,0:T(8,128)(2,1)S(1)}, bf16[32,128,128]{2,1,0:T(8,128)(2,1)S(1)}, u32[]{:S(2)}, u32[]{:S(2)}) collective-permute-start(bf16[32,128,128]{2,1,0:T(8,128)(2,1)S(1)} %all_to_all.16.own), channel_id=1, source_target_pairs={{0,1},{1,0},{2,3},{3,2},{4,5},{5,4},{6,7},{7,6},{8,9},{9,8},{10,11... | collective-permute-start | bytes 3145736 | tf_op jit(solution)/shard_map/ppermute | solution.py:360
  95.3 0.6 slice.3
  95.9 1.7 %collective-permute-done.5.other = bf16[32,128,128]{2,1,0:T(8,128)(2,1)S(1)} collective-permute-done((bf16[32,128,128]{2,1,0:T(8,128)(2,1)S(1)}, bf16[32,128,128]{2,1,0:T(8,128)(2,1)S(1)}, u32[]{:S(2)}, u32[]{:S(2)}) %collective-permute-start.5) | collective-permute-done | bytes 1048608 | tf_op jit(solution)/shard_map/ppermute | solution.py:360
  97.6 4.3 %final.1 = (f32[1536,512]{1,0:T(8,128)}, f32[512,512]{1,0:T(8,128)}) custom-call(s32[4]{0:T(128)S(1)} %pad_add_fusion.scalars, bf16[32,128,128]{2,1,0:T(8,128)(2,1)S(1)} %all_to_all.16.own, bf16[32,128,128]{2,1,0:T(8,128)(2,1)S(1)} %collective-permute-done.5.other), custom_call_target="tpu_custom_call" | custom-call | tf_op jit(solution)/shard_map/final/pallas_call | solution.py:504
  (20 shorter events, 0.2 us)
Async XLA Ops:
  1.6 11.9 %collective-permute-start.1 = (bf16[256,512]{1,0:T(8,128)(2,1)S(1)}, bf16[256,512]{1,0:T(8,128)(2,1)S(1)}, u32[]{:S(2)}, u32[]{:S(2)}) collective-permute-start(bf16[256,512]{1,0:T(8,128)(2,1)S(1)} %stack.17.stack_own), channel_id=1, source_target_pairs={{2,0},{4,2},{6,4},{8,6},{10,8},{12,10},{14,12},{16,14},{18,16},{20... | collective-permute-start | bytes 786440 | tf_op jit(solution)/shard_map/ppermute | solution.py:356
  2.9 10.6 %collective-permute-start = (bf16[256,512]{1,0:T(8,128)(2,1)S(1)}, bf16[256,512]{1,0:T(8,128)(2,1)S(1)}, u32[]{:S(2)}, u32[]{:S(2)}) collective-permute-start(bf16[256,512]{1,0:T(8,128)(2,1)S(1)} %stack.17.stack_own), channel_id=1, source_target_pairs={{0,2},{2,4},{4,6},{6,8},{8,10},{10,12},{12,14},{14,16},{16,18},{18... | collective-permute-start | bytes 786440 | tf_op jit(solution)/shard_map/ppermute | solution.py:356
  8.7 4.8 %copy-start = (bf16[1,1024,512]{2,1,0:T(8,128)(2,1)S(1)}, bf16[1,1024,512]{2,1,0:T(8,128)(2,1)}, u32[]{:S(2)}) copy-start(bf16[1,1024,512]{2,1,0:T(8,128)(2,1)} %param.12) | copy-start | bytes 3145732
  8.7 4.8 %copy-start.2 = (bf16[1536,512]{1,0:T(8,128)(2,1)S(1)}, bf16[1536,512]{1,0:T(8,128)(2,1)}, u32[]{:S(2)}) copy-start(bf16[1536,512]{1,0:T(8,128)(2,1)} %w_first.5) | copy-start | bytes 4718596
  8.7 4.9 %copy-start.4 = (bf16[512,512]{1,0:T(8,128)(2,1)S(1)}, bf16[512,512]{1,0:T(8,128)(2,1)}, u32[]{:S(2)}) copy-start(bf16[512,512]{1,0:T(8,128)(2,1)} %w_second.1) | copy-start | bytes 1572868
  8.7 4.9 %copy-start.6 = (s32[1024]{0:T(1024)S(1)}, s32[1024]{0:T(1024)}, u32[]{:S(2)}) copy-start(s32[1024]{0:T(1024)} %param.18) | copy-start | bytes 12292
  8.7 4.9 %copy-start.7 = (f32[512]{0:T(512)S(1)}, f32[512]{0:T(512)}, u32[]{:S(2)}) copy-start(f32[512]{0:T(512)} %param.16) | copy-start | bytes 6148
  20.6 5.2 %collective-permute-start.2 = (bf16[1040,512]{1,0:T(8,128)(2,1)S(1)}, bf16[1040,512]{1,0:T(8,128)(2,1)S(1)}, u32[]{:S(2)}, u32[]{:S(2)}) collective-permute-start(bf16[1040,512]{1,0:T(8,128)(2,1)S(1)} %get-tuple-element.31), channel_id=1, source_target_pairs={{0,1},{1,0},{2,3},{3,2},{4,5},{5,4},{6,7},{7,6},{8,9},{9,8},{10,11... | collective-permute-start | bytes 3194888 | tf_op jit(solution)/shard_map/ppermute | solution.py:360
  26.9 15.6 %copy-start.5 = (s32[1024]{0:T(1024)S(1)}, s32[1024]{0:T(1024)}, u32[]{:S(2)}) copy-start(s32[1024]{0:T(1024)} %param.17) | copy-start | bytes 12292
  26.9 33.5 %all-to-all-start = ((bf16[32,136,128]{2,1,0:T(8,128)(2,1)}), bf16[32,136,128]{2,1,0:T(8,128)(2,1)S(1)}, u32[]{:S(2)}, u32[]{:S(2)}) async-start(bf16[32,136,128]{2,1,0:T(8,128)(2,1)} %get-tuple-element.39), calls=%async_computation | async-start | bytes 2228224 | tf_op jit(solution)/shard_map/all_to_all | solution.py:483
  42.6 1.4 %copy-start.3 = (bf16[1536,512]{1,0:T(8,128)(2,1)S(1)}, bf16[1536,512]{1,0:T(8,128)(2,1)}, u32[]{:S(2)}) copy-start(bf16[1536,512]{1,0:T(8,128)(2,1)} %w_first.5) | copy-start | bytes 4718596
  48.0 10.7 %collective-permute-start.3 = (bf16[128,512]{1,0:T(8,128)(2,1)S(1)}, bf16[128,512]{1,0:T(8,128)(2,1)S(1)}, u32[]{:S(2)}, u32[]{:S(2)}) collective-permute-start(bf16[128,512]{1,0:T(8,128)(2,1)S(1)} %get-tuple-element.36), channel_id=1, source_target_pairs={{2,0},{4,2},{6,4},{8,6},{10,8},{12,10},{14,12},{16,14},{18,16},{20... | collective-permute-start | bytes 393224 | tf_op jit(solution)/shard_map/ppermute | solution.py:356
  49.3 9.4 %collective-permute-start.4 = (bf16[128,512]{1,0:T(8,128)(2,1)S(1)}, bf16[128,512]{1,0:T(8,128)(2,1)S(1)}, u32[]{:S(2)}, u32[]{:S(2)}) collective-permute-start(bf16[128,512]{1,0:T(8,128)(2,1)S(1)} %get-tuple-element.37), channel_id=1, source_target_pairs={{0,2},{2,4},{4,6},{6,8},{8,10},{10,12},{12,14},{14,16},{16,18},{18... | collective-permute-start | bytes 393224 | tf_op jit(solution)/shard_map/ppermute | solution.py:356
  58.7 33.6 %copy-start.1 = (f32[128,512]{1,0:T(8,128)}, f32[128,512]{1,0:T(8,128)S(1)}, u32[]{:S(2)}) copy-start(f32[128,512]{1,0:T(8,128)S(1)} %convert_add_fusion.after) | copy-start | bytes 786436
  92.3 5.3 %collective-permute-start.5 = (bf16[32,128,128]{2,1,0:T(8,128)(2,1)S(1)}, bf16[32,128,128]{2,1,0:T(8,128)(2,1)S(1)}, u32[]{:S(2)}, u32[]{:S(2)}) collective-permute-start(bf16[32,128,128]{2,1,0:T(8,128)(2,1)S(1)} %all_to_all.16.own), channel_id=1, source_target_pairs={{0,1},{1,0},{2,3},{3,2},{4,5},{5,4},{6,7},{7,6},{8,9},{9,8},{10,11... | collective-permute-start | bytes 3145736 | tf_op jit(solution)/shard_map/ppermute | solution.py:360

commit v4 on v3

--- a/solution.py
+++ b/solution.py
@@ -118,37 +118,46 @@
     grid,
     edge,
     w_first,
+    w_second,
     partial,
     grid_picked,
+    edge_here,
+    w_first_here,
+    w_second_here,
     senders_here,
     grid_here,
-    edge_here,
-    w_here,
     sems,
 ):
     rows_grid, width = grid.shape
+    tiles = range(0, edge.shape[0], TILE)
+    pairs = [(senders, senders_here), (grid, grid_here)]
+    for first in (width, 0):
+        rows = pl.ds(first, width)
+        pairs.append((w_first.at[rows], w_first_here.at[rows]))
+    for start in tiles:
+        rows = pl.ds(start, TILE)
+        pairs.append((edge.at[rows], edge_here.at[rows]))
+    rows = pl.ds(2 * width, width)
+    pairs += [(w_first.at[rows], w_first_here.at[rows]), (w_second, w_second_here)]
     copies = [
-        pltpu.make_async_copy(senders, senders_here, sems.at[0]),
-        pltpu.make_async_copy(grid, grid_here, sems.at[1]),
-        pltpu.make_async_copy(w_first.at[pl.ds(0, 2 * width)], w_here, sems.at[2]),
+        pltpu.make_async_copy(source, target, sems.at[place])
+        for place, (source, target) in enumerate(pairs)
     ]
-    tiles = range(0, edge.shape[0], TILE)
-    for place, start in enumerate(tiles):
-        rows = pl.ds(start, TILE)
-        copies.append(pltpu.make_async_copy(edge.at[rows], edge_here.at[rows], sems.at[place + 3]))
     for copy in copies:
         copy.start()
-    for copy in copies[:3]:
+    for copy in copies[:4]:
         copy.wait()
-    for start, copy in zip(tiles, copies[3:]):
+    for start, copy in zip(tiles, copies[4:]):
         rows = pl.ds(start, TILE)
         table = picks(senders_here[:, rows] - scalars[0], rows_grid)
         picked = dot(table, grid_here[...]).astype(jnp.bfloat16)
         grid_picked[rows, :] = picked
         copy.wait()
-        partial[rows, :] = dot(edge_here[rows, :], w_here[0:width, :]) + dot(
-            picked, w_here[width : 2 * width, :]
+        partial[rows, :] = dot(edge_here[rows, :], w_first_here[0:width, :]) + dot(
+            picked, w_first_here[width : 2 * width, :]
         )
+    for copy in copies[-2:]:
+        copy.wait()
 
 
 def live_receivers(scalars, receivers, start):
@@ -268,7 +277,7 @@
         copies[place] = row
 
 
-def whole_sum_kernel(factor, shares, copies, gain_grad):
+def whole_sum_kernel(factor, shares, after, copies, gain_grad):
     total = shares[0].astype(jnp.float32)
     for place in range(1, shares.shape[0]):
         total = total + shares[place].astype(jnp.float32)
@@ -316,38 +325,48 @@
     grid_grad[...] = through(here, width).astype(jnp.bfloat16)
 
 
-def final_kernel(scalars, own, other, first, second):
-    step = pl.program_id(0)
-    height, width = first.shape
-    part = own.shape[1] * LANES // width
-    shares = height // part
-    blocks = own.shape[0] // shares
-    mine = (step // blocks) == scalars[3]
-
-    def put(into):
-        def put_from(half):
-            for place in range(shares):
-                share = half[(step % blocks) * shares + place].astype(jnp.float32)
-                for g in range(width // LANES):
-                    into[place * part : (place + 1) * part, g * LANES : (g + 1) * LANES] = share[
-                        g * part : (g + 1) * part
-                    ]
-
-        @pl.when(mine)
+def put_half(scalars, flip, shares, first, second, wide, sems):
+    half, width = wide.shape
+    count = shares.shape[0]
+    part = half // count
+    half_index = 1 - scalars[3] if flip else scalars[3]
+    size = sems.shape[0]
+    rows = half // size
+
+    def each(place, act):
+        source = wide.at[pl.ds(place * rows, rows)]
+
+        @pl.when(half_index == 0)
         def _():
-            put_from(own)
-
-        @pl.when(jnp.logical_not(mine))
+            act(pltpu.make_async_copy(source, first.at[pl.ds(place * rows, rows)], sems.at[place]))
+
+        @pl.when(half_index != 0)
         def _():
-            put_from(other)
-
-    @pl.when(step * height < 3 * width)
-    def _():
-        put(first)
-
-    @pl.when(step * height >= 3 * width)
-    def _():
-        put(second)
+            start = half + place * rows
+            if start < first.shape[0]:
+                target = first.at[pl.ds(start, rows)]
+            else:
+                target = second.at[pl.ds(start - first.shape[0], rows)]
+            act(pltpu.make_async_copy(source, target, sems.at[place]))
+
+    for place in range(size):
+        for index in range(place * count // size, (place + 1) * count // size):
+            share = shares[index].astype(jnp.float32)
+            for g in range(width // LANES):
+                wide[index * part : (index + 1) * part, g * LANES : (g + 1) * LANES] = share[
+                    g * part : (g + 1) * part
+                ]
+        each(place, lambda copy: copy.start())
+    for place in range(size):
+        each(place, lambda copy: copy.wait())
+
+
+def own_half_kernel(scalars, shares, first, second, wide, sems):
+    put_half(scalars, False, shares, first, second, wide, sems)
+
+
+def other_half_kernel(scalars, shares, first_in, second_in, first, second, wide, sems):
+    put_half(scalars, True, shares, first, second, wide, sems)
 
 
 def passed_along(value, steps):
@@ -404,19 +423,23 @@
         [pltpu.SemaphoreType.DMA((2,))],
     )
     stack_before, stack_after = passed_along(stacked, 1), passed_along(stacked, -1)
-    partial, grid_picked = call(
+    partial, grid_picked, edge, w_first, w_second = call(
         near_kernel,
         "near",
-        [in_smem()] + [in_hbm()] * 4,
-        [floats((slots, width)), matrix((slots, width))],
-        (scalars, senders, grid, edge, w_first),
+        [in_smem()] + [in_hbm()] * 5,
+        [
+            floats((slots, width)),
+            matrix((slots, width)),
+            pltpu.VMEM((slots, width), jnp.bfloat16),
+            pltpu.VMEM((3 * width, width), jnp.bfloat16),
+            pltpu.VMEM((width, width), jnp.bfloat16),
+        ],
+        (scalars, senders, grid, edge, w_first, w_second),
         3 * unit,
         [
             pltpu.VMEM((1, slots), jnp.int32),
             pltpu.VMEM((rows_grid, width), jnp.bfloat16),
-            pltpu.VMEM((slots, width), jnp.bfloat16),
-            pltpu.VMEM((2 * width, width), jnp.bfloat16),
-            pltpu.SemaphoreType.DMA((3 + slots // TILE,)),
+            pltpu.SemaphoreType.DMA((6 + slots // TILE,)),
         ],
     )
     sent, gain_term, grad_pre, grad_output, hidden, mesh_picked = call(
@@ -486,33 +509,39 @@
         "group_sum",
         [in_vmem(), anywhere()],
         [matrix((groups, part + extra, LANES))],
-        (shares, mesh_grad),
+        (shares, mesh_own),
         0,
     )
     shares = lax.all_to_all(copies, "hi", 0, 0)
     copies, gain_grad = call(
         functools.partial(whole_sum_kernel, factor),
         "whole_sum",
-        [in_vmem()],
+        [in_vmem(), anywhere()],
         [matrix((group, part, LANES)), floats((8, width))],
-        (shares,),
+        (shares, mesh_grad),
         0,
     )
     total = lax.all_to_all(copies, GROUP, 0, 0)
     other = swapped(total)
-    steps, height = 8, width // 2
-    first_grad, second_grad = pl.pallas_call(
-        final_kernel,
-        grid=(steps,),
-        out_shape=[floats((3 * width, width)), floats((width, width))],
-        in_specs=[in_smem()] + [in_vmem()] * 2,
-        out_specs=[
-            pl.BlockSpec((height, width), lambda i: (jnp.minimum(i, 5), 0)),
-            pl.BlockSpec((height, width), lambda i: (jnp.maximum(i - 6, 0), 0)),
+    outs = [floats((3 * width, width)), floats((width, width))]
+    halves = functools.partial(
+        pl.pallas_call,
+        out_shape=outs,
+        out_specs=[in_hbm()] * 2,
+        scratch_shapes=[
+            pltpu.VMEM((2 * width, width), jnp.float32),
+            pltpu.SemaphoreType.DMA((8,)),
         ],
         compiler_params=pltpu.CompilerParams(vmem_limit_bytes=24 * MIB),
-        name="final",
-    )(scalars, total, other)
+        cost_estimate=pl.CostEstimate(flops=0, bytes_accessed=6 * MIB, transcendentals=0),
+    )
+    written = halves(own_half_kernel, in_specs=[in_smem(), in_vmem()], name="own_half")(scalars, total)
+    first_grad, second_grad = halves(
+        other_half_kernel,
+        in_specs=[in_smem(), in_vmem()] + [in_hbm()] * 2,
+        input_output_aliases={2: 0, 3: 1},
+        name="other_half",
+    )(scalars, other, *written)
     return (
         grid_grad[None],
         mesh_grad[None],

time: 102 us -> 99.9 us (0.979)
  blocking collectives: 31.5 us -> 19.8 us
  waiting for transfers between devices: 9.35 us -> 14.9 us
  starting transfers between devices: 33.1 us -> 36.5 us
    all_to_all x1 -> x0, blocking collectives: 9.71 us -> none  [per_device(): shares = lax.all_to_all(copies, 'hi', 0, 0)]
    all_to_all x0 -> x1, waiting for transfers between devices: none -> 7.21 us  [per_device(): shares = lax.all_to_all(copies, 'hi', 0, 0)]
    all_to_all x1, waiting for transfers between devices: 1.8 us -> 7.22 us  [per_device(): shares = lax.all_to_all(packed, GROUP, 0, 0)]
    ppermute x4, waiting for transfers between devices: 5.37 us -> 0.01 us  [passed_along(): lax.ppermute(value, SHARDS, [(s, s + steps) for s in range(leading, last)])]
    all_to_all x0 -> x1, starting transfers between devices: none -> 3.33 us  [per_device(): shares = lax.all_to_all(copies, 'hi', 0, 0)]
    all_to_all x1, blocking collectives: 21.8 us -> 19.8 us  [per_device(): total = lax.all_to_all(copies, GROUP, 0, 0)]
    ppermute x2, waiting for transfers between devices: 2.18 us -> 0.48 us  [swapped(): return lax.ppermute(value, 'rep', [(0, 1), (1, 0)])]
    pallas_call x1 -> x2, Pallas kernels: 4.32 us -> 3.87 us  [the longest x1 1.94 us: per_device(): halves(other_half_kernel, in_specs=[in_smem(), in_vmem()] + [in_hbm()] *...]
  transfers between devices with their start and end apart: 7 -> 8, of which waited for: 4 -> 3; matrix products, arithmetic and copies ran while one was open for 1% -> 1% of each run, Pallas kernels for 10% -> 13%
where the time goes in v4:
time: 99.9 us; the launch traced here: 99.4 us
  starting transfers between devices  36.5 us (37%)
  Pallas kernels  24.3 us (24%)
  blocking collectives  19.8 us (20%)
  waiting for transfers between devices  14.9 us (15%)
  local copies, waits for them, and re-layouts  2.01 us (2%)
  between operations  1.66 us (2%)
    pallas_call x8, Pallas kernels, call(): pl.pallas_call(kernel, out_shape=outs, in_specs=specs, out_specs=[in_vmem...  20.5 us
    all_to_all x1, blocking collectives, per_device(): total = lax.all_to_all(copies, GROUP, 0, 0)  19.8 us
    all_to_all x1, starting transfers between devices, per_device(): shares = lax.all_to_all(packed, GROUP, 0, 0)  15.9 us
    ppermute x4, starting transfers between devices, passed_along(): lax.ppermute(value, SHARDS, [(s, s + steps) for s in range(leading, last)])  11.6 us
    all_to_all x1, waiting for transfers between devices, per_device(): shares = lax.all_to_all(packed, GROUP, 0, 0)  7.22 us
    all_to_all x1, waiting for transfers between devices, per_device(): shares = lax.all_to_all(copies, 'hi', 0, 0)  7.21 us
    ppermute x2, starting transfers between devices, swapped(): return lax.ppermute(value, 'rep', [(0, 1), (1, 0)])  5.69 us
    all_to_all x1, starting transfers between devices, per_device(): shares = lax.all_to_all(copies, 'hi', 0, 0)  3.33 us
  transfers between devices with their start and end apart: 8, of which 3 were waited for; matrix products, arithmetic and copies ran while one was open for 1% of the time, Pallas kernels for 13%

profile of v4, /device:TPU:1, one launch (start us, length us, event | category | flops | bytes accessed | tf_op | source)
XLA Modules:
  0.0 99.4 jit_solution(13207707768117845022)
XLA Ops:
  0.6 1.0 stack.17.stack_own
  1.6 1.3 %collective-permute-start.1 = (bf16[256,512]{1,0:T(8,128)(2,1)S(1)}, bf16[256,512]{1,0:T(8,128)(2,1)S(1)}, u32[]{:S(2)}, u32[]{:S(2)}) collective-permute-start(bf16[256,512]{1,0:T(8,128)(2,1)S(1)} %stack.17.stack_own), channel_id=1, source_target_pairs={{2,0},{4,2},{6,4},{8,6},{10,8},{12,10},{14,12},{16,14},{18,16},{20... | collective-permute-start | bytes 786440 | tf_op jit(solution)/shard_map/ppermute | solution.py:375
  2.9 5.0 %collective-permute-start = (bf16[256,512]{1,0:T(8,128)(2,1)S(1)}, bf16[256,512]{1,0:T(8,128)(2,1)S(1)}, u32[]{:S(2)}, u32[]{:S(2)}) collective-permute-start(bf16[256,512]{1,0:T(8,128)(2,1)S(1)} %stack.17.stack_own), channel_id=1, source_target_pairs={{0,2},{2,4},{4,6},{6,8},{8,10},{10,12},{12,14},{14,16},{16,18},{18... | collective-permute-start | bytes 786440 | tf_op jit(solution)/shard_map/ppermute | solution.py:375
  8.7 4.5 %near.1 = (f32[1024,512]{1,0:T(8,128)S(1)}, bf16[1024,512]{1,0:T(8,128)(2,1)S(1)}, bf16[1024,512]{1,0:T(8,128)(2,1)S(1)}, bf16[1536,512]{1,0:T(8,128)(2,1)S(1)}, bf16[512,512]{1,0:T(8,128)(2,1)S(1)}) custom-call(s32[4]{0:T(128)S(1)} %pad_add_fusion.scalars, s32[1,1024]{1,0:T(1,128)} %bitcast.15, bf16[512,512]{1,0:T(8,128)(2,1)} %bitcast.24, ...), custom_call_target="tpu_custom_call" | custom-call | flops 1610612736 | bytes 9965584 | tf_op jit(solution)/shard_map/near/pallas_call | solution.py:91
  13.3 7.0 %edges.1 = (bf16[1040,512]{1,0:T(8,128)(2,1)S(1)}, f32[8,512]{1,0:T(8,128)S(1)}, bf16[1024,512]{1,0:T(8,128)(2,1)S(1)}, bf16[1024,512]{1,0:T(8,128)(2,1)S(1)}, b...) custom-call(s32[4]{0:T(128)S(1)} %pad_add_fusion.scalars, s32[1,1024]{1,0:T(1,128)S(1)} %bitcast.17, ...), custom_call_target="tpu_custom_call" | custom-call | flops 3758096384 | bytes 12359696 | tf_op jit(solution)/shard_map/edges/pallas_call | solution.py:91
  20.3 2.9 %collective-permute-start.2 = (bf16[1040,512]{1,0:T(8,128)(2,1)S(1)}, bf16[1040,512]{1,0:T(8,128)(2,1)S(1)}, u32[]{:S(2)}, u32[]{:S(2)}) collective-permute-start(bf16[1040,512]{1,0:T(8,128)(2,1)S(1)} %get-tuple-element.39), channel_id=1, source_target_pairs={{0,1},{1,0},{2,3},{3,2},{4,5},{5,4},{6,7},{7,6},{8,9},{9,8},{10,11... | collective-permute-start | bytes 3194888 | tf_op jit(solution)/shard_map/ppermute | solution.py:379
  23.2 1.8 %kept.1 = f32[1024,512]{1,0:T(8,128)S(1)} custom-call(s32[4]{0:T(128)S(1)} %pad_add_fusion.scalars, bf16[1024,512]{1,0:T(8,128)(2,1)S(1)} %get-tuple-element.32.edge, bf16[1024,512]{1,0:T(8,128)(2,1)S(1)} %get-tuple-element.31.grid_picked, bf16[1024,512]{1,0:T(8,128)(2,1)S(1)} %get-tuple-element.36.mesh_picked, ...), custom_call_target="tpu_custom_call" | custom-call | flops 1073741824 | bytes 8388624 | tf_op jit(solution)/shard_map/kept/pallas_call | solution.py:91
  25.0 0.5 collective-permute-done.2.got
  25.5 1.2 %pack.1 = (bf16[32,136,128]{2,1,0:T(8,128)(2,1)}, f32[8,128]{1,0:T(8,128)S(1)}) custom-call(f32[1024,512]{1,0:T(8,128)S(1)} %kept.1, bf16[1040,512]{1,0:T(8,128)(2,1)S(1)} %collective-permute-done.2.got, f32[8,512]{1,0:T(8,128)S(1)} %get-tuple-element.40.gain_term), custom_call_target="tpu_custom_call" | custom-call | bytes 4296704 | tf_op jit(solution)/shard_map/pack/pallas_call | solution.py:91
  26.7 15.9 %all-to-all-start = ((bf16[32,136,128]{2,1,0:T(8,128)(2,1)}), bf16[32,136,128]{2,1,0:T(8,128)(2,1)S(1)}, u32[]{:S(2)}, u32[]{:S(2)}) async-start(bf16[32,136,128]{2,1,0:T(8,128)(2,1)} %get-tuple-element.47), calls=%async_computation | async-start | bytes 2228224 | tf_op jit(solution)/shard_map/all_to_all | solution.py:506
  42.7 1.4 %copy-done.5 = bf16[1536,512]{1,0:T(8,128)(2,1)S(1)} copy-done((bf16[1536,512]{1,0:T(8,128)(2,1)S(1)}, bf16[1536,512]{1,0:T(8,128)(2,1)}, u32[]{:S(2)}) %copy-start.5) | copy-done | bytes 1572888
  44.1 4.0 %nodes.1 = (bf16[1024,512]{1,0:T(8,128)(2,1)}, bf16[512,512]{1,0:T(8,128)(2,1)}, f32[128,512]{1,0:T(8,128)S(1)}, bf16[128,512]{1,0:T(8,128)(2,1)S(1)}, bf16[128,512]{1,0:T(8,128)(2,1)S(1)}) custom-call(s32[4]{0:T(128)S(1)} %pad_add_fusion.scalars, s32[1,1024]{1,0:T(1,128)S(1)} %bitcast.16, s32[1,1024]{1,0:T(1,128)S(1)} %bitcast.18, ...), custom_call_target="tpu_custom_call" | custom-call | flops 2147483648 | bytes 4730896 | tf_op jit(solution)/shard_map/nodes/pallas_call | solution.py:91
  48.0 1.3 %collective-permute-start.3 = (bf16[128,512]{1,0:T(8,128)(2,1)S(1)}, bf16[128,512]{1,0:T(8,128)(2,1)S(1)}, u32[]{:S(2)}, u32[]{:S(2)}) collective-permute-start(bf16[128,512]{1,0:T(8,128)(2,1)S(1)} %get-tuple-element.44), channel_id=1, source_target_pairs={{2,0},{4,2},{6,4},{8,6},{10,8},{12,10},{14,12},{16,14},{18,16},{20... | collective-permute-start | bytes 393224 | tf_op jit(solution)/shard_map/ppermute | solution.py:375
  49.3 4.0 %collective-permute-start.4 = (bf16[128,512]{1,0:T(8,128)(2,1)S(1)}, bf16[128,512]{1,0:T(8,128)(2,1)S(1)}, u32[]{:S(2)}, u32[]{:S(2)}) collective-permute-start(bf16[128,512]{1,0:T(8,128)(2,1)S(1)} %get-tuple-element.45), channel_id=1, source_target_pairs={{0,2},{2,4},{4,6},{6,8},{8,10},{10,12},{12,14},{14,16},{16,18},{18... | collective-permute-start | bytes 393224 | tf_op jit(solution)/shard_map/ppermute | solution.py:375
  53.3 7.2 %all-to-all-done.shares = bf16[32,136,128]{2,1,0:T(8,128)(2,1)S(1)} async-done(((bf16[32,136,128]{2,1,0:T(8,128)(2,1)}), bf16[32,136,128]{2,1,0:T(8,128)(2,1)S(1)}, u32[]{:S(2)}, u32[]{:S(2)}) %all-to-all-start) | async-done | bytes 1114144 | tf_op jit(solution)/shard_map/all_to_all | solution.py:506
  60.5 0.8 group_sum.1
  61.4 3.3 %all-to-all-start.1 = ((bf16[4,136,128]{2,1,0:T(8,128)(2,1)}), bf16[4,136,128]{2,1,0:T(8,128)(2,1)S(1)}, u32[]{:S(2)}, u32[]{:S(2)}) async-start(bf16[4,136,128]{2,1,0:T(8,128)(2,1)} %group_sum.1), calls=%async_computation.1 | async-start | bytes 278528 | tf_op jit(solution)/shard_map/all_to_all | solution.py:515
  64.8 7.2 %all-to-all-done.1.shares = bf16[4,136,128]{2,1,0:T(8,128)(2,1)S(1)} async-done(((bf16[4,136,128]{2,1,0:T(8,128)(2,1)}), bf16[4,136,128]{2,1,0:T(8,128)(2,1)S(1)}, u32[]{:S(2)}, u32[]{:S(2)}) %all-to-all-start.1) | async-done | bytes 139296 | tf_op jit(solution)/shard_map/all_to_all | solution.py:515
  72.0 0.1 whole_sum.1
  72.1 19.8 %all_to_all.15.shares = bf16[32,128,128]{2,1,0:T(8,128)(2,1)S(1)} all-to-all(bf16[32,128,128]{2,1,0:T(8,128)(2,1)S(1)} %get-tuple-element.48), channel_id=1, replica_groups=mesh['band'=16,'hi'=4,'lo'=2,'rep'=2] {'band','lo'}, dimensions={0} | all-to-all | bytes 2097152 | tf_op jit(solution)/shard_map/all_to_all | solution.py:524
  91.9 2.8 %collective-permute-start.5 = (bf16[32,128,128]{2,1,0:T(8,128)(2,1)S(1)}, bf16[32,128,128]{2,1,0:T(8,128)(2,1)S(1)}, u32[]{:S(2)}, u32[]{:S(2)}) collective-permute-start(bf16[32,128,128]{2,1,0:T(8,128)(2,1)S(1)} %all_to_all.15.shares), channel_id=1, source_target_pairs={{0,1},{1,0},{2,3},{3,2},{4,5},{5,4},{6,7},{7,6},{8,9},{9,8},{10,11... | collective-permute-start | bytes 3145736 | tf_op jit(solution)/shard_map/ppermute | solution.py:379
  94.7 0.6 slice.3
  95.3 1.9 %own_half.1 = (f32[1536,512]{1,0:T(8,128)}, f32[512,512]{1,0:T(8,128)}) custom-call(s32[4]{0:T(128)S(1)} %pad_add_fusion.scalars, bf16[32,128,128]{2,1,0:T(8,128)(2,1)S(1)} %all_to_all.15.shares), custom_call_target="tpu_custom_call" | custom-call | bytes 6291456 | tf_op jit(solution)/shard_map/own_half/pallas_call | solution.py:538
  97.3 1.9 %other_half.1 = (f32[1536,512]{1,0:T(8,128)}, f32[512,512]{1,0:T(8,128)}) custom-call(s32[4]{0:T(128)S(1)} %pad_add_fusion.scalars, bf16[32,128,128]{2,1,0:T(8,128)(2,1)S(1)} %collective-permute-done.5.shares, f32[1536,512]{1,0:T(8,128)} %get-tuple-element.49.first_in, ...), custom_call_target="tpu_custom_call", output_to_operand_aliasing={{0}: (2, {}), {1}: (3, {})} | custom-call | bytes 6291456 | tf_op jit(solution)/shard_map/other_half/pallas_call | solution.py:539
  (18 shorter events, 0.2 us)
Async XLA Ops:
  1.6 11.6 %collective-permute-start.1 = (bf16[256,512]{1,0:T(8,128)(2,1)S(1)}, bf16[256,512]{1,0:T(8,128)(2,1)S(1)}, u32[]{:S(2)}, u32[]{:S(2)}) collective-permute-start(bf16[256,512]{1,0:T(8,128)(2,1)S(1)} %stack.17.stack_own), channel_id=1, source_target_pairs={{2,0},{4,2},{6,4},{8,6},{10,8},{12,10},{14,12},{16,14},{18,16},{20... | collective-permute-start | bytes 786440 | tf_op jit(solution)/shard_map/ppermute | solution.py:375
  2.9 10.3 %collective-permute-start = (bf16[256,512]{1,0:T(8,128)(2,1)S(1)}, bf16[256,512]{1,0:T(8,128)(2,1)S(1)}, u32[]{:S(2)}, u32[]{:S(2)}) collective-permute-start(bf16[256,512]{1,0:T(8,128)(2,1)S(1)} %stack.17.stack_own), channel_id=1, source_target_pairs={{0,2},{2,4},{4,6},{6,8},{8,10},{10,12},{12,14},{14,16},{16,18},{18... | collective-permute-start | bytes 786440 | tf_op jit(solution)/shard_map/ppermute | solution.py:375
  8.7 4.6 %copy-start.2 = (s32[1024]{0:T(1024)S(1)}, s32[1024]{0:T(1024)}, u32[]{:S(2)}) copy-start(s32[1024]{0:T(1024)} %param.18) | copy-start | bytes 12292
  8.7 4.6 %copy-start.3 = (f32[512]{0:T(512)S(1)}, f32[512]{0:T(512)}, u32[]{:S(2)}) copy-start(f32[512]{0:T(512)} %param.16) | copy-start | bytes 6148
  13.2 7.1 %copy-start.4 = (bf16[1536,512]{1,0:T(8,128)(2,1)}, bf16[1536,512]{1,0:T(8,128)(2,1)S(1)}, u32[]{:S(2)}) copy-start(bf16[1536,512]{1,0:T(8,128)(2,1)S(1)} %get-tuple-element.33.w_first) | copy-start | bytes 4718596
  20.3 5.2 %collective-permute-start.2 = (bf16[1040,512]{1,0:T(8,128)(2,1)S(1)}, bf16[1040,512]{1,0:T(8,128)(2,1)S(1)}, u32[]{:S(2)}, u32[]{:S(2)}) collective-permute-start(bf16[1040,512]{1,0:T(8,128)(2,1)S(1)} %get-tuple-element.39), channel_id=1, source_target_pairs={{0,1},{1,0},{2,3},{3,2},{4,5},{5,4},{6,7},{7,6},{8,9},{9,8},{10,11... | collective-permute-start | bytes 3194888 | tf_op jit(solution)/shard_map/ppermute | solution.py:379
  26.7 15.9 %copy-start.1 = (s32[1024]{0:T(1024)S(1)}, s32[1024]{0:T(1024)}, u32[]{:S(2)}) copy-start(s32[1024]{0:T(1024)} %param.17) | copy-start | bytes 12292
  26.7 33.8 %all-to-all-start = ((bf16[32,136,128]{2,1,0:T(8,128)(2,1)}), bf16[32,136,128]{2,1,0:T(8,128)(2,1)S(1)}, u32[]{:S(2)}, u32[]{:S(2)}) async-start(bf16[32,136,128]{2,1,0:T(8,128)(2,1)} %get-tuple-element.47), calls=%async_computation | async-start | bytes 2228224 | tf_op jit(solution)/shard_map/all_to_all | solution.py:506
  42.6 1.4 %copy-start.5 = (bf16[1536,512]{1,0:T(8,128)(2,1)S(1)}, bf16[1536,512]{1,0:T(8,128)(2,1)}, u32[]{:S(2)}) copy-start(bf16[1536,512]{1,0:T(8,128)(2,1)} %copy-done.4) | copy-start | bytes 4718596
  48.0 16.7 %collective-permute-start.3 = (bf16[128,512]{1,0:T(8,128)(2,1)S(1)}, bf16[128,512]{1,0:T(8,128)(2,1)S(1)}, u32[]{:S(2)}, u32[]{:S(2)}) collective-permute-start(bf16[128,512]{1,0:T(8,128)(2,1)S(1)} %get-tuple-element.44), channel_id=1, source_target_pairs={{2,0},{4,2},{6,4},{8,6},{10,8},{12,10},{14,12},{16,14},{18,16},{20... | collective-permute-start | bytes 393224 | tf_op jit(solution)/shard_map/ppermute | solution.py:375
  49.3 15.4 %collective-permute-start.4 = (bf16[128,512]{1,0:T(8,128)(2,1)S(1)}, bf16[128,512]{1,0:T(8,128)(2,1)S(1)}, u32[]{:S(2)}, u32[]{:S(2)}) collective-permute-start(bf16[128,512]{1,0:T(8,128)(2,1)S(1)} %get-tuple-element.45), channel_id=1, source_target_pairs={{0,2},{2,4},{4,6},{6,8},{8,10},{10,12},{12,14},{14,16},{16,18},{18... | collective-permute-start | bytes 393224 | tf_op jit(solution)/shard_map/ppermute | solution.py:375
  61.4 10.6 %all-to-all-start.1 = ((bf16[4,136,128]{2,1,0:T(8,128)(2,1)}), bf16[4,136,128]{2,1,0:T(8,128)(2,1)S(1)}, u32[]{:S(2)}, u32[]{:S(2)}) async-start(bf16[4,136,128]{2,1,0:T(8,128)(2,1)} %group_sum.1), calls=%async_computation.1 | async-start | bytes 278528 | tf_op jit(solution)/shard_map/all_to_all | solution.py:515
  64.8 32.5 %copy-start = (f32[128,512]{1,0:T(8,128)}, f32[128,512]{1,0:T(8,128)S(1)}, u32[]{:S(2)}) copy-start(f32[128,512]{1,0:T(8,128)S(1)} %convert_add_fusion.after) | copy-start | bytes 786436
  91.9 5.3 %collective-permute-start.5 = (bf16[32,128,128]{2,1,0:T(8,128)(2,1)S(1)}, bf16[32,128,128]{2,1,0:T(8,128)(2,1)S(1)}, u32[]{:S(2)}, u32[]{:S(2)}) collective-permute-start(bf16[32,128,128]{2,1,0:T(8,128)(2,1)S(1)} %all_to_all.15.shares), channel_id=1, source_target_pairs={{0,1},{1,0},{2,3},{3,2},{4,5},{5,4},{6,7},{7,6},{8,9},{9,8},{10,11... | collective-permute-start | bytes 3145736 | tf_op jit(solution)/shard_map/ppermute | solution.py:379

commit v5 on v4

--- a/solution.py
+++ b/solution.py
@@ -160,8 +160,13 @@
         copy.wait()
 
 
-def live_receivers(scalars, receivers, start):
+def live_receivers(scalars, receivers, start, rows_mesh):
     row = receivers[:, pl.ds(start, TILE)] - scalars[1]
+    row = jnp.where(
+        row < rows_mesh,
+        row + scalars[4],
+        jnp.where(row >= 2 * rows_mesh, row - scalars[4], row),
+    )
     slot = start + lax.broadcasted_iota(jnp.int32, (1, TILE), 1)
     return jnp.where(slot < scalars[2], row, -1)
 
@@ -172,9 +177,9 @@
     partial,
     grid_picked,
     edge,
-    stack_before,
+    stack_first,
     stack_own,
-    stack_after,
+    stack_second,
     w_first,
     w_second,
     norm_gain,
@@ -190,18 +195,18 @@
     gain_sum = jnp.zeros((1, width), jnp.float32)
     for start in range(0, edge.shape[0], TILE):
         rows = pl.ds(start, TILE)
-        table = picks(live_receivers(scalars, receivers, start), 3 * rows_mesh)
+        table = picks(live_receivers(scalars, receivers, start, rows_mesh), 3 * rows_mesh)
 
         def picked_rows(first):
             part = pl.ds(first, rows_mesh)
-            near = jnp.concatenate([stack_before[part, :], stack_own[part, :], stack_after[part, :]], axis=0)
+            near = jnp.concatenate([stack_first[part, :], stack_own[part, :], stack_second[part, :]], axis=0)
             return dot(table, near)
 
         latents = picked_rows(0).astype(jnp.bfloat16)
         upstream = picked_rows(rows_mesh)
         mesh_picked[rows, :] = latents
         pre_act = partial[rows, :] + dot(latents, w_first[2 * width : 3 * width, :])
-        sigmoid = jax.nn.sigmoid(pre_act)
+        sigmoid = 0.5 * jnp.tanh(0.5 * pre_act) + 0.5
         hid = (pre_act * sigmoid).astype(jnp.bfloat16)
         hidden[rows, :] = hid
         output = dot(hid, w_second[...])
@@ -299,8 +304,8 @@
     edge_grad,
     grid_grad,
     mesh_own,
-    to_below,
-    to_above,
+    to_first,
+    to_second,
 ):
     edges, width = grad_pre.shape
     rows_grid, rows_mesh = grid_grad.shape[0], mesh_own.shape[0]
@@ -315,13 +320,15 @@
     for start in range(0, edges, TILE):
         rows = pl.ds(start, TILE)
         terms = grad_pre[rows, :]
-        near = near + dot(spreads(live_receivers(scalars, receivers, start), 3 * rows_mesh), terms)
+        near = near + dot(
+            spreads(live_receivers(scalars, receivers, start, rows_mesh), 3 * rows_mesh), terms
+        )
         here = here + dot(spreads(senders[:, rows] - scalars[0], rows_grid), terms)
         edge_grad[rows, :] = dot(terms, w_first[0:width, :], 1, 1).astype(jnp.bfloat16)
     mesh_terms = through(near, 2 * width)
-    to_below[...] = mesh_terms[0:rows_mesh].astype(jnp.bfloat16)
+    to_first[...] = mesh_terms[0:rows_mesh].astype(jnp.bfloat16)
     mesh_own[...] = mesh_terms[rows_mesh : 2 * rows_mesh]
-    to_above[...] = mesh_terms[2 * rows_mesh : 3 * rows_mesh].astype(jnp.bfloat16)
+    to_second[...] = mesh_terms[2 * rows_mesh : 3 * rows_mesh].astype(jnp.bfloat16)
     grid_grad[...] = through(here, width).astype(jnp.bfloat16)
 
 
@@ -369,10 +376,10 @@
     put_half(scalars, True, shares, first, second, wide, sems)
 
 
-def passed_along(value, steps):
+def exchanged(value, turn):
     count = lax.axis_size(SHARDS)
-    leading, last = (max(0, -steps), min(count, count - steps))
-    return lax.ppermute(value, SHARDS, [(s, s + steps) for s in range(leading, last)])
+    pairs = [(s, s + 1) for s in range(turn, count - 1, 2)]
+    return lax.ppermute(value, SHARDS, pairs + [(d, s) for s, d in pairs])
 
 
 def swapped(value):
@@ -404,6 +411,7 @@
             (shard - 1) * rows_mesh,
             live_counts[0],
             lax.axis_index("rep").astype(jnp.int32),
+            jnp.where(shard % 2 == 0, 2 * rows_mesh, 0),
         ]
     ).astype(jnp.int32)
     senders, receivers = senders[None], receivers[None]
@@ -422,7 +430,7 @@
         0,
         [pltpu.SemaphoreType.DMA((2,))],
     )
-    stack_before, stack_after = passed_along(stacked, 1), passed_along(stacked, -1)
+    stack_first, stack_second = exchanged(stacked, 0), exchanged(stacked, 1)
     partial, grid_picked, edge, w_first, w_second = call(
         near_kernel,
         "near",
@@ -458,9 +466,9 @@
             partial,
             grid_picked,
             edge,
-            stack_before,
+            stack_first,
             stacked,
-            stack_after,
+            stack_second,
             w_first,
             w_second,
             gain,
@@ -486,7 +494,7 @@
         (kept, got, gain_term),
         0,
     )
-    edge_grad, grid_grad, mesh_own, to_below, to_above = call(
+    edge_grad, grid_grad, mesh_own, to_first, to_second = call(
         node_kernel,
         "nodes",
         [in_smem()] + [in_vmem()] * 4 + [anywhere()],
@@ -500,9 +508,9 @@
         (scalars, senders, receivers, grad_pre, w_first, done),
         4 * unit,
     )
-    from_above = passed_along(to_below, -1).astype(jnp.float32)
-    from_below = passed_along(to_above, 1).astype(jnp.float32)
-    mesh_grad = mesh_own + from_above + from_below
+    from_first = exchanged(to_first, 0).astype(jnp.float32)
+    from_second = exchanged(to_second, 1).astype(jnp.float32)
+    mesh_grad = mesh_own + from_first + from_second
     shares = lax.all_to_all(packed, GROUP, 0, 0)
     (copies,) = call(
         group_sum_kernel,

time: 99.9 us -> 98.4 us (0.985)
  starting transfers between devices: 36.5 us -> 29 us
  waiting for transfers between devices: 14.9 us -> 19.1 us
  blocking collectives: 19.8 us -> 21.9 us
    all_to_all x1, starting transfers between devices: 15.9 us -> 11.1 us  [per_device(): shares = lax.all_to_all(packed, GROUP, 0, 0)]
    ppermute x4, starting transfers between devices: 11.6 us -> 7.81 us  [exchanged(): return lax.ppermute(value, SHARDS, pairs + [(d, s) for s, d in pairs])]
    all_to_all x1, waiting for transfers between devices: 7.22 us -> 11 us  [per_device(): shares = lax.all_to_all(packed, GROUP, 0, 0)]
    all_to_all x1, starting transfers between devices: 3.33 us -> 5.59 us  [per_device(): shares = lax.all_to_all(copies, 'hi', 0, 0)]
    all_to_all x1, blocking collectives: 19.8 us -> 21.9 us  [per_device(): total = lax.all_to_all(copies, GROUP, 0, 0)]
    ppermute x2, starting transfers between devices: 5.69 us -> 4.44 us  [swapped(): return lax.ppermute(value, 'rep', [(0, 1), (1, 0)])]
  transfers between devices with their start and end apart: 8 -> 8, of which waited for: 3 -> 4; matrix products, arithmetic and copies ran while one was open for 1% -> 1% of each run, Pallas kernels for 13% -> 13%
where the time goes in v5:
time: 98.4 us; the launch traced here: 97.9 us
  starting transfers between devices  29 us (29%)
  Pallas kernels  24.3 us (25%)
  blocking collectives  21.9 us (22%)
  waiting for transfers between devices  19.1 us (19%)
  local copies, waits for them, and re-layouts  2.09 us (2%)
  between operations  1.6 us (2%)
    all_to_all x1, blocking collectives, per_device(): total = lax.all_to_all(copies, GROUP, 0, 0)  21.9 us
    pallas_call x8, Pallas kernels, call(): pl.pallas_call(kernel, out_shape=outs, in_specs=specs, out_specs=[in_vmem...  20.4 us
    all_to_all x1, starting transfers between devices, per_device(): shares = lax.all_to_all(packed, GROUP, 0, 0)  11.1 us
    all_to_all x1, waiting for transfers between devices, per_device(): shares = lax.all_to_all(packed, GROUP, 0, 0)  11 us
    ppermute x4, starting transfers between devices, exchanged(): return lax.ppermute(value, SHARDS, pairs + [(d, s) for s, d in pairs])  7.81 us
    all_to_all x1, waiting for transfers between devices, per_device(): shares = lax.all_to_all(copies, 'hi', 0, 0)  7.2 us
    all_to_all x1, starting transfers between devices, per_device(): shares = lax.all_to_all(copies, 'hi', 0, 0)  5.59 us
    ppermute x2, starting transfers between devices, swapped(): return lax.ppermute(value, 'rep', [(0, 1), (1, 0)])  4.44 us
  transfers between devices with their start and end apart: 8, of which 4 were waited for; matrix products, arithmetic and copies ran while one was open for 1% of the time, Pallas kernels for 13%

profile of v5, /device:TPU:1, one launch (start us, length us, event | category | flops | bytes accessed | tf_op | source)
XLA Modules:
  0.0 97.9 jit_solution(4985976154711076838)
XLA Ops:
  0.6 1.0 %stack.21.stack_own = bf16[256,512]{1,0:T(8,128)(2,1)S(1)} custom-call(bf16[128,512]{1,0:T(8,128)(2,1)} %bitcast.21, bf16[128,512]{1,0:T(8,128)(2,1)} %bitcast.22), custom_call_target="tpu_custom_call" | custom-call | bytes 524288 | tf_op jit(solution)/shard_map/stack/pallas_call | solution.py:91
  1.6 0.7 collective-permute-start.1
  2.3 5.4 %collective-permute-start = (bf16[256,512]{1,0:T(8,128)(2,1)S(1)}, bf16[256,512]{1,0:T(8,128)(2,1)S(1)}, u32[]{:S(2)}, u32[]{:S(2)}) collective-permute-start(bf16[256,512]{1,0:T(8,128)(2,1)S(1)} %stack.21.stack_own), channel_id=1, source_target_pairs={{0,2},{4,6},{8,10},{12,14},{16,18},{20,22},{24,26},{28,30},{32,34}... | collective-permute-start | bytes 786440 | tf_op jit(solution)/shard_map/ppermute | solution.py:382
  8.5 4.5 %near.1 = (f32[1024,512]{1,0:T(8,128)S(1)}, bf16[1024,512]{1,0:T(8,128)(2,1)S(1)}, bf16[1024,512]{1,0:T(8,128)(2,1)S(1)}, bf16[1536,512]{1,0:T(8,128)(2,1)S(1)}, bf16[512,512]{1,0:T(8,128)(2,1)S(1)}) custom-call(s32[5]{0:T(128)S(1)} %stack.20.scalars, s32[1,1024]{1,0:T(1,128)} %bitcast.16, bf16[512,512]{1,0:T(8,128)(2,1)} %bitcast.25, ...), custom_call_target="tpu_custom_call" | custom-call | flops 1610612736 | bytes 9965588 | tf_op jit(solution)/shard_map/near/pallas_call | solution.py:91
  13.0 0.4 collective-permute-done.stack_first
  13.5 7.0 %edges.1 = (bf16[1040,512]{1,0:T(8,128)(2,1)S(1)}, f32[8,512]{1,0:T(8,128)S(1)}, bf16[1024,512]{1,0:T(8,128)(2,1)S(1)}, bf16[1024,512]{1,0:T(8,128)(2,1)S(1)}, b...) custom-call(s32[5]{0:T(128)S(1)} %stack.20.scalars, s32[1,1024]{1,0:T(1,128)S(1)} %bitcast.18, ...), custom_call_target="tpu_custom_call" | custom-call | flops 3758096384 | bytes 12359700 | tf_op jit(solution)/shard_map/edges/pallas_call | solution.py:91
  20.4 1.6 %collective-permute-start.2 = (bf16[1040,512]{1,0:T(8,128)(2,1)S(1)}, bf16[1040,512]{1,0:T(8,128)(2,1)S(1)}, u32[]{:S(2)}, u32[]{:S(2)}) collective-permute-start(bf16[1040,512]{1,0:T(8,128)(2,1)S(1)} %get-tuple-element.39), channel_id=1, source_target_pairs={{0,1},{1,0},{2,3},{3,2},{4,5},{5,4},{6,7},{7,6},{8,9},{9,8},{10,11... | collective-permute-start | bytes 3194888 | tf_op jit(solution)/shard_map/ppermute | solution.py:386
  22.1 1.8 %kept.1 = f32[1024,512]{1,0:T(8,128)S(1)} custom-call(s32[5]{0:T(128)S(1)} %stack.20.scalars, bf16[1024,512]{1,0:T(8,128)(2,1)S(1)} %get-tuple-element.32.edge, bf16[1024,512]{1,0:T(8,128)(2,1)S(1)} %get-tuple-element.31.grid_picked, bf16[1024,512]{1,0:T(8,128)(2,1)S(1)} %get-tuple-element.36.mesh_picked, bf16[1024,512]{1,0:T(8,128)(2,1)S(1)} %get-tuple-element.37.hidden, ...), custom_call_target="tpu_custom_call" | custom-call | flops 1073741824 | bytes 8388628 | tf_op jit(solution)/shard_map/kept/pallas_call | solution.py:91
  23.9 0.5 collective-permute-done.2.got
  24.4 1.2 %pack.1 = (bf16[32,136,128]{2,1,0:T(8,128)(2,1)}, f32[8,128]{1,0:T(8,128)S(1)}) custom-call(f32[1024,512]{1,0:T(8,128)S(1)} %kept.1, bf16[1040,512]{1,0:T(8,128)(2,1)S(1)} %collective-permute-done.2.got, f32[8,512]{1,0:T(8,128)S(1)} %get-tuple-element.40.gain_term), custom_call_target="tpu_custom_call" | custom-call | bytes 4296704 | tf_op jit(solution)/shard_map/pack/pallas_call | solution.py:91
  25.6 11.1 %all-to-all-start = ((bf16[32,136,128]{2,1,0:T(8,128)(2,1)}), bf16[32,136,128]{2,1,0:T(8,128)(2,1)S(1)}, u32[]{:S(2)}, u32[]{:S(2)}) async-start(bf16[32,136,128]{2,1,0:T(8,128)(2,1)} %get-tuple-element.47), calls=%async_computation | async-start | bytes 2228224 | tf_op jit(solution)/shard_map/all_to_all | solution.py:514
  36.7 1.4 %copy-done.5 = bf16[1536,512]{1,0:T(8,128)(2,1)S(1)} copy-done((bf16[1536,512]{1,0:T(8,128)(2,1)S(1)}, bf16[1536,512]{1,0:T(8,128)(2,1)}, u32[]{:S(2)}) %copy-start.5) | copy-done | bytes 1572888
  38.1 4.0 %nodes.1 = (bf16[1024,512]{1,0:T(8,128)(2,1)}, bf16[512,512]{1,0:T(8,128)(2,1)}, f32[128,512]{1,0:T(8,128)S(1)}, bf16[128,512]{1,0:T(8,128)(2,1)S(1)}, bf16[128,512]{1,0:T(8,128)(2,1)S(1)}) custom-call(s32[5]{0:T(128)S(1)} %stack.20.scalars, s32[1,1024]{1,0:T(1,128)S(1)} %bitcast.17, s32[1,1024]{1,0:T(1,128)S(1)} %bitcast.19, ...), custom_call_target="tpu_custom_call" | custom-call | flops 2147483648 | bytes 4730900 | tf_op jit(solution)/shard_map/nodes/pallas_call | solution.py:91
  42.1 1.1 %collective-permute-start.3 = (bf16[128,512]{1,0:T(8,128)(2,1)S(1)}, bf16[128,512]{1,0:T(8,128)(2,1)S(1)}, u32[]{:S(2)}, u32[]{:S(2)}) collective-permute-start(bf16[128,512]{1,0:T(8,128)(2,1)S(1)} %get-tuple-element.44), channel_id=1, source_target_pairs={{0,2},{4,6},{8,10},{12,14},{16,18},{20,22},{24,26},{28,30},{32,34}... | collective-permute-start | bytes 393224 | tf_op jit(solution)/shard_map/ppermute | solution.py:382
  43.2 0.7 collective-permute-start.4
  43.8 11.0 %all-to-all-done.shares = bf16[32,136,128]{2,1,0:T(8,128)(2,1)S(1)} async-done(((bf16[32,136,128]{2,1,0:T(8,128)(2,1)}), bf16[32,136,128]{2,1,0:T(8,128)(2,1)S(1)}, u32[]{:S(2)}, u32[]{:S(2)}) %all-to-all-start) | async-done | bytes 1114144 | tf_op jit(solution)/shard_map/all_to_all | solution.py:514
  54.8 0.8 group_sum.1
  55.6 5.6 %all-to-all-start.1 = ((bf16[4,136,128]{2,1,0:T(8,128)(2,1)}), bf16[4,136,128]{2,1,0:T(8,128)(2,1)S(1)}, u32[]{:S(2)}, u32[]{:S(2)}) async-start(bf16[4,136,128]{2,1,0:T(8,128)(2,1)} %group_sum.1), calls=%async_computation.1 | async-start | bytes 278528 | tf_op jit(solution)/shard_map/all_to_all | solution.py:523
  61.3 7.2 %all-to-all-done.1.shares = bf16[4,136,128]{2,1,0:T(8,128)(2,1)S(1)} async-done(((bf16[4,136,128]{2,1,0:T(8,128)(2,1)}), bf16[4,136,128]{2,1,0:T(8,128)(2,1)S(1)}, u32[]{:S(2)}, u32[]{:S(2)}) %all-to-all-start.1) | async-done | bytes 139296 | tf_op jit(solution)/shard_map/all_to_all | solution.py:523
  68.6 21.9 %all_to_all.15.shares = bf16[32,128,128]{2,1,0:T(8,128)(2,1)S(1)} all-to-all(bf16[32,128,128]{2,1,0:T(8,128)(2,1)S(1)} %get-tuple-element.48), channel_id=1, replica_groups=mesh['band'=16,'hi'=4,'lo'=2,'rep'=2] {'band','lo'}, dimensions={0} | all-to-all | bytes 2097152 | tf_op jit(solution)/shard_map/all_to_all | solution.py:532
  90.5 2.8 %collective-permute-start.5 = (bf16[32,128,128]{2,1,0:T(8,128)(2,1)S(1)}, bf16[32,128,128]{2,1,0:T(8,128)(2,1)S(1)}, u32[]{:S(2)}, u32[]{:S(2)}) collective-permute-start(bf16[32,128,128]{2,1,0:T(8,128)(2,1)S(1)} %all_to_all.15.shares), channel_id=1, source_target_pairs={{0,1},{1,0},{2,3},{3,2},{4,5},{5,4},{6,7},{7,6},{8,9},{9,8},{10,11... | collective-permute-start | bytes 3145736 | tf_op jit(solution)/shard_map/ppermute | solution.py:386
  93.3 0.6 slice.3
  93.9 1.9 %own_half.1 = (f32[1536,512]{1,0:T(8,128)}, f32[512,512]{1,0:T(8,128)}) custom-call(s32[5]{0:T(128)S(1)} %stack.20.scalars, bf16[32,128,128]{2,1,0:T(8,128)(2,1)S(1)} %all_to_all.15.shares), custom_call_target="tpu_custom_call" | custom-call | bytes 6291456 | tf_op jit(solution)/shard_map/own_half/pallas_call | solution.py:546
  95.9 1.9 %other_half.1 = (f32[1536,512]{1,0:T(8,128)}, f32[512,512]{1,0:T(8,128)}) custom-call(s32[5]{0:T(128)S(1)} %stack.20.scalars, bf16[32,128,128]{2,1,0:T(8,128)(2,1)S(1)} %collective-permute-done.5.shares, f32[1536,512]{1,0:T(8,128)} %get-tuple-element.49.first_in, f32[512,512]{1,0:T(8,128)} %get-tuple-element.50.second_in), custom_call_target="tpu_custom_call", output_to_operand_aliasing={{0}: (2, {}), {1}: (3, {})} | custom-call | bytes 6291456 | tf_op jit(solution)/shard_map/other_half/pallas_call | solution.py:547
  (18 shorter events, 0.3 us)
Async XLA Ops:
  1.6 11.4 %collective-permute-start.1 = (bf16[256,512]{1,0:T(8,128)(2,1)S(1)}, bf16[256,512]{1,0:T(8,128)(2,1)S(1)}, u32[]{:S(2)}, u32[]{:S(2)}) collective-permute-start(bf16[256,512]{1,0:T(8,128)(2,1)S(1)} %stack.21.stack_own), channel_id=1, source_target_pairs={{2,4},{6,8},{10,12},{14,16},{18,20},{22,24},{26,28},{30,32},{34,36... | collective-permute-start | bytes 786440 | tf_op jit(solution)/shard_map/ppermute | solution.py:382
  2.3 11.1 %collective-permute-start = (bf16[256,512]{1,0:T(8,128)(2,1)S(1)}, bf16[256,512]{1,0:T(8,128)(2,1)S(1)}, u32[]{:S(2)}, u32[]{:S(2)}) collective-permute-start(bf16[256,512]{1,0:T(8,128)(2,1)S(1)} %stack.21.stack_own), channel_id=1, source_target_pairs={{0,2},{4,6},{8,10},{12,14},{16,18},{20,22},{24,26},{28,30},{32,34}... | collective-permute-start | bytes 786440 | tf_op jit(solution)/shard_map/ppermute | solution.py:382
  8.5 5.0 %copy-start.2 = (s32[1024]{0:T(1024)S(1)}, s32[1024]{0:T(1024)}, u32[]{:S(2)}) copy-start(s32[1024]{0:T(1024)} %param.18) | copy-start | bytes 12292
  8.5 5.0 %copy-start.3 = (f32[512]{0:T(512)S(1)}, f32[512]{0:T(512)}, u32[]{:S(2)}) copy-start(f32[512]{0:T(512)} %param.16) | copy-start | bytes 6148
  13.0 7.4 %copy-start.4 = (bf16[1536,512]{1,0:T(8,128)(2,1)}, bf16[1536,512]{1,0:T(8,128)(2,1)S(1)}, u32[]{:S(2)}) copy-start(bf16[1536,512]{1,0:T(8,128)(2,1)S(1)} %get-tuple-element.33.w_first) | copy-start | bytes 4718596
  20.4 3.9 %collective-permute-start.2 = (bf16[1040,512]{1,0:T(8,128)(2,1)S(1)}, bf16[1040,512]{1,0:T(8,128)(2,1)S(1)}, u32[]{:S(2)}, u32[]{:S(2)}) collective-permute-start(bf16[1040,512]{1,0:T(8,128)(2,1)S(1)} %get-tuple-element.39), channel_id=1, source_target_pairs={{0,1},{1,0},{2,3},{3,2},{4,5},{5,4},{6,7},{7,6},{8,9},{9,8},{10,11... | collective-permute-start | bytes 3194888 | tf_op jit(solution)/shard_map/ppermute | solution.py:386
  25.6 11.1 %copy-start.1 = (s32[1024]{0:T(1024)S(1)}, s32[1024]{0:T(1024)}, u32[]{:S(2)}) copy-start(s32[1024]{0:T(1024)} %param.17) | copy-start | bytes 12292
  25.6 29.2 %all-to-all-start = ((bf16[32,136,128]{2,1,0:T(8,128)(2,1)}), bf16[32,136,128]{2,1,0:T(8,128)(2,1)S(1)}, u32[]{:S(2)}, u32[]{:S(2)}) async-start(bf16[32,136,128]{2,1,0:T(8,128)(2,1)} %get-tuple-element.47), calls=%async_computation | async-start | bytes 2228224 | tf_op jit(solution)/shard_map/all_to_all | solution.py:514
  36.7 1.4 %copy-start.5 = (bf16[1536,512]{1,0:T(8,128)(2,1)S(1)}, bf16[1536,512]{1,0:T(8,128)(2,1)}, u32[]{:S(2)}) copy-start(bf16[1536,512]{1,0:T(8,128)(2,1)} %copy-done.4) | copy-start | bytes 4718596
  42.1 19.1 %collective-permute-start.3 = (bf16[128,512]{1,0:T(8,128)(2,1)S(1)}, bf16[128,512]{1,0:T(8,128)(2,1)S(1)}, u32[]{:S(2)}, u32[]{:S(2)}) collective-permute-start(bf16[128,512]{1,0:T(8,128)(2,1)S(1)} %get-tuple-element.44), channel_id=1, source_target_pairs={{0,2},{4,6},{8,10},{12,14},{16,18},{20,22},{24,26},{28,30},{32,34}... | collective-permute-start | bytes 393224 | tf_op jit(solution)/shard_map/ppermute | solution.py:382
  43.2 18.1 %collective-permute-start.4 = (bf16[128,512]{1,0:T(8,128)(2,1)S(1)}, bf16[128,512]{1,0:T(8,128)(2,1)S(1)}, u32[]{:S(2)}, u32[]{:S(2)}) collective-permute-start(bf16[128,512]{1,0:T(8,128)(2,1)S(1)} %get-tuple-element.45), channel_id=1, source_target_pairs={{2,4},{6,8},{10,12},{14,16},{18,20},{22,24},{26,28},{30,32},{34,36... | collective-permute-start | bytes 393224 | tf_op jit(solution)/shard_map/ppermute | solution.py:382
  55.6 12.9 %all-to-all-start.1 = ((bf16[4,136,128]{2,1,0:T(8,128)(2,1)}), bf16[4,136,128]{2,1,0:T(8,128)(2,1)S(1)}, u32[]{:S(2)}, u32[]{:S(2)}) async-start(bf16[4,136,128]{2,1,0:T(8,128)(2,1)} %group_sum.1), calls=%async_computation.1 | async-start | bytes 278528 | tf_op jit(solution)/shard_map/all_to_all | solution.py:523
  61.3 34.6 %copy-start = (f32[128,512]{1,0:T(8,128)}, f32[128,512]{1,0:T(8,128)S(1)}, u32[]{:S(2)}) copy-start(f32[128,512]{1,0:T(8,128)S(1)} %convert_add_fusion.after) | copy-start | bytes 786436
  90.5 5.3 %collective-permute-start.5 = (bf16[32,128,128]{2,1,0:T(8,128)(2,1)S(1)}, bf16[32,128,128]{2,1,0:T(8,128)(2,1)S(1)}, u32[]{:S(2)}, u32[]{:S(2)}) collective-permute-start(bf16[32,128,128]{2,1,0:T(8,128)(2,1)S(1)} %all_to_all.15.shares), channel_id=1, source_target_pairs={{0,1},{1,0},{2,3},{3,2},{4,5},{5,4},{6,7},{7,6},{8,9},{9,8},{10,11... | collective-permute-start | bytes 3145736 | tf_op jit(solution)/shard_map/ppermute | solution.py:386

commit v6 on v5

--- a/solution.py
+++ b/solution.py
@@ -271,22 +271,18 @@
     done[...] = jnp.zeros(done.shape, jnp.float32)
 
 
-def group_sum_kernel(shares, after, copies):
+def group_sum_kernel(shares, after, packed):
     total = shares[0].astype(jnp.float32)
     for place in range(1, shares.shape[0]):
         total = total + shares[place].astype(jnp.float32)
     data = total.shape[0] - 8
     gain = gain_rows(gain_of(total[data:]), LANES)
-    row = jnp.concatenate([total[:data], gain], axis=0).astype(jnp.bfloat16)
-    for place in range(copies.shape[0]):
-        copies[place] = row
-
-
-def whole_sum_kernel(factor, shares, after, copies, gain_grad):
-    total = shares[0].astype(jnp.float32)
-    for place in range(1, shares.shape[0]):
-        total = total + shares[place].astype(jnp.float32)
-    total = total * factor
+    packed[...] = jnp.concatenate([total[:data], gain], axis=0).astype(jnp.bfloat16)
+
+
+def whole_sum_kernel(factor, own, ahead, across, behind, after, copies, gain_grad):
+    own, ahead, across, behind = [part[...].astype(jnp.float32) for part in (own, ahead, across, behind)]
+    total = ((own + across) + (ahead + behind)) * factor
     data = copies.shape[1]
     gain_grad[...] = jnp.broadcast_to(gain_of(total[data:]), gain_grad.shape)
     share = total[:data].astype(jnp.bfloat16)
@@ -512,21 +508,24 @@
     from_second = exchanged(to_second, 1).astype(jnp.float32)
     mesh_grad = mesh_own + from_first + from_second
     shares = lax.all_to_all(packed, GROUP, 0, 0)
-    (copies,) = call(
+    (packed,) = call(
         group_sum_kernel,
         "group_sum",
         [in_vmem(), anywhere()],
-        [matrix((groups, part + extra, LANES))],
+        [matrix((part + extra, LANES))],
         (shares, mesh_own),
         0,
     )
-    shares = lax.all_to_all(copies, "hi", 0, 0)
+    turns = [
+        lax.ppermute(packed, "hi", [(i, (i + turn) % groups) for i in range(groups)])
+        for turn in (1, 2, 3)
+    ]
     copies, gain_grad = call(
         functools.partial(whole_sum_kernel, factor),
         "whole_sum",
-        [in_vmem(), anywhere()],
+        [in_vmem()] * 4 + [anywhere()],
         [matrix((group, part, LANES)), floats((8, width))],
-        (shares, mesh_grad),
+        (packed, *turns, mesh_grad),
         0,
     )
     total = lax.all_to_all(copies, GROUP, 0, 0)
@@ -563,7 +562,7 @@
 def solution(mesh):
     bands, meshes, cores = mesh.devices.shape
     mesh = jax.sharding.Mesh(
-        mesh.devices.reshape(bands, meshes // 2, 2, cores), ("band", "hi", "lo", "rep")
+        mesh.devices.reshape(bands, 4, meshes // 4, cores), ("band", "hi", "lo", "rep")
     )
     in_specs = (
         P("rep", SHARDS, None),

time: 98.4 us -> 95.8 us (0.974)
  waiting for transfers between devices: 19.1 us -> 16.7 us
  starting transfers between devices: 29 us -> 30.2 us
    all_to_all x1 -> x0, waiting for transfers between devices: 7.2 us -> none  [per_device(): shares = lax.all_to_all(copies, 'hi', 0, 0)]
    ppermute x0 -> x3, starting transfers between devices: none -> 6.58 us  [per_device(): lax.ppermute(packed, 'hi', [(i, (i + turn) % groups) for i in range(group...]
    all_to_all x1 -> x0, starting transfers between devices: 5.59 us -> none  [per_device(): shares = lax.all_to_all(copies, 'hi', 0, 0)]
    ppermute x0 -> x3, waiting for transfers between devices: none -> 4.8 us  [per_device(): lax.ppermute(packed, 'hi', [(i, (i + turn) % groups) for i in range(group...]
  transfers between devices with their start and end apart: 8 -> 10, of which waited for: 4 -> 4; matrix products, arithmetic and copies ran while one was open for 1% -> 1% of each run, Pallas kernels for 13% -> 13%
where the time goes in v6:
time: 95.8 us; the launch traced here: 95.4 us
  starting transfers between devices  30.2 us (32%)
  Pallas kernels  23.6 us (25%)
  blocking collectives  21.2 us (22%)
  waiting for transfers between devices  16.7 us (17%)
  local copies, waits for them, and re-layouts  2.09 us (2%)
  between operations  1.6 us (2%)
    all_to_all x1, blocking collectives, per_device(): total = lax.all_to_all(copies, GROUP, 0, 0)  21.2 us
    pallas_call x8, Pallas kernels, call(): pl.pallas_call(kernel, out_shape=outs, in_specs=specs, out_specs=[in_vmem...  19.7 us
    all_to_all x1, starting transfers between devices, per_device(): shares = lax.all_to_all(packed, GROUP, 0, 0)  11.1 us
    all_to_all x1, waiting for transfers between devices, per_device(): shares = lax.all_to_all(packed, GROUP, 0, 0)  11 us
    ppermute x4, starting transfers between devices, exchanged(): return lax.ppermute(value, SHARDS, pairs + [(d, s) for s, d in pairs])  7.81 us
    ppermute x3, starting transfers between devices, per_device(): lax.ppermute(packed, 'hi', [(i, (i + turn) % groups) for i in range(group...  6.58 us
    ppermute x3, waiting for transfers between devices, per_device(): lax.ppermute(packed, 'hi', [(i, (i + turn) % groups) for i in range(group...  4.8 us
    ppermute x2, starting transfers between devices, swapped(): return lax.ppermute(value, 'rep', [(0, 1), (1, 0)])  4.68 us
  transfers between devices with their start and end apart: 10, of which 4 were waited for; matrix products, arithmetic and copies ran while one was open for 1% of the time, Pallas kernels for 13%

profile of v6, /device:TPU:1, one launch (start us, length us, event | category | flops | bytes accessed | tf_op | source)
XLA Modules:
  0.0 95.4 jit_solution(11595294459380354729)
XLA Ops:
  0.6 1.0 %stack.21.stack_own = bf16[256,512]{1,0:T(8,128)(2,1)S(1)} custom-call(bf16[128,512]{1,0:T(8,128)(2,1)} %bitcast.21, bf16[128,512]{1,0:T(8,128)(2,1)} %bitcast.22), custom_call_target="tpu_custom_call" | custom-call | bytes 524288 | tf_op jit(solution)/shard_map/stack/pallas_call | solution.py:91
  1.6 0.7 collective-permute-start.1
  2.3 5.4 %collective-permute-start = (bf16[256,512]{1,0:T(8,128)(2,1)S(1)}, bf16[256,512]{1,0:T(8,128)(2,1)S(1)}, u32[]{:S(2)}, u32[]{:S(2)}) collective-permute-start(bf16[256,512]{1,0:T(8,128)(2,1)S(1)} %stack.21.stack_own), channel_id=1, source_target_pairs={{0,2},{4,6},{8,10},{12,14},{16,18},{20,22},{24,26},{28,30},{32,34}... | collective-permute-start | bytes 786440 | tf_op jit(solution)/shard_map/ppermute | solution.py:378
  8.5 4.5 %near.1 = (f32[1024,512]{1,0:T(8,128)S(1)}, bf16[1024,512]{1,0:T(8,128)(2,1)S(1)}, bf16[1024,512]{1,0:T(8,128)(2,1)S(1)}, bf16[1536,512]{1,0:T(8,128)(2,1)S(1)}, bf16[512,512]{1,0:T(8,128)(2,1)S(1)}) custom-call(s32[5]{0:T(128)S(1)} %stack.20.scalars, s32[1,1024]{1,0:T(1,128)} %bitcast.16, bf16[512,512]{1,0:T(8,128)(2,1)} %bitcast.25, ...), custom_call_target="tpu_custom_call" | custom-call | flops 1610612736 | bytes 9965588 | tf_op jit(solution)/shard_map/near/pallas_call | solution.py:91
  13.0 0.4 collective-permute-done.stack_first
  13.5 7.0 %edges.1 = (bf16[1040,512]{1,0:T(8,128)(2,1)S(1)}, f32[8,512]{1,0:T(8,128)S(1)}, bf16[1024,512]{1,0:T(8,128)(2,1)S(1)}, bf16[1024,512]{1,0:T(8,128)(2,1)S(1)}, b...) custom-call(s32[5]{0:T(128)S(1)} %stack.20.scalars, s32[1,1024]{1,0:T(1,128)S(1)} %bitcast.18, ...), custom_call_target="tpu_custom_call" | custom-call | flops 3758096384 | bytes 12359700 | tf_op jit(solution)/shard_map/edges/pallas_call | solution.py:91
  20.4 1.6 %collective-permute-start.2 = (bf16[1040,512]{1,0:T(8,128)(2,1)S(1)}, bf16[1040,512]{1,0:T(8,128)(2,1)S(1)}, u32[]{:S(2)}, u32[]{:S(2)}) collective-permute-start(bf16[1040,512]{1,0:T(8,128)(2,1)S(1)} %get-tuple-element.39), channel_id=1, source_target_pairs={{0,1},{1,0},{2,3},{3,2},{4,5},{5,4},{6,7},{7,6},{8,9},{9,8},{10,11... | collective-permute-start | bytes 3194888 | tf_op jit(solution)/shard_map/ppermute | solution.py:382
  22.1 1.8 %kept.1 = f32[1024,512]{1,0:T(8,128)S(1)} custom-call(s32[5]{0:T(128)S(1)} %stack.20.scalars, bf16[1024,512]{1,0:T(8,128)(2,1)S(1)} %get-tuple-element.32.edge, bf16[1024,512]{1,0:T(8,128)(2,1)S(1)} %get-tuple-element.31.grid_picked, bf16[1024,512]{1,0:T(8,128)(2,1)S(1)} %get-tuple-element.36.mesh_picked, bf16[1024,512]{1,0:T(8,128)(2,1)S(1)} %get-tuple-element.37.hidden, ...), custom_call_target="tpu_custom_call" | custom-call | flops 1073741824 | bytes 8388628 | tf_op jit(solution)/shard_map/kept/pallas_call | solution.py:91
  23.9 0.5 collective-permute-done.2.got
  24.4 1.2 %pack.1 = (bf16[32,136,128]{2,1,0:T(8,128)(2,1)}, f32[8,128]{1,0:T(8,128)S(1)}) custom-call(f32[1024,512]{1,0:T(8,128)S(1)} %kept.1, bf16[1040,512]{1,0:T(8,128)(2,1)S(1)} %collective-permute-done.2.got, f32[8,512]{1,0:T(8,128)S(1)} %get-tuple-element.40.gain_term), custom_call_target="tpu_custom_call" | custom-call | bytes 4296704 | tf_op jit(solution)/shard_map/pack/pallas_call | solution.py:91
  25.6 11.1 %all-to-all-start = ((bf16[32,136,128]{2,1,0:T(8,128)(2,1)}), bf16[32,136,128]{2,1,0:T(8,128)(2,1)S(1)}, u32[]{:S(2)}, u32[]{:S(2)}) async-start(bf16[32,136,128]{2,1,0:T(8,128)(2,1)} %get-tuple-element.47), calls=%async_computation | async-start | bytes 2228224 | tf_op jit(solution)/shard_map/all_to_all | solution.py:510
  36.7 1.4 %copy-done.5 = bf16[1536,512]{1,0:T(8,128)(2,1)S(1)} copy-done((bf16[1536,512]{1,0:T(8,128)(2,1)S(1)}, bf16[1536,512]{1,0:T(8,128)(2,1)}, u32[]{:S(2)}) %copy-start.5) | copy-done | bytes 1572888
  38.1 4.0 %nodes.1 = (bf16[1024,512]{1,0:T(8,128)(2,1)}, bf16[512,512]{1,0:T(8,128)(2,1)}, f32[128,512]{1,0:T(8,128)S(1)}, bf16[128,512]{1,0:T(8,128)(2,1)S(1)}, bf16[128,512]{1,0:T(8,128)(2,1)S(1)}) custom-call(s32[5]{0:T(128)S(1)} %stack.20.scalars, s32[1,1024]{1,0:T(1,128)S(1)} %bitcast.17, s32[1,1024]{1,0:T(1,128)S(1)} %bitcast.19, ...), custom_call_target="tpu_custom_call" | custom-call | flops 2147483648 | bytes 4730900 | tf_op jit(solution)/shard_map/nodes/pallas_call | solution.py:91
  42.1 1.1 %collective-permute-start.3 = (bf16[128,512]{1,0:T(8,128)(2,1)S(1)}, bf16[128,512]{1,0:T(8,128)(2,1)S(1)}, u32[]{:S(2)}, u32[]{:S(2)}) collective-permute-start(bf16[128,512]{1,0:T(8,128)(2,1)S(1)} %get-tuple-element.44), channel_id=1, source_target_pairs={{0,2},{4,6},{8,10},{12,14},{16,18},{20,22},{24,26},{28,30},{32,34}... | collective-permute-start | bytes 393224 | tf_op jit(solution)/shard_map/ppermute | solution.py:378
  43.2 0.7 collective-permute-start.4
  43.8 11.0 %all-to-all-done.shares = bf16[32,136,128]{2,1,0:T(8,128)(2,1)S(1)} async-done(((bf16[32,136,128]{2,1,0:T(8,128)(2,1)}), bf16[32,136,128]{2,1,0:T(8,128)(2,1)S(1)}, u32[]{:S(2)}, u32[]{:S(2)}) %all-to-all-start) | async-done | bytes 1114144 | tf_op jit(solution)/shard_map/all_to_all | solution.py:510
  54.9 4.4 %collective-permute-start.7 = (bf16[136,128]{1,0:T(8,128)(2,1)S(1)}, bf16[136,128]{1,0:T(8,128)(2,1)S(1)}, u32[]{:S(2)}, u32[]{:S(2)}) collective-permute-start(bf16[136,128]{1,0:T(8,128)(2,1)S(1)} %group_sum.1.own), channel_id=1, source_target_pairs={{0,12},{4,0},{8,4},{12,8},{1,13},{5,1},{9,5},{13,9},{2,14},{6,2},{... | collective-permute-start | bytes 104456 | tf_op jit(solution)/shard_map/ppermute | solution.py:520
  59.4 2.1 %collective-permute-start.5 = (bf16[136,128]{1,0:T(8,128)(2,1)S(1)}, bf16[136,128]{1,0:T(8,128)(2,1)S(1)}, u32[]{:S(2)}, u32[]{:S(2)}) collective-permute-start(bf16[136,128]{1,0:T(8,128)(2,1)S(1)} %group_sum.1.own), channel_id=1, source_target_pairs={{0,4},{4,8},{8,12},{12,0},{1,5},{5,9},{9,13},{13,1},{2,6},{6,10},{... | collective-permute-start | bytes 104456 | tf_op jit(solution)/shard_map/ppermute | solution.py:520
  61.6 4.8 %collective-permute-done.6.across = bf16[136,128]{1,0:T(8,128)(2,1)S(1)} collective-permute-done((bf16[136,128]{1,0:T(8,128)(2,1)S(1)}, bf16[136,128]{1,0:T(8,128)(2,1)S(1)}, u32[]{:S(2)}, u32[]{:S(2)}) %collective-permute-start.6) | collective-permute-done | bytes 34848 | tf_op jit(solution)/shard_map/ppermute | solution.py:520
  66.5 21.2 %all_to_all.10.shares = bf16[32,128,128]{2,1,0:T(8,128)(2,1)S(1)} all-to-all(bf16[32,128,128]{2,1,0:T(8,128)(2,1)S(1)} %get-tuple-element.48), channel_id=1, replica_groups=mesh['band'=16,'hi'=4,'lo'=2,'rep'=2] {'band','lo'}, dimensions={0} | all-to-all | bytes 2097152 | tf_op jit(solution)/shard_map/all_to_all | solution.py:531
  87.7 3.0 %collective-permute-start.8 = (bf16[32,128,128]{2,1,0:T(8,128)(2,1)S(1)}, bf16[32,128,128]{2,1,0:T(8,128)(2,1)S(1)}, u32[]{:S(2)}, u32[]{:S(2)}) collective-permute-start(bf16[32,128,128]{2,1,0:T(8,128)(2,1)S(1)} %all_to_all.10.shares), channel_id=1, source_target_pairs={{0,1},{1,0},{2,3},{3,2},{4,5},{5,4},{6,7},{7,6},{8,9},{9,8},{10,11... | collective-permute-start | bytes 3145736 | tf_op jit(solution)/shard_map/ppermute | solution.py:382
  90.8 0.6 slice.3
  91.4 1.9 %own_half.1 = (f32[1536,512]{1,0:T(8,128)}, f32[512,512]{1,0:T(8,128)}) custom-call(s32[5]{0:T(128)S(1)} %stack.20.scalars, bf16[32,128,128]{2,1,0:T(8,128)(2,1)S(1)} %all_to_all.10.shares), custom_call_target="tpu_custom_call" | custom-call | bytes 6291456 | tf_op jit(solution)/shard_map/own_half/pallas_call | solution.py:545
  93.3 1.9 %other_half.1 = (f32[1536,512]{1,0:T(8,128)}, f32[512,512]{1,0:T(8,128)}) custom-call(s32[5]{0:T(128)S(1)} %stack.20.scalars, bf16[32,128,128]{2,1,0:T(8,128)(2,1)S(1)} %collective-permute-done.8.shares, f32[1536,512]{1,0:T(8,128)} %get-tuple-element.49.first_in, f32[512,512]{1,0:T(8,128)} %get-tuple-element.50.second_in), custom_call_target="tpu_custom_call", output_to_operand_aliasing={{0}: (2, {}), {1}: (3, {})} | custom-call | bytes 6291456 | tf_op jit(solution)/shard_map/other_half/pallas_call | solution.py:546
  (22 shorter events, 0.5 us)
Async XLA Ops:
  1.6 11.4 %collective-permute-start.1 = (bf16[256,512]{1,0:T(8,128)(2,1)S(1)}, bf16[256,512]{1,0:T(8,128)(2,1)S(1)}, u32[]{:S(2)}, u32[]{:S(2)}) collective-permute-start(bf16[256,512]{1,0:T(8,128)(2,1)S(1)} %stack.21.stack_own), channel_id=1, source_target_pairs={{2,4},{6,8},{10,12},{14,16},{18,20},{22,24},{26,28},{30,32},{34,36... | collective-permute-start | bytes 786440 | tf_op jit(solution)/shard_map/ppermute | solution.py:378
  2.3 11.1 %collective-permute-start = (bf16[256,512]{1,0:T(8,128)(2,1)S(1)}, bf16[256,512]{1,0:T(8,128)(2,1)S(1)}, u32[]{:S(2)}, u32[]{:S(2)}) collective-permute-start(bf16[256,512]{1,0:T(8,128)(2,1)S(1)} %stack.21.stack_own), channel_id=1, source_target_pairs={{0,2},{4,6},{8,10},{12,14},{16,18},{20,22},{24,26},{28,30},{32,34}... | collective-permute-start | bytes 786440 | tf_op jit(solution)/shard_map/ppermute | solution.py:378
  8.5 5.0 %copy-start.2 = (s32[1024]{0:T(1024)S(1)}, s32[1024]{0:T(1024)}, u32[]{:S(2)}) copy-start(s32[1024]{0:T(1024)} %param.18) | copy-start | bytes 12292
  8.5 5.0 %copy-start.3 = (f32[512]{0:T(512)S(1)}, f32[512]{0:T(512)}, u32[]{:S(2)}) copy-start(f32[512]{0:T(512)} %param.16) | copy-start | bytes 6148
  13.0 7.4 %copy-start.4 = (bf16[1536,512]{1,0:T(8,128)(2,1)}, bf16[1536,512]{1,0:T(8,128)(2,1)S(1)}, u32[]{:S(2)}) copy-start(bf16[1536,512]{1,0:T(8,128)(2,1)S(1)} %get-tuple-element.33.w_first) | copy-start | bytes 4718596
  20.4 3.9 %collective-permute-start.2 = (bf16[1040,512]{1,0:T(8,128)(2,1)S(1)}, bf16[1040,512]{1,0:T(8,128)(2,1)S(1)}, u32[]{:S(2)}, u32[]{:S(2)}) collective-permute-start(bf16[1040,512]{1,0:T(8,128)(2,1)S(1)} %get-tuple-element.39), channel_id=1, source_target_pairs={{0,1},{1,0},{2,3},{3,2},{4,5},{5,4},{6,7},{7,6},{8,9},{9,8},{10,11... | collective-permute-start | bytes 3194888 | tf_op jit(solution)/shard_map/ppermute | solution.py:382
  25.6 11.1 %copy-start.1 = (s32[1024]{0:T(1024)S(1)}, s32[1024]{0:T(1024)}, u32[]{:S(2)}) copy-start(s32[1024]{0:T(1024)} %param.17) | copy-start | bytes 12292
  25.6 29.2 %all-to-all-start = ((bf16[32,136,128]{2,1,0:T(8,128)(2,1)}), bf16[32,136,128]{2,1,0:T(8,128)(2,1)S(1)}, u32[]{:S(2)}, u32[]{:S(2)}) async-start(bf16[32,136,128]{2,1,0:T(8,128)(2,1)} %get-tuple-element.47), calls=%async_computation | async-start | bytes 2228224 | tf_op jit(solution)/shard_map/all_to_all | solution.py:510
  36.7 1.4 %copy-start.5 = (bf16[1536,512]{1,0:T(8,128)(2,1)S(1)}, bf16[1536,512]{1,0:T(8,128)(2,1)}, u32[]{:S(2)}) copy-start(bf16[1536,512]{1,0:T(8,128)(2,1)} %copy-done.4) | copy-start | bytes 4718596
  42.1 19.4 %collective-permute-start.3 = (bf16[128,512]{1,0:T(8,128)(2,1)S(1)}, bf16[128,512]{1,0:T(8,128)(2,1)S(1)}, u32[]{:S(2)}, u32[]{:S(2)}) collective-permute-start(bf16[128,512]{1,0:T(8,128)(2,1)S(1)} %get-tuple-element.44), channel_id=1, source_target_pairs={{0,2},{4,6},{8,10},{12,14},{16,18},{20,22},{24,26},{28,30},{32,34}... | collective-permute-start | bytes 393224 | tf_op jit(solution)/shard_map/ppermute | solution.py:378
  43.2 18.4 %collective-permute-start.4 = (bf16[128,512]{1,0:T(8,128)(2,1)S(1)}, bf16[128,512]{1,0:T(8,128)(2,1)S(1)}, u32[]{:S(2)}, u32[]{:S(2)}) collective-permute-start(bf16[128,512]{1,0:T(8,128)(2,1)S(1)} %get-tuple-element.45), channel_id=1, source_target_pairs={{2,4},{6,8},{10,12},{14,16},{18,20},{22,24},{26,28},{30,32},{34,36... | collective-permute-start | bytes 393224 | tf_op jit(solution)/shard_map/ppermute | solution.py:378
  54.9 6.6 %collective-permute-start.7 = (bf16[136,128]{1,0:T(8,128)(2,1)S(1)}, bf16[136,128]{1,0:T(8,128)(2,1)S(1)}, u32[]{:S(2)}, u32[]{:S(2)}) collective-permute-start(bf16[136,128]{1,0:T(8,128)(2,1)S(1)} %group_sum.1.own), channel_id=1, source_target_pairs={{0,12},{4,0},{8,4},{12,8},{1,13},{5,1},{9,5},{13,9},{2,14},{6,2},{... | collective-permute-start | bytes 104456 | tf_op jit(solution)/shard_map/ppermute | solution.py:520
  59.3 7.1 %collective-permute-start.6 = (bf16[136,128]{1,0:T(8,128)(2,1)S(1)}, bf16[136,128]{1,0:T(8,128)(2,1)S(1)}, u32[]{:S(2)}, u32[]{:S(2)}) collective-permute-start(bf16[136,128]{1,0:T(8,128)(2,1)S(1)} %group_sum.1.own), channel_id=1, source_target_pairs={{0,8},{4,12},{8,0},{12,4},{1,9},{5,13},{9,1},{13,5},{2,10},{6,14},... | collective-permute-start | bytes 104456 | tf_op jit(solution)/shard_map/ppermute | solution.py:520
  59.4 7.0 %collective-permute-start.5 = (bf16[136,128]{1,0:T(8,128)(2,1)S(1)}, bf16[136,128]{1,0:T(8,128)(2,1)S(1)}, u32[]{:S(2)}, u32[]{:S(2)}) collective-permute-start(bf16[136,128]{1,0:T(8,128)(2,1)S(1)} %group_sum.1.own), channel_id=1, source_target_pairs={{0,4},{4,8},{8,12},{12,0},{1,5},{5,9},{9,13},{13,1},{2,6},{6,10},{... | collective-permute-start | bytes 104456 | tf_op jit(solution)/shard_map/ppermute | solution.py:520
  61.6 31.7 %copy-start = (f32[128,512]{1,0:T(8,128)}, f32[128,512]{1,0:T(8,128)S(1)}, u32[]{:S(2)}) copy-start(f32[128,512]{1,0:T(8,128)S(1)} %convert_add_fusion.after) | copy-start | bytes 786436
  87.7 5.6 %collective-permute-start.8 = (bf16[32,128,128]{2,1,0:T(8,128)(2,1)S(1)}, bf16[32,128,128]{2,1,0:T(8,128)(2,1)S(1)}, u32[]{:S(2)}, u32[]{:S(2)}) collective-permute-start(bf16[32,128,128]{2,1,0:T(8,128)(2,1)S(1)} %all_to_all.10.shares), channel_id=1, source_target_pairs={{0,1},{1,0},{2,3},{3,2},{4,5},{5,4},{6,7},{7,6},{8,9},{9,8},{10,11... | collective-permute-start | bytes 3145736 | tf_op jit(solution)/shard_map/ppermute | solution.py:382

commit v7 on v6

--- a/solution.py
+++ b/solution.py
@@ -98,18 +98,6 @@
         cost_estimate=pl.CostEstimate(flops=int(flops), bytes_accessed=size, transcendentals=0),
         name=name,
     )(*operands)
-
-
-def stack_kernel(mesh, cot, stacked, sems):
-    rows = mesh.shape[0]
-    copies = [
-        pltpu.make_async_copy(mesh, stacked.at[pl.ds(0, rows)], sems.at[0]),
-        pltpu.make_async_copy(cot, stacked.at[pl.ds(rows, rows)], sems.at[1]),
-    ]
-    for copy in copies:
-        copy.start()
-    for copy in copies:
-        copy.wait()
 
 
 def near_kernel(
@@ -160,74 +148,87 @@
         copy.wait()
 
 
-def live_receivers(scalars, receivers, start, rows_mesh):
-    row = receivers[:, pl.ds(start, TILE)] - scalars[1]
+def live_receivers(scalars, receivers, start, tile, rows_mesh):
+    row = receivers[:, pl.ds(start, tile)] - scalars[1]
     row = jnp.where(
         row < rows_mesh,
         row + scalars[4],
         jnp.where(row >= 2 * rows_mesh, row - scalars[4], row),
     )
-    slot = start + lax.broadcasted_iota(jnp.int32, (1, TILE), 1)
+    slot = start + lax.broadcasted_iota(jnp.int32, (1, tile), 1)
     return jnp.where(slot < scalars[2], row, -1)
 
 
-def edge_kernel(
+def picked_near(scalars, receivers, first, own, second):
+    rows_mesh = own.shape[0]
+    table = picks(live_receivers(scalars, receivers, 0, receivers.shape[1], rows_mesh), 3 * rows_mesh)
+    return dot(table, jnp.concatenate([first[...], own[...], second[...]], axis=0))
+
+
+def forward_kernel(
     scalars,
     receivers,
     partial,
+    mesh_first,
+    mesh_own,
+    mesh_second,
+    w_first,
+    w_second,
+    pre_act,
+    output,
+    hidden,
+    mesh_picked,
+):
+    width = w_second.shape[0]
+    latents = picked_near(scalars, receivers, mesh_first, mesh_own, mesh_second).astype(jnp.bfloat16)
+    mesh_picked[...] = latents
+    pre = partial[...] + dot(latents, w_first[2 * width : 3 * width, :])
+    pre_act[...] = pre
+    hid = (pre * (0.5 * jnp.tanh(0.5 * pre) + 0.5)).astype(jnp.bfloat16)
+    hidden[...] = hid
+    output[...] = dot(hid, w_second[...])
+
+
+def backward_kernel(
+    scalars,
+    receivers,
+    cot_first,
+    cot_own,
+    cot_second,
+    pre_act,
+    output,
+    hidden,
+    mesh_picked,
     grid_picked,
     edge,
-    stack_first,
-    stack_own,
-    stack_second,
-    w_first,
     w_second,
     norm_gain,
     sent,
     gain_term,
     grad_pre,
     grad_output,
-    hidden,
-    mesh_picked,
 ):
     width = w_second.shape[0]
-    rows_mesh = stack_own.shape[0] // 2
-    gain_sum = jnp.zeros((1, width), jnp.float32)
-    for start in range(0, edge.shape[0], TILE):
-        rows = pl.ds(start, TILE)
-        table = picks(live_receivers(scalars, receivers, start, rows_mesh), 3 * rows_mesh)
-
-        def picked_rows(first):
-            part = pl.ds(first, rows_mesh)
-            near = jnp.concatenate([stack_first[part, :], stack_own[part, :], stack_second[part, :]], axis=0)
-            return dot(table, near)
-
-        latents = picked_rows(0).astype(jnp.bfloat16)
-        upstream = picked_rows(rows_mesh)
-        mesh_picked[rows, :] = latents
-        pre_act = partial[rows, :] + dot(latents, w_first[2 * width : 3 * width, :])
-        sigmoid = 0.5 * jnp.tanh(0.5 * pre_act) + 0.5
-        hid = (pre_act * sigmoid).astype(jnp.bfloat16)
-        hidden[rows, :] = hid
-        output = dot(hid, w_second[...])
-        centered = output - jnp.mean(output, axis=1, keepdims=True)
-        inverse = lax.rsqrt(jnp.mean(centered * centered, axis=1, keepdims=True) + NORM_EPS)
-        normed = centered * inverse
-        gain_sum = gain_sum + jnp.sum(upstream * normed, axis=0, keepdims=True)
-        scaled = upstream * norm_gain[...]
-        grad_out = (
-            inverse
-            * (
-                scaled
-                - jnp.mean(scaled, axis=1, keepdims=True)
-                - normed * jnp.mean(scaled * normed, axis=1, keepdims=True)
-            )
-        ).astype(jnp.bfloat16)
-        grad_output[rows, :] = grad_out
-        grad_hidden = dot(grad_out, w_second[...], 1, 1)
-        grad_pre[rows, :] = (grad_hidden * sigmoid * (1.0 + pre_act * (1.0 - sigmoid))).astype(
-            jnp.bfloat16
+    upstream = picked_near(scalars, receivers, cot_first, cot_own, cot_second)
+    out = output[...]
+    centered = out - jnp.mean(out, axis=1, keepdims=True)
+    inverse = lax.rsqrt(jnp.mean(centered * centered, axis=1, keepdims=True) + NORM_EPS)
+    normed = centered * inverse
+    gain_sum = jnp.sum(upstream * normed, axis=0, keepdims=True)
+    scaled = upstream * norm_gain[...]
+    grad_out = (
+        inverse
+        * (
+            scaled
+            - jnp.mean(scaled, axis=1, keepdims=True)
+            - normed * jnp.mean(scaled * normed, axis=1, keepdims=True)
         )
+    ).astype(jnp.bfloat16)
+    grad_output[...] = grad_out
+    grad_hidden = dot(grad_out, w_second[...], 1, 1)
+    pre = pre_act[...]
+    sigmoid = 0.5 * jnp.tanh(0.5 * pre) + 0.5
+    grad_pre[...] = (grad_hidden * sigmoid * (1.0 + pre * (1.0 - sigmoid))).astype(jnp.bfloat16)
     gain_term[...] = jnp.broadcast_to(gain_sum, gain_term.shape)
     sent[2 * width : 2 * width + 16, :] = jnp.concatenate(
         [gain_rows(gain_sum, width), jnp.zeros((14, width), jnp.float32)], axis=0
@@ -280,9 +281,15 @@
     packed[...] = jnp.concatenate([total[:data], gain], axis=0).astype(jnp.bfloat16)
 
 
-def whole_sum_kernel(factor, own, ahead, across, behind, after, copies, gain_grad):
-    own, ahead, across, behind = [part[...].astype(jnp.float32) for part in (own, ahead, across, behind)]
-    total = ((own + across) + (ahead + behind)) * factor
+def pair_sum_kernel(own, other, packed):
+    total = own[...].astype(jnp.float32) + other[...].astype(jnp.float32)
+    data = total.shape[0] - 8
+    gain = gain_rows(gain_of(total[data:]), LANES)
+    packed[...] = jnp.concatenate([total[:data], gain], axis=0).astype(jnp.bfloat16)
+
+
+def whole_sum_kernel(factor, own, other, after, copies, gain_grad):
+    total = (own[...].astype(jnp.float32) + other[...].astype(jnp.float32)) * factor
     data = copies.shape[1]
     gain_grad[...] = jnp.broadcast_to(gain_of(total[data:]), gain_grad.shape)
     share = total[:data].astype(jnp.bfloat16)
@@ -317,7 +324,7 @@
         rows = pl.ds(start, TILE)
         terms = grad_pre[rows, :]
         near = near + dot(
-            spreads(live_receivers(scalars, receivers, start, rows_mesh), 3 * rows_mesh), terms
+            spreads(live_receivers(scalars, receivers, start, TILE, rows_mesh), 3 * rows_mesh), terms
         )
         here = here + dot(spreads(senders[:, rows] - scalars[0], rows_grid), terms)
         edge_grad[rows, :] = dot(terms, w_first[0:width, :], 1, 1).astype(jnp.bfloat16)
@@ -372,14 +379,17 @@
     put_half(scalars, True, shares, first, second, wide, sems)
 
 
+def swap_pairs(value, axis, pairs):
+    return lax.ppermute(value, axis, pairs + [(d, s) for s, d in pairs])
+
+
 def exchanged(value, turn):
     count = lax.axis_size(SHARDS)
-    pairs = [(s, s + 1) for s in range(turn, count - 1, 2)]
-    return lax.ppermute(value, SHARDS, pairs + [(d, s) for s, d in pairs])
+    return swap_pairs(value, SHARDS, [(s, s + 1) for s in range(turn, count - 1, 2)])
 
 
 def swapped(value):
-    return lax.ppermute(value, "rep", [(0, 1), (1, 0)])
+    return swap_pairs(value, "rep", [(0, 1)])
 
 
 def per_device(
@@ -417,16 +427,8 @@
     floats = functools.partial(jax.ShapeDtypeStruct, dtype=jnp.float32)
     unit = 2.0 * slots * width * width
 
-    (stacked,) = call(
-        stack_kernel,
-        "stack",
-        [in_hbm()] * 2,
-        [matrix((2 * rows_mesh, width))],
-        (mesh, cot),
-        0,
-        [pltpu.SemaphoreType.DMA((2,))],
-    )
-    stack_first, stack_second = exchanged(stacked, 0), exchanged(stacked, 1)
+    mesh_second, mesh_first = exchanged(mesh, 1), exchanged(mesh, 0)
+    cot_second, cot_first = exchanged(cot, 1), exchanged(cot, 0)
     partial, grid_picked, edge, w_first, w_second = call(
         near_kernel,
         "near",
@@ -446,30 +448,40 @@
             pltpu.SemaphoreType.DMA((6 + slots // TILE,)),
         ],
     )
-    sent, gain_term, grad_pre, grad_output, hidden, mesh_picked = call(
-        edge_kernel,
-        "edges",
-        [in_smem()] + [in_vmem()] * 10,
+    pre_act, output, hidden, mesh_picked = call(
+        forward_kernel,
+        "forward",
+        [in_smem()] + [in_vmem()] * 7,
+        [floats((slots, width))] * 2 + [matrix((slots, width))] * 2,
+        (scalars, receivers, partial, mesh_first, mesh, mesh_second, w_first, w_second),
+        3 * unit,
+    )
+    sent, gain_term, grad_pre, grad_output = call(
+        backward_kernel,
+        "backward",
+        [in_smem()] + [in_vmem()] * 12,
         [
             matrix((2 * width + 16, width)),
             floats((8, width)),
             pltpu.VMEM((slots, width), jnp.bfloat16),
-        ]
-        + [matrix((slots, width))] * 3,
+            matrix((slots, width)),
+        ],
         (
             scalars,
             receivers,
-            partial,
+            cot_first,
+            cot,
+            cot_second,
+            pre_act,
+            output,
+            hidden,
+            mesh_picked,
             grid_picked,
             edge,
-            stack_first,
-            stacked,
-            stack_second,
-            w_first,
             w_second,
             gain,
         ),
-        7 * unit,
+        4 * unit,
     )
     got = swapped(sent)
     (kept,) = call(
@@ -516,16 +528,17 @@
         (shares, mesh_own),
         0,
     )
-    turns = [
-        lax.ppermute(packed, "hi", [(i, (i + turn) % groups) for i in range(groups)])
-        for turn in (1, 2, 3)
-    ]
+    met = swap_pairs(packed, "hi", [(0, 1), (2, 3)])
+    (packed,) = call(
+        pair_sum_kernel, "pair_sum", [in_vmem()] * 2, [matrix((part + extra, LANES))], (packed, met), 0
+    )
+    met = swap_pairs(packed, "hi", [(0, 3), (1, 2)])
     copies, gain_grad = call(
         functools.partial(whole_sum_kernel, factor),
         "whole_sum",
-        [in_vmem()] * 4 + [anywhere()],
+        [in_vmem()] * 2 + [anywhere()],
         [matrix((group, part, LANES)), floats((8, width))],
-        (packed, *turns, mesh_grad),
+        (packed, met, mesh_grad),
         0,
     )
     total = lax.all_to_all(copies, GROUP, 0, 0)

time: 95.8 us -> 95.2 us (level)
    ppermute x9 -> x10, starting transfers between devices: 19.1 us -> 22.7 us  [swap_pairs(): return lax.ppermute(value, axis, pairs + [(d, s) for s, d in pairs])]
    all_to_all x1, starting transfers between devices: 11.1 us -> 7.67 us  [per_device(): shares = lax.all_to_all(packed, GROUP, 0, 0)]
    pallas_call x8 -> x9, Pallas kernels: 19.7 us -> 18.9 us  [call(): pl.pallas_call(kernel, out_shape=outs, in_specs=specs, out_specs=[in_vmem...]
    ppermute x9 -> x10, waiting for transfers between devices: 5.71 us -> 5.8 us  [swap_pairs(): return lax.ppermute(value, axis, pairs + [(d, s) for s, d in pairs])]
  transfers between devices with their start and end apart: 10 -> 11, of which waited for: 4 -> 4; matrix products, arithmetic and copies ran while one was open for 1% -> 1% of each run, Pallas kernels for 13% -> 16%
where the time goes in v7:
time: 95.2 us; the launch traced here: 94.9 us
  starting transfers between devices  30.4 us (32%)
  Pallas kernels  22.7 us (24%)
  blocking collectives  21 us (22%)
  waiting for transfers between devices  16.9 us (18%)
  local copies, waits for them, and re-layouts  2.1 us (2%)
  between operations  1.67 us (2%)
    ppermute x10, starting transfers between devices, swap_pairs(): return lax.ppermute(value, axis, pairs + [(d, s) for s, d in pairs])  22.7 us
    all_to_all x1, blocking collectives, per_device(): total = lax.all_to_all(copies, GROUP, 0, 0)  21 us
    pallas_call x9, Pallas kernels, call(): pl.pallas_call(kernel, out_shape=outs, in_specs=specs, out_specs=[in_vmem...  18.9 us
    all_to_all x1, waiting for transfers between devices, per_device(): shares = lax.all_to_all(packed, GROUP, 0, 0)  11.1 us
    all_to_all x1, starting transfers between devices, per_device(): shares = lax.all_to_all(packed, GROUP, 0, 0)  7.67 us
    ppermute x10, waiting for transfers between devices, swap_pairs(): return lax.ppermute(value, axis, pairs + [(d, s) for s, d in pairs])  5.8 us
    pallas_call x1, Pallas kernels, per_device(): halves(other_half_kernel, in_specs=[in_smem(), in_vmem()] + [in_hbm()] *...  1.94 us
    pallas_call x1, Pallas kernels, per_device(): halves(own_half_kernel, in_specs=[in_smem(), in_vmem()], name='own_half')  1.93 us
  transfers between devices with their start and end apart: 11, of which 4 were waited for; matrix products, arithmetic and copies ran while one was open for 1% of the time, Pallas kernels for 16%

profile of v7, /device:TPU:1, one launch (start us, length us, event | category | flops | bytes accessed | tf_op | source)
XLA Modules:
  0.0 94.9 jit_solution(1724968602403826158)
XLA Ops:
  0.6 0.7 collective-permute-start.3
  1.3 5.4 %collective-permute-start.2 = (bf16[128,512]{1,0:T(8,128)(2,1)}, bf16[128,512]{1,0:T(8,128)(2,1)S(1)}, u32[]{:S(2)}, u32[]{:S(2)}) collective-permute-start(bf16[128,512]{1,0:T(8,128)(2,1)} %bitcast.24), channel_id=1, source_target_pairs={{0,2},{4,6},{8,10},{12,14},{16,18},{20,22},{24,26},{28,30},{32,34}... | collective-permute-start | bytes 393224 | tf_op jit(solution)/shard_map/ppermute | solution.py:383
  6.7 0.7 collective-permute-start.1
  7.4 5.8 %collective-permute-start = (bf16[128,512]{1,0:T(8,128)(2,1)}, bf16[128,512]{1,0:T(8,128)(2,1)S(1)}, u32[]{:S(2)}, u32[]{:S(2)}) collective-permute-start(bf16[128,512]{1,0:T(8,128)(2,1)} %bitcast.17), channel_id=1, source_target_pairs={{0,2},{4,6},{8,10},{12,14},{16,18},{20,22},{24,26},{28,30},{32,34}... | collective-permute-start | bytes 393224 | tf_op jit(solution)/shard_map/ppermute | solution.py:383
  14.0 4.5 %near.1 = (f32[1024,512]{1,0:T(8,128)S(1)}, bf16[1024,512]{1,0:T(8,128)(2,1)S(1)}, bf16[1024,512]{1,0:T(8,128)(2,1)S(1)}, bf16[1536,512]{1,0:T(8,128)(2,1)S(1)}, bf16[512,512]{1,0:T(8,128)(2,1)S(1)}) custom-call(s32[5]{0:T(128)S(1)} %stack.19.scalars, s32[1,1024]{1,0:T(1,128)} %bitcast.26, bf16[512,512]{1,0:T(8,128)(2,1)} %bitcast.30, ...), custom_call_target="tpu_custom_call" | custom-call | flops 1610612736 | bytes 9965588 | tf_op jit(solution)/shard_map/near/pallas_call | solution.py:91
  18.6 2.5 %forward.1 = (f32[1024,512]{1,0:T(8,128)S(1)}, f32[1024,512]{1,0:T(8,128)S(1)}, bf16[1024,512]{1,0:T(8,128)(2,1)S(1)}, bf16[1024,512]{1,0:T(8,128)(2,1)S(1)}) custom-call(s32[5]{0:T(128)S(1)} %stack.19.scalars, s32[1,1024]{1,0:T(1,128)S(1)} %bitcast.19, f32[1024,512]{1,0:T(8,128)S(1)} %get-tuple-element.32.partial, ...), custom_call_target="tpu_custom_call" | custom-call | flops 1610612736 | bytes 10883092 | tf_op jit(solution)/shard_map/forward/pallas_call | solution.py:91
  21.1 4.5 %backward.1 = (bf16[1040,512]{1,0:T(8,128)(2,1)S(1)}, f32[8,512]{1,0:T(8,128)S(1)}, bf16[1024,512]{1,0:T(8,128)(2,1)S(1)}, bf16[1024,512]{1,0:T(8,128)(2,1)S(1)}) custom-call(s32[5]{0:T(128)S(1)} %stack.19.scalars, s32[1,1024]{1,0:T(1,128)S(1)} %bitcast.20, bf16[128,512]{1,0:T(8,128)(2,1)S(1)} %collective-permute-done.cot_first, ...), custom_call_target="tpu_custom_call" | custom-call | flops 2147483648 | bytes 12490772 | tf_op jit(solution)/shard_map/backward/pallas_call | solution.py:91
  25.6 1.9 %collective-permute-start.4 = (bf16[1040,512]{1,0:T(8,128)(2,1)S(1)}, bf16[1040,512]{1,0:T(8,128)(2,1)S(1)}, u32[]{:S(2)}, u32[]{:S(2)}) collective-permute-start(bf16[1040,512]{1,0:T(8,128)(2,1)S(1)} %get-tuple-element.43), channel_id=1, source_target_pairs={{0,1},{1,0},{2,3},{3,2},{4,5},{5,4},{6,7},{7,6},{8,9},{9,8},{10,11... | collective-permute-start | bytes 3194888 | tf_op jit(solution)/shard_map/ppermute | solution.py:383
  27.5 1.8 %kept.1 = f32[1024,512]{1,0:T(8,128)S(1)} custom-call(s32[5]{0:T(128)S(1)} %stack.19.scalars, bf16[1024,512]{1,0:T(8,128)(2,1)S(1)} %get-tuple-element.40.edge, bf16[1024,512]{1,0:T(8,128)(2,1)S(1)} %get-tuple-element.39.grid_picked, bf16[1024,512]{1,0:T(8,128)(2,1)S(1)} %get-tuple-element.38.mesh_picked, bf16[1024,512]{1,0:T(8,128)(2,1)S(1)} %get-tuple-element.37.hidden, ...), custom_call_target="tpu_custom_call" | custom-call | flops 1073741824 | bytes 8388628 | tf_op jit(solution)/shard_map/kept/pallas_call | solution.py:91
  29.9 1.3 %pack.1 = (bf16[32,136,128]{2,1,0:T(8,128)(2,1)}, f32[8,128]{1,0:T(8,128)S(1)}) custom-call(f32[1024,512]{1,0:T(8,128)S(1)} %kept.1, bf16[1040,512]{1,0:T(8,128)(2,1)S(1)} %collective-permute-done.4.got, f32[8,512]{1,0:T(8,128)S(1)} %get-tuple-element.44.gain_term), custom_call_target="tpu_custom_call" | custom-call | bytes 4296704 | tf_op jit(solution)/shard_map/pack/pallas_call | solution.py:91
  31.1 7.7 %all-to-all-start = ((bf16[32,136,128]{2,1,0:T(8,128)(2,1)}), bf16[32,136,128]{2,1,0:T(8,128)(2,1)S(1)}, u32[]{:S(2)}, u32[]{:S(2)}) async-start(bf16[32,136,128]{2,1,0:T(8,128)(2,1)} %get-tuple-element.51), calls=%async_computation | async-start | bytes 2228224 | tf_op jit(solution)/shard_map/all_to_all | solution.py:522
  38.8 1.4 %copy-done.7 = bf16[1536,512]{1,0:T(8,128)(2,1)S(1)} copy-done((bf16[1536,512]{1,0:T(8,128)(2,1)S(1)}, bf16[1536,512]{1,0:T(8,128)(2,1)}, u32[]{:S(2)}) %copy-start.7) | copy-done | bytes 1572888
  40.2 4.0 %nodes.1 = (bf16[1024,512]{1,0:T(8,128)(2,1)}, bf16[512,512]{1,0:T(8,128)(2,1)}, f32[128,512]{1,0:T(8,128)S(1)}, bf16[128,512]{1,0:T(8,128)(2,1)S(1)}, bf16[128,512]{1,0:T(8,128)(2,1)S(1)}) custom-call(s32[5]{0:T(128)S(1)} %stack.19.scalars, s32[1,1024]{1,0:T(1,128)S(1)} %bitcast.27, s32[1,1024]{1,0:T(1,128)S(1)} %bitcast.21, ...), custom_call_target="tpu_custom_call" | custom-call | flops 2147483648 | bytes 4730900 | tf_op jit(solution)/shard_map/nodes/pallas_call | solution.py:91
  44.2 1.1 %collective-permute-start.5 = (bf16[128,512]{1,0:T(8,128)(2,1)S(1)}, bf16[128,512]{1,0:T(8,128)(2,1)S(1)}, u32[]{:S(2)}, u32[]{:S(2)}) collective-permute-start(bf16[128,512]{1,0:T(8,128)(2,1)S(1)} %get-tuple-element.48), channel_id=1, source_target_pairs={{0,2},{4,6},{8,10},{12,14},{16,18},{20,22},{24,26},{28,30},{32,34}... | collective-permute-start | bytes 393224 | tf_op jit(solution)/shard_map/ppermute | solution.py:383
  45.2 0.7 collective-permute-start.6
  45.9 11.1 %all-to-all-done.shares = bf16[32,136,128]{2,1,0:T(8,128)(2,1)S(1)} async-done(((bf16[32,136,128]{2,1,0:T(8,128)(2,1)}), bf16[32,136,128]{2,1,0:T(8,128)(2,1)S(1)}, u32[]{:S(2)}, u32[]{:S(2)}) %all-to-all-start) | async-done | bytes 1114144 | tf_op jit(solution)/shard_map/all_to_all | solution.py:522
  57.8 3.2 %collective-permute-done.7.other = bf16[136,128]{1,0:T(8,128)(2,1)S(1)} collective-permute-done((bf16[136,128]{1,0:T(8,128)(2,1)S(1)}, bf16[136,128]{1,0:T(8,128)(2,1)S(1)}, u32[]{:S(2)}, u32[]{:S(2)}) %collective-permute-start.7) | collective-permute-done | bytes 34848 | tf_op jit(solution)/shard_map/ppermute | solution.py:383
  61.0 3.2 %collective-permute-start.8 = (bf16[136,128]{1,0:T(8,128)(2,1)S(1)}, bf16[136,128]{1,0:T(8,128)(2,1)S(1)}, u32[]{:S(2)}, u32[]{:S(2)}) collective-permute-start(bf16[136,128]{1,0:T(8,128)(2,1)S(1)} %pair_sum.1.own), channel_id=1, source_target_pairs={{0,12},{4,8},{12,0},{8,4},{1,13},{5,9},{13,1},{9,5},{2,14},{6,10},... | collective-permute-start | bytes 104456 | tf_op jit(solution)/shard_map/ppermute | solution.py:383
  64.2 2.1 %collective-permute-done.8.other = bf16[136,128]{1,0:T(8,128)(2,1)S(1)} collective-permute-done((bf16[136,128]{1,0:T(8,128)(2,1)S(1)}, bf16[136,128]{1,0:T(8,128)(2,1)S(1)}, u32[]{:S(2)}, u32[]{:S(2)}) %collective-permute-start.8) | collective-permute-done | bytes 34848 | tf_op jit(solution)/shard_map/ppermute | solution.py:383
  66.4 21.0 %all_to_all.10.shares = bf16[32,128,128]{2,1,0:T(8,128)(2,1)S(1)} all-to-all(bf16[32,128,128]{2,1,0:T(8,128)(2,1)S(1)} %get-tuple-element.52), channel_id=1, replica_groups=mesh['band'=16,'hi'=4,'lo'=2,'rep'=2] {'band','lo'}, dimensions={0} | all-to-all | bytes 2097152 | tf_op jit(solution)/shard_map/all_to_all | solution.py:544
  87.5 2.8 %collective-permute-start.9 = (bf16[32,128,128]{2,1,0:T(8,128)(2,1)S(1)}, bf16[32,128,128]{2,1,0:T(8,128)(2,1)S(1)}, u32[]{:S(2)}, u32[]{:S(2)}) collective-permute-start(bf16[32,128,128]{2,1,0:T(8,128)(2,1)S(1)} %all_to_all.10.shares), channel_id=1, source_target_pairs={{0,1},{1,0},{2,3},{3,2},{4,5},{5,4},{6,7},{7,6},{8,9},{9,8},{10,11... | collective-permute-start | bytes 3145736 | tf_op jit(solution)/shard_map/ppermute | solution.py:383
  90.2 0.6 slice.3
  90.8 1.9 %own_half.1 = (f32[1536,512]{1,0:T(8,128)}, f32[512,512]{1,0:T(8,128)}) custom-call(s32[5]{0:T(128)S(1)} %stack.19.scalars, bf16[32,128,128]{2,1,0:T(8,128)(2,1)S(1)} %all_to_all.10.shares), custom_call_target="tpu_custom_call" | custom-call | bytes 6291456 | tf_op jit(solution)/shard_map/own_half/pallas_call | solution.py:558
  92.7 1.9 %other_half.1 = (f32[1536,512]{1,0:T(8,128)}, f32[512,512]{1,0:T(8,128)}) custom-call(s32[5]{0:T(128)S(1)} %stack.19.scalars, bf16[32,128,128]{2,1,0:T(8,128)(2,1)S(1)} %collective-permute-done.9.shares, f32[1536,512]{1,0:T(8,128)} %get-tuple-element.53.first_in, f32[512,512]{1,0:T(8,128)} %get-tuple-element.54.second_in), custom_call_target="tpu_custom_call", output_to_operand_aliasing={{0}: (2, {}), {1}: (3, {})} | custom-call | bytes 6291456 | tf_op jit(solution)/shard_map/other_half/pallas_call | solution.py:559
  (29 shorter events, 1.5 us)
Async XLA Ops:
  0.6 17.9 %collective-permute-start.3 = (bf16[128,512]{1,0:T(8,128)(2,1)}, bf16[128,512]{1,0:T(8,128)(2,1)S(1)}, u32[]{:S(2)}, u32[]{:S(2)}) collective-permute-start(bf16[128,512]{1,0:T(8,128)(2,1)} %bitcast.23), channel_id=1, source_target_pairs={{2,4},{6,8},{10,12},{14,16},{18,20},{22,24},{26,28},{30,32},{34,36... | collective-permute-start | bytes 393224 | tf_op jit(solution)/shard_map/ppermute | solution.py:383
  1.3 17.2 %collective-permute-start.2 = (bf16[128,512]{1,0:T(8,128)(2,1)}, bf16[128,512]{1,0:T(8,128)(2,1)S(1)}, u32[]{:S(2)}, u32[]{:S(2)}) collective-permute-start(bf16[128,512]{1,0:T(8,128)(2,1)} %bitcast.24), channel_id=1, source_target_pairs={{0,2},{4,6},{8,10},{12,14},{16,18},{20,22},{24,26},{28,30},{32,34}... | collective-permute-start | bytes 393224 | tf_op jit(solution)/shard_map/ppermute | solution.py:383
  6.7 14.3 %collective-permute-start.1 = (bf16[128,512]{1,0:T(8,128)(2,1)}, bf16[128,512]{1,0:T(8,128)(2,1)S(1)}, u32[]{:S(2)}, u32[]{:S(2)}) collective-permute-start(bf16[128,512]{1,0:T(8,128)(2,1)} %bitcast.16), channel_id=1, source_target_pairs={{2,4},{6,8},{10,12},{14,16},{18,20},{22,24},{26,28},{30,32},{34,36... | collective-permute-start | bytes 393224 | tf_op jit(solution)/shard_map/ppermute | solution.py:383
  7.4 13.7 %collective-permute-start = (bf16[128,512]{1,0:T(8,128)(2,1)}, bf16[128,512]{1,0:T(8,128)(2,1)S(1)}, u32[]{:S(2)}, u32[]{:S(2)}) collective-permute-start(bf16[128,512]{1,0:T(8,128)(2,1)} %bitcast.17), channel_id=1, source_target_pairs={{0,2},{4,6},{8,10},{12,14},{16,18},{20,22},{24,26},{28,30},{32,34}... | collective-permute-start | bytes 393224 | tf_op jit(solution)/shard_map/ppermute | solution.py:383
  14.0 4.6 %copy-start.2 = (s32[1024]{0:T(1024)S(1)}, s32[1024]{0:T(1024)}, u32[]{:S(2)}) copy-start(s32[1024]{0:T(1024)} %param.18) | copy-start | bytes 12292
  14.0 4.6 %copy-start.4 = (bf16[1,128,512]{2,1,0:T(8,128)(2,1)S(1)}, bf16[1,128,512]{2,1,0:T(8,128)(2,1)}, u32[]{:S(2)}) copy-start(bf16[1,128,512]{2,1,0:T(8,128)(2,1)} %param.11) | copy-start | bytes 393220
  18.5 2.6 %copy-start.6 = (bf16[1536,512]{1,0:T(8,128)(2,1)}, bf16[1536,512]{1,0:T(8,128)(2,1)S(1)}, u32[]{:S(2)}) copy-start(bf16[1536,512]{1,0:T(8,128)(2,1)S(1)} %get-tuple-element.33.w_first) | copy-start | bytes 4718596
  18.5 2.6 %copy-start.1 = (bf16[1,128,512]{2,1,0:T(8,128)(2,1)S(1)}, bf16[1,128,512]{2,1,0:T(8,128)(2,1)}, u32[]{:S(2)}) copy-start(bf16[1,128,512]{2,1,0:T(8,128)(2,1)} %param.13) | copy-start | bytes 393220
  18.5 2.6 %copy-start.3 = (f32[512]{0:T(512)S(1)}, f32[512]{0:T(512)}, u32[]{:S(2)}) copy-start(f32[512]{0:T(512)} %param.16) | copy-start | bytes 6148
  25.6 4.2 %collective-permute-start.4 = (bf16[1040,512]{1,0:T(8,128)(2,1)S(1)}, bf16[1040,512]{1,0:T(8,128)(2,1)S(1)}, u32[]{:S(2)}, u32[]{:S(2)}) collective-permute-start(bf16[1040,512]{1,0:T(8,128)(2,1)S(1)} %get-tuple-element.43), channel_id=1, source_target_pairs={{0,1},{1,0},{2,3},{3,2},{4,5},{5,4},{6,7},{7,6},{8,9},{9,8},{10,11... | collective-permute-start | bytes 3194888 | tf_op jit(solution)/shard_map/ppermute | solution.py:383
  29.9 8.9 %copy-start.5 = (s32[1024]{0:T(1024)S(1)}, s32[1024]{0:T(1024)}, u32[]{:S(2)}) copy-start(s32[1024]{0:T(1024)} %param.17) | copy-start | bytes 12292
  31.1 25.9 %all-to-all-start = ((bf16[32,136,128]{2,1,0:T(8,128)(2,1)}), bf16[32,136,128]{2,1,0:T(8,128)(2,1)S(1)}, u32[]{:S(2)}, u32[]{:S(2)}) async-start(bf16[32,136,128]{2,1,0:T(8,128)(2,1)} %get-tuple-element.51), calls=%async_computation | async-start | bytes 2228224 | tf_op jit(solution)/shard_map/all_to_all | solution.py:522
  38.8 1.4 %copy-start.7 = (bf16[1536,512]{1,0:T(8,128)(2,1)S(1)}, bf16[1536,512]{1,0:T(8,128)(2,1)}, u32[]{:S(2)}) copy-start(bf16[1536,512]{1,0:T(8,128)(2,1)} %copy-done.6) | copy-start | bytes 4718596
  44.2 20.0 %collective-permute-start.5 = (bf16[128,512]{1,0:T(8,128)(2,1)S(1)}, bf16[128,512]{1,0:T(8,128)(2,1)S(1)}, u32[]{:S(2)}, u32[]{:S(2)}) collective-permute-start(bf16[128,512]{1,0:T(8,128)(2,1)S(1)} %get-tuple-element.48), channel_id=1, source_target_pairs={{0,2},{4,6},{8,10},{12,14},{16,18},{20,22},{24,26},{28,30},{32,34}... | collective-permute-start | bytes 393224 | tf_op jit(solution)/shard_map/ppermute | solution.py:383
  45.2 18.9 %collective-permute-start.6 = (bf16[128,512]{1,0:T(8,128)(2,1)S(1)}, bf16[128,512]{1,0:T(8,128)(2,1)S(1)}, u32[]{:S(2)}, u32[]{:S(2)}) collective-permute-start(bf16[128,512]{1,0:T(8,128)(2,1)S(1)} %get-tuple-element.49), channel_id=1, source_target_pairs={{2,4},{6,8},{10,12},{14,16},{18,20},{22,24},{26,28},{30,32},{34,36... | collective-permute-start | bytes 393224 | tf_op jit(solution)/shard_map/ppermute | solution.py:383
  57.2 3.8 %collective-permute-start.7 = (bf16[136,128]{1,0:T(8,128)(2,1)S(1)}, bf16[136,128]{1,0:T(8,128)(2,1)S(1)}, u32[]{:S(2)}, u32[]{:S(2)}) collective-permute-start(bf16[136,128]{1,0:T(8,128)(2,1)S(1)} %group_sum.1.own), channel_id=1, source_target_pairs={{0,4},{8,12},{4,0},{12,8},{1,5},{9,13},{5,1},{13,9},{2,6},{10,14},... | collective-permute-start | bytes 104456 | tf_op jit(solution)/shard_map/ppermute | solution.py:383
  61.0 5.4 %collective-permute-start.8 = (bf16[136,128]{1,0:T(8,128)(2,1)S(1)}, bf16[136,128]{1,0:T(8,128)(2,1)S(1)}, u32[]{:S(2)}, u32[]{:S(2)}) collective-permute-start(bf16[136,128]{1,0:T(8,128)(2,1)S(1)} %pair_sum.1.own), channel_id=1, source_target_pairs={{0,12},{4,8},{12,0},{8,4},{1,13},{5,9},{13,1},{9,5},{2,14},{6,10},... | collective-permute-start | bytes 104456 | tf_op jit(solution)/shard_map/ppermute | solution.py:383
  64.2 30.5 %copy-start = (f32[128,512]{1,0:T(8,128)}, f32[128,512]{1,0:T(8,128)S(1)}, u32[]{:S(2)}) copy-start(f32[128,512]{1,0:T(8,128)S(1)} %convert_add_fusion.after) | copy-start | bytes 786436
  87.5 5.3 %collective-permute-start.9 = (bf16[32,128,128]{2,1,0:T(8,128)(2,1)S(1)}, bf16[32,128,128]{2,1,0:T(8,128)(2,1)S(1)}, u32[]{:S(2)}, u32[]{:S(2)}) collective-permute-start(bf16[32,128,128]{2,1,0:T(8,128)(2,1)S(1)} %all_to_all.10.shares), channel_id=1, source_target_pairs={{0,1},{1,0},{2,3},{3,2},{4,5},{5,4},{6,7},{7,6},{8,9},{9,8},{10,11... | collective-permute-start | bytes 3145736 | tf_op jit(solution)/shard_map/ppermute | solution.py:383

commit v8 on v6

--- a/solution.py
+++ b/solution.py
@@ -12,6 +12,7 @@
 SHARDS = ("band", "hi", "lo")
 GROUP = ("band", "lo")
 TILE = 256
+EDGE_TILE = 1024
 LANES = 128
 MIB = 1 << 20
 
@@ -160,14 +161,14 @@
         copy.wait()
 
 
-def live_receivers(scalars, receivers, start, rows_mesh):
-    row = receivers[:, pl.ds(start, TILE)] - scalars[1]
+def live_receivers(scalars, receivers, start, tile, rows_mesh):
+    row = receivers[:, pl.ds(start, tile)] - scalars[1]
     row = jnp.where(
         row < rows_mesh,
         row + scalars[4],
         jnp.where(row >= 2 * rows_mesh, row - scalars[4], row),
     )
-    slot = start + lax.broadcasted_iota(jnp.int32, (1, TILE), 1)
+    slot = start + lax.broadcasted_iota(jnp.int32, (1, tile), 1)
     return jnp.where(slot < scalars[2], row, -1)
 
 
@@ -193,9 +194,9 @@
     width = w_second.shape[0]
     rows_mesh = stack_own.shape[0] // 2
     gain_sum = jnp.zeros((1, width), jnp.float32)
-    for start in range(0, edge.shape[0], TILE):
-        rows = pl.ds(start, TILE)
-        table = picks(live_receivers(scalars, receivers, start, rows_mesh), 3 * rows_mesh)
+    for start in range(0, edge.shape[0], EDGE_TILE):
+        rows = pl.ds(start, EDGE_TILE)
+        table = picks(live_receivers(scalars, receivers, start, EDGE_TILE, rows_mesh), 3 * rows_mesh)
 
         def picked_rows(first):
             part = pl.ds(first, rows_mesh)
@@ -280,9 +281,9 @@
     packed[...] = jnp.concatenate([total[:data], gain], axis=0).astype(jnp.bfloat16)
 
 
-def whole_sum_kernel(factor, own, ahead, across, behind, after, copies, gain_grad):
-    own, ahead, across, behind = [part[...].astype(jnp.float32) for part in (own, ahead, across, behind)]
-    total = ((own + across) + (ahead + behind)) * factor
+def whole_sum_kernel(factor, own, near, across, far, after, copies, gain_grad):
+    own, near, across, far = [part[...].astype(jnp.float32) for part in (own, near, across, far)]
+    total = ((own + across) + (near + far)) * factor
     data = copies.shape[1]
     gain_grad[...] = jnp.broadcast_to(gain_of(total[data:]), gain_grad.shape)
     share = total[:data].astype(jnp.bfloat16)
@@ -317,7 +318,7 @@
         rows = pl.ds(start, TILE)
         terms = grad_pre[rows, :]
         near = near + dot(
-            spreads(live_receivers(scalars, receivers, start, rows_mesh), 3 * rows_mesh), terms
+            spreads(live_receivers(scalars, receivers, start, TILE, rows_mesh), 3 * rows_mesh), terms
         )
         here = here + dot(spreads(senders[:, rows] - scalars[0], rows_grid), terms)
         edge_grad[rows, :] = dot(terms, w_first[0:width, :], 1, 1).astype(jnp.bfloat16)
@@ -372,14 +373,17 @@
     put_half(scalars, True, shares, first, second, wide, sems)
 
 
+def swap_pairs(value, axis, pairs):
+    return lax.ppermute(value, axis, pairs + [(d, s) for s, d in pairs])
+
+
 def exchanged(value, turn):
     count = lax.axis_size(SHARDS)
-    pairs = [(s, s + 1) for s in range(turn, count - 1, 2)]
-    return lax.ppermute(value, SHARDS, pairs + [(d, s) for s, d in pairs])
+    return swap_pairs(value, SHARDS, [(s, s + 1) for s in range(turn, count - 1, 2)])
 
 
 def swapped(value):
-    return lax.ppermute(value, "rep", [(0, 1), (1, 0)])
+    return swap_pairs(value, "rep", [(0, 1)])
 
 
 def per_device(
@@ -517,8 +521,8 @@
         0,
     )
     turns = [
-        lax.ppermute(packed, "hi", [(i, (i + turn) % groups) for i in range(groups)])
-        for turn in (1, 2, 3)
+        swap_pairs(packed, "hi", pairs)
+        for pairs in ([(0, 1), (2, 3)], [(0, 2), (1, 3)], [(0, 3), (1, 2)])
     ]
     copies, gain_grad = call(
         functools.partial(whole_sum_kernel, factor),

time: 95.8 us -> 94.7 us (0.989)
  Pallas kernels: 23.6 us -> 22.5 us
    pallas_call x8, Pallas kernels: 19.7 us -> 18.7 us  [call(): pl.pallas_call(kernel, out_shape=outs, in_specs=specs, out_specs=[in_vmem...]
where the time goes in v8:
time: 94.7 us; the launch traced here: 94.3 us
  starting transfers between devices  30.2 us (32%)
  Pallas kernels  22.5 us (24%)
  blocking collectives  21.2 us (22%)
  waiting for transfers between devices  16.7 us (18%)
  local copies, waits for them, and re-layouts  2.09 us (2%)
  between operations  1.6 us (2%)
    all_to_all x1, blocking collectives, per_device(): total = lax.all_to_all(copies, GROUP, 0, 0)  21.2 us
    ppermute x9, starting transfers between devices, swap_pairs(): return lax.ppermute(value, axis, pairs + [(d, s) for s, d in pairs])  19 us
    pallas_call x8, Pallas kernels, call(): pl.pallas_call(kernel, out_shape=outs, in_specs=specs, out_specs=[in_vmem...  18.7 us
    all_to_all x1, starting transfers between devices, per_device(): shares = lax.all_to_all(packed, GROUP, 0, 0)  11.1 us
    all_to_all x1, waiting for transfers between devices, per_device(): shares = lax.all_to_all(packed, GROUP, 0, 0)  11 us
    ppermute x9, waiting for transfers between devices, swap_pairs(): return lax.ppermute(value, axis, pairs + [(d, s) for s, d in pairs])  5.71 us
    pallas_call x1, Pallas kernels, per_device(): halves(other_half_kernel, in_specs=[in_smem(), in_vmem()] + [in_hbm()] *...  1.94 us
    pallas_call x1, Pallas kernels, per_device(): halves(own_half_kernel, in_specs=[in_smem(), in_vmem()], name='own_half')  1.93 us
  transfers between devices with their start and end apart: 10, of which 4 were waited for; matrix products, arithmetic and copies ran while one was open for 1% of the time, Pallas kernels for 13%

profile of v8, /device:TPU:1, one launch (start us, length us, event | category | flops | bytes accessed | tf_op | source)
XLA Modules:
  0.0 94.3 jit_solution(16009626860107805011)
XLA Ops:
  0.6 1.0 %stack.21.stack_own = bf16[256,512]{1,0:T(8,128)(2,1)S(1)} custom-call(bf16[128,512]{1,0:T(8,128)(2,1)} %bitcast.21, bf16[128,512]{1,0:T(8,128)(2,1)} %bitcast.22), custom_call_target="tpu_custom_call" | custom-call | bytes 524288 | tf_op jit(solution)/shard_map/stack/pallas_call | solution.py:92
  1.6 0.7 collective-permute-start.1
  2.3 5.4 %collective-permute-start = (bf16[256,512]{1,0:T(8,128)(2,1)S(1)}, bf16[256,512]{1,0:T(8,128)(2,1)S(1)}, u32[]{:S(2)}, u32[]{:S(2)}) collective-permute-start(bf16[256,512]{1,0:T(8,128)(2,1)S(1)} %stack.21.stack_own), channel_id=1, source_target_pairs={{0,2},{4,6},{8,10},{12,14},{16,18},{20,22},{24,26},{28,30},{32,34}... | collective-permute-start | bytes 786440 | tf_op jit(solution)/shard_map/ppermute | solution.py:377
  8.5 4.5 %near.1 = (f32[1024,512]{1,0:T(8,128)S(1)}, bf16[1024,512]{1,0:T(8,128)(2,1)S(1)}, bf16[1024,512]{1,0:T(8,128)(2,1)S(1)}, bf16[1536,512]{1,0:T(8,128)(2,1)S(1)}, bf16[512,512]{1,0:T(8,128)(2,1)S(1)}) custom-call(s32[5]{0:T(128)S(1)} %stack.20.scalars, s32[1,1024]{1,0:T(1,128)} %bitcast.16, bf16[512,512]{1,0:T(8,128)(2,1)} %bitcast.25, ...), custom_call_target="tpu_custom_call" | custom-call | flops 1610612736 | bytes 9965588 | tf_op jit(solution)/shard_map/near/pallas_call | solution.py:92
  13.0 0.4 collective-permute-done.stack_first
  13.5 5.9 %edges.1 = (bf16[1040,512]{1,0:T(8,128)(2,1)S(1)}, f32[8,512]{1,0:T(8,128)S(1)}, bf16[1024,512]{1,0:T(8,128)(2,1)S(1)}, bf16[1024,512]{1,0:T(8,128)(2,1)S(1)}, b...) custom-call(s32[5]{0:T(128)S(1)} %stack.20.scalars, s32[1,1024]{1,0:T(1,128)S(1)} %bitcast.18, ...), custom_call_target="tpu_custom_call" | custom-call | flops 3758096384 | bytes 12359700 | tf_op jit(solution)/shard_map/edges/pallas_call | solution.py:92
  19.4 1.6 %collective-permute-start.2 = (bf16[1040,512]{1,0:T(8,128)(2,1)S(1)}, bf16[1040,512]{1,0:T(8,128)(2,1)S(1)}, u32[]{:S(2)}, u32[]{:S(2)}) collective-permute-start(bf16[1040,512]{1,0:T(8,128)(2,1)S(1)} %get-tuple-element.39), channel_id=1, source_target_pairs={{0,1},{1,0},{2,3},{3,2},{4,5},{5,4},{6,7},{7,6},{8,9},{9,8},{10,11... | collective-permute-start | bytes 3194888 | tf_op jit(solution)/shard_map/ppermute | solution.py:377
  21.0 1.8 %kept.1 = f32[1024,512]{1,0:T(8,128)S(1)} custom-call(s32[5]{0:T(128)S(1)} %stack.20.scalars, bf16[1024,512]{1,0:T(8,128)(2,1)S(1)} %get-tuple-element.32.edge, bf16[1024,512]{1,0:T(8,128)(2,1)S(1)} %get-tuple-element.31.grid_picked, bf16[1024,512]{1,0:T(8,128)(2,1)S(1)} %get-tuple-element.36.mesh_picked, bf16[1024,512]{1,0:T(8,128)(2,1)S(1)} %get-tuple-element.37.hidden, ...), custom_call_target="tpu_custom_call" | custom-call | flops 1073741824 | bytes 8388628 | tf_op jit(solution)/shard_map/kept/pallas_call | solution.py:92
  22.8 0.5 collective-permute-done.2.got
  23.3 1.2 %pack.1 = (bf16[32,136,128]{2,1,0:T(8,128)(2,1)}, f32[8,128]{1,0:T(8,128)S(1)}) custom-call(f32[1024,512]{1,0:T(8,128)S(1)} %kept.1, bf16[1040,512]{1,0:T(8,128)(2,1)S(1)} %collective-permute-done.2.got, f32[8,512]{1,0:T(8,128)S(1)} %get-tuple-element.40.gain_term), custom_call_target="tpu_custom_call" | custom-call | bytes 4296704 | tf_op jit(solution)/shard_map/pack/pallas_call | solution.py:92
  24.5 11.1 %all-to-all-start = ((bf16[32,136,128]{2,1,0:T(8,128)(2,1)}), bf16[32,136,128]{2,1,0:T(8,128)(2,1)S(1)}, u32[]{:S(2)}, u32[]{:S(2)}) async-start(bf16[32,136,128]{2,1,0:T(8,128)(2,1)} %get-tuple-element.47), calls=%async_computation | async-start | bytes 2228224 | tf_op jit(solution)/shard_map/all_to_all | solution.py:514
  35.7 1.4 %copy-done.5 = bf16[1536,512]{1,0:T(8,128)(2,1)S(1)} copy-done((bf16[1536,512]{1,0:T(8,128)(2,1)S(1)}, bf16[1536,512]{1,0:T(8,128)(2,1)}, u32[]{:S(2)}) %copy-start.5) | copy-done | bytes 1572888
  37.1 4.0 %nodes.1 = (bf16[1024,512]{1,0:T(8,128)(2,1)}, bf16[512,512]{1,0:T(8,128)(2,1)}, f32[128,512]{1,0:T(8,128)S(1)}, bf16[128,512]{1,0:T(8,128)(2,1)S(1)}, bf16[128,512]{1,0:T(8,128)(2,1)S(1)}) custom-call(s32[5]{0:T(128)S(1)} %stack.20.scalars, s32[1,1024]{1,0:T(1,128)S(1)} %bitcast.17, s32[1,1024]{1,0:T(1,128)S(1)} %bitcast.19, ...), custom_call_target="tpu_custom_call" | custom-call | flops 2147483648 | bytes 4730900 | tf_op jit(solution)/shard_map/nodes/pallas_call | solution.py:92
  41.0 1.1 %collective-permute-start.3 = (bf16[128,512]{1,0:T(8,128)(2,1)S(1)}, bf16[128,512]{1,0:T(8,128)(2,1)S(1)}, u32[]{:S(2)}, u32[]{:S(2)}) collective-permute-start(bf16[128,512]{1,0:T(8,128)(2,1)S(1)} %get-tuple-element.44), channel_id=1, source_target_pairs={{0,2},{4,6},{8,10},{12,14},{16,18},{20,22},{24,26},{28,30},{32,34}... | collective-permute-start | bytes 393224 | tf_op jit(solution)/shard_map/ppermute | solution.py:377
  42.1 0.7 collective-permute-start.4
  42.8 11.0 %all-to-all-done.shares = bf16[32,136,128]{2,1,0:T(8,128)(2,1)S(1)} async-done(((bf16[32,136,128]{2,1,0:T(8,128)(2,1)}), bf16[32,136,128]{2,1,0:T(8,128)(2,1)S(1)}, u32[]{:S(2)}, u32[]{:S(2)}) %all-to-all-start) | async-done | bytes 1114144 | tf_op jit(solution)/shard_map/all_to_all | solution.py:514
  53.9 4.4 %collective-permute-start.7 = (bf16[136,128]{1,0:T(8,128)(2,1)S(1)}, bf16[136,128]{1,0:T(8,128)(2,1)S(1)}, u32[]{:S(2)}, u32[]{:S(2)}) collective-permute-start(bf16[136,128]{1,0:T(8,128)(2,1)S(1)} %group_sum.1.own), channel_id=1, source_target_pairs={{0,12},{4,8},{12,0},{8,4},{1,13},{5,9},{13,1},{9,5},{2,14},{6,10},... | collective-permute-start | bytes 104456 | tf_op jit(solution)/shard_map/ppermute | solution.py:377
  58.3 2.1 %collective-permute-start.5 = (bf16[136,128]{1,0:T(8,128)(2,1)S(1)}, bf16[136,128]{1,0:T(8,128)(2,1)S(1)}, u32[]{:S(2)}, u32[]{:S(2)}) collective-permute-start(bf16[136,128]{1,0:T(8,128)(2,1)S(1)} %group_sum.1.own), channel_id=1, source_target_pairs={{0,4},{8,12},{4,0},{12,8},{1,5},{9,13},{5,1},{13,9},{2,6},{10,14},... | collective-permute-start | bytes 104456 | tf_op jit(solution)/shard_map/ppermute | solution.py:377
  60.5 4.8 %collective-permute-done.6.across = bf16[136,128]{1,0:T(8,128)(2,1)S(1)} collective-permute-done((bf16[136,128]{1,0:T(8,128)(2,1)S(1)}, bf16[136,128]{1,0:T(8,128)(2,1)S(1)}, u32[]{:S(2)}, u32[]{:S(2)}) %collective-permute-start.6) | collective-permute-done | bytes 34848 | tf_op jit(solution)/shard_map/ppermute | solution.py:377
  65.4 21.2 %all_to_all.10.shares = bf16[32,128,128]{2,1,0:T(8,128)(2,1)S(1)} all-to-all(bf16[32,128,128]{2,1,0:T(8,128)(2,1)S(1)} %get-tuple-element.48), channel_id=1, replica_groups=mesh['band'=16,'hi'=4,'lo'=2,'rep'=2] {'band','lo'}, dimensions={0} | all-to-all | bytes 2097152 | tf_op jit(solution)/shard_map/all_to_all | solution.py:535
  86.7 3.0 %collective-permute-start.8 = (bf16[32,128,128]{2,1,0:T(8,128)(2,1)S(1)}, bf16[32,128,128]{2,1,0:T(8,128)(2,1)S(1)}, u32[]{:S(2)}, u32[]{:S(2)}) collective-permute-start(bf16[32,128,128]{2,1,0:T(8,128)(2,1)S(1)} %all_to_all.10.shares), channel_id=1, source_target_pairs={{0,1},{1,0},{2,3},{3,2},{4,5},{5,4},{6,7},{7,6},{8,9},{9,8},{10,11... | collective-permute-start | bytes 3145736 | tf_op jit(solution)/shard_map/ppermute | solution.py:377
  89.7 0.6 slice.3
  90.3 1.9 %own_half.1 = (f32[1536,512]{1,0:T(8,128)}, f32[512,512]{1,0:T(8,128)}) custom-call(s32[5]{0:T(128)S(1)} %stack.20.scalars, bf16[32,128,128]{2,1,0:T(8,128)(2,1)S(1)} %all_to_all.10.shares), custom_call_target="tpu_custom_call" | custom-call | bytes 6291456 | tf_op jit(solution)/shard_map/own_half/pallas_call | solution.py:549
  92.2 1.9 %other_half.1 = (f32[1536,512]{1,0:T(8,128)}, f32[512,512]{1,0:T(8,128)}) custom-call(s32[5]{0:T(128)S(1)} %stack.20.scalars, bf16[32,128,128]{2,1,0:T(8,128)(2,1)S(1)} %collective-permute-done.8.shares, f32[1536,512]{1,0:T(8,128)} %get-tuple-element.49.first_in, f32[512,512]{1,0:T(8,128)} %get-tuple-element.50.second_in), custom_call_target="tpu_custom_call", output_to_operand_aliasing={{0}: (2, {}), {1}: (3, {})} | custom-call | bytes 6291456 | tf_op jit(solution)/shard_map/other_half/pallas_call | solution.py:550
  (22 shorter events, 0.5 us)
Async XLA Ops:
  1.6 11.4 %collective-permute-start.1 = (bf16[256,512]{1,0:T(8,128)(2,1)S(1)}, bf16[256,512]{1,0:T(8,128)(2,1)S(1)}, u32[]{:S(2)}, u32[]{:S(2)}) collective-permute-start(bf16[256,512]{1,0:T(8,128)(2,1)S(1)} %stack.21.stack_own), channel_id=1, source_target_pairs={{2,4},{6,8},{10,12},{14,16},{18,20},{22,24},{26,28},{30,32},{34,36... | collective-permute-start | bytes 786440 | tf_op jit(solution)/shard_map/ppermute | solution.py:377
  2.3 11.1 %collective-permute-start = (bf16[256,512]{1,0:T(8,128)(2,1)S(1)}, bf16[256,512]{1,0:T(8,128)(2,1)S(1)}, u32[]{:S(2)}, u32[]{:S(2)}) collective-permute-start(bf16[256,512]{1,0:T(8,128)(2,1)S(1)} %stack.21.stack_own), channel_id=1, source_target_pairs={{0,2},{4,6},{8,10},{12,14},{16,18},{20,22},{24,26},{28,30},{32,34}... | collective-permute-start | bytes 786440 | tf_op jit(solution)/shard_map/ppermute | solution.py:377
  8.5 5.0 %copy-start.2 = (s32[1024]{0:T(1024)S(1)}, s32[1024]{0:T(1024)}, u32[]{:S(2)}) copy-start(s32[1024]{0:T(1024)} %param.18) | copy-start | bytes 12292
  8.5 5.0 %copy-start.3 = (f32[512]{0:T(512)S(1)}, f32[512]{0:T(512)}, u32[]{:S(2)}) copy-start(f32[512]{0:T(512)} %param.16) | copy-start | bytes 6148
  13.0 6.4 %copy-start.4 = (bf16[1536,512]{1,0:T(8,128)(2,1)}, bf16[1536,512]{1,0:T(8,128)(2,1)S(1)}, u32[]{:S(2)}) copy-start(bf16[1536,512]{1,0:T(8,128)(2,1)S(1)} %get-tuple-element.33.w_first) | copy-start | bytes 4718596
  19.4 3.9 %collective-permute-start.2 = (bf16[1040,512]{1,0:T(8,128)(2,1)S(1)}, bf16[1040,512]{1,0:T(8,128)(2,1)S(1)}, u32[]{:S(2)}, u32[]{:S(2)}) collective-permute-start(bf16[1040,512]{1,0:T(8,128)(2,1)S(1)} %get-tuple-element.39), channel_id=1, source_target_pairs={{0,1},{1,0},{2,3},{3,2},{4,5},{5,4},{6,7},{7,6},{8,9},{9,8},{10,11... | collective-permute-start | bytes 3194888 | tf_op jit(solution)/shard_map/ppermute | solution.py:377
  24.5 11.1 %copy-start.1 = (s32[1024]{0:T(1024)S(1)}, s32[1024]{0:T(1024)}, u32[]{:S(2)}) copy-start(s32[1024]{0:T(1024)} %param.17) | copy-start | bytes 12292
  24.5 29.2 %all-to-all-start = ((bf16[32,136,128]{2,1,0:T(8,128)(2,1)}), bf16[32,136,128]{2,1,0:T(8,128)(2,1)S(1)}, u32[]{:S(2)}, u32[]{:S(2)}) async-start(bf16[32,136,128]{2,1,0:T(8,128)(2,1)} %get-tuple-element.47), calls=%async_computation | async-start | bytes 2228224 | tf_op jit(solution)/shard_map/all_to_all | solution.py:514
  35.7 1.4 %copy-start.5 = (bf16[1536,512]{1,0:T(8,128)(2,1)S(1)}, bf16[1536,512]{1,0:T(8,128)(2,1)}, u32[]{:S(2)}) copy-start(bf16[1536,512]{1,0:T(8,128)(2,1)} %copy-done.4) | copy-start | bytes 4718596
  41.0 19.4 %collective-permute-start.3 = (bf16[128,512]{1,0:T(8,128)(2,1)S(1)}, bf16[128,512]{1,0:T(8,128)(2,1)S(1)}, u32[]{:S(2)}, u32[]{:S(2)}) collective-permute-start(bf16[128,512]{1,0:T(8,128)(2,1)S(1)} %get-tuple-element.44), channel_id=1, source_target_pairs={{0,2},{4,6},{8,10},{12,14},{16,18},{20,22},{24,26},{28,30},{32,34}... | collective-permute-start | bytes 393224 | tf_op jit(solution)/shard_map/ppermute | solution.py:377
  42.1 18.4 %collective-permute-start.4 = (bf16[128,512]{1,0:T(8,128)(2,1)S(1)}, bf16[128,512]{1,0:T(8,128)(2,1)S(1)}, u32[]{:S(2)}, u32[]{:S(2)}) collective-permute-start(bf16[128,512]{1,0:T(8,128)(2,1)S(1)} %get-tuple-element.45), channel_id=1, source_target_pairs={{2,4},{6,8},{10,12},{14,16},{18,20},{22,24},{26,28},{30,32},{34,36... | collective-permute-start | bytes 393224 | tf_op jit(solution)/shard_map/ppermute | solution.py:377
  53.9 6.6 %collective-permute-start.7 = (bf16[136,128]{1,0:T(8,128)(2,1)S(1)}, bf16[136,128]{1,0:T(8,128)(2,1)S(1)}, u32[]{:S(2)}, u32[]{:S(2)}) collective-permute-start(bf16[136,128]{1,0:T(8,128)(2,1)S(1)} %group_sum.1.own), channel_id=1, source_target_pairs={{0,12},{4,8},{12,0},{8,4},{1,13},{5,9},{13,1},{9,5},{2,14},{6,10},... | collective-permute-start | bytes 104456 | tf_op jit(solution)/shard_map/ppermute | solution.py:377
  58.3 7.1 %collective-permute-start.6 = (bf16[136,128]{1,0:T(8,128)(2,1)S(1)}, bf16[136,128]{1,0:T(8,128)(2,1)S(1)}, u32[]{:S(2)}, u32[]{:S(2)}) collective-permute-start(bf16[136,128]{1,0:T(8,128)(2,1)S(1)} %group_sum.1.own), channel_id=1, source_target_pairs={{0,8},{4,12},{8,0},{12,4},{1,9},{5,13},{9,1},{13,5},{2,10},{6,14},... | collective-permute-start | bytes 104456 | tf_op jit(solution)/shard_map/ppermute | solution.py:377
  58.3 7.0 %collective-permute-start.5 = (bf16[136,128]{1,0:T(8,128)(2,1)S(1)}, bf16[136,128]{1,0:T(8,128)(2,1)S(1)}, u32[]{:S(2)}, u32[]{:S(2)}) collective-permute-start(bf16[136,128]{1,0:T(8,128)(2,1)S(1)} %group_sum.1.own), channel_id=1, source_target_pairs={{0,4},{8,12},{4,0},{12,8},{1,5},{9,13},{5,1},{13,9},{2,6},{10,14},... | collective-permute-start | bytes 104456 | tf_op jit(solution)/shard_map/ppermute | solution.py:377
  60.5 31.7 %copy-start = (f32[128,512]{1,0:T(8,128)}, f32[128,512]{1,0:T(8,128)S(1)}, u32[]{:S(2)}) copy-start(f32[128,512]{1,0:T(8,128)S(1)} %convert_add_fusion.after) | copy-start | bytes 786436
  86.7 5.6 %collective-permute-start.8 = (bf16[32,128,128]{2,1,0:T(8,128)(2,1)S(1)}, bf16[32,128,128]{2,1,0:T(8,128)(2,1)S(1)}, u32[]{:S(2)}, u32[]{:S(2)}) collective-permute-start(bf16[32,128,128]{2,1,0:T(8,128)(2,1)S(1)} %all_to_all.10.shares), channel_id=1, source_target_pairs={{0,1},{1,0},{2,3},{3,2},{4,5},{5,4},{6,7},{7,6},{8,9},{9,8},{10,11... | collective-permute-start | bytes 3145736 | tf_op jit(solution)/shard_map/ppermute | solution.py:377

commit v9 on v8

--- a/solution.py
+++ b/solution.py
@@ -9,8 +9,9 @@
 from jax.sharding import PartitionSpec as P
 
 NORM_EPS = 1e-05
-SHARDS = ("band", "hi", "lo")
-GROUP = ("band", "lo")
+SHARDS = ("x_far", "x_near", "y_far", "y_near", "z_far", "z_near")
+GROUP = ("x_near", "y_near", "z_near")
+FAR = ("x_far", "y_far", "z_far")
 TILE = 256
 EDGE_TILE = 1024
 LANES = 128
@@ -276,19 +277,29 @@
     total = shares[0].astype(jnp.float32)
     for place in range(1, shares.shape[0]):
         total = total + shares[place].astype(jnp.float32)
-    data = total.shape[0] - 8
-    gain = gain_rows(gain_of(total[data:]), LANES)
-    packed[...] = jnp.concatenate([total[:data], gain], axis=0).astype(jnp.bfloat16)
-
-
-def whole_sum_kernel(factor, own, near, across, far, after, copies, gain_grad):
-    own, near, across, far = [part[...].astype(jnp.float32) for part in (own, near, across, far)]
-    total = ((own + across) + (near + far)) * factor
+    count = packed.shape[0]
+    rows = packed.shape[1] - 8
+    gain = gain_rows(gain_of(total[rows * count :]), LANES)
+    for place in range(count):
+        data = total[place * rows : (place + 1) * rows]
+        packed[place] = jnp.concatenate([data, gain], axis=0).astype(jnp.bfloat16)
+
+
+def whole_sum_kernel(factor, pieces, copies, gain_grad):
+    total = pieces[0].astype(jnp.float32)
+    for place in range(1, pieces.shape[0]):
+        total = total + pieces[place].astype(jnp.float32)
+    total = total * factor
     data = copies.shape[1]
     gain_grad[...] = jnp.broadcast_to(gain_of(total[data:]), gain_grad.shape)
-    share = total[:data].astype(jnp.bfloat16)
+    piece = total[:data].astype(jnp.bfloat16)
     for place in range(copies.shape[0]):
-        copies[place] = share
+        copies[place] = piece
+
+
+def copies_kernel(share, after, copies):
+    for place in range(copies.shape[0]):
+        copies[place] = share[...]
 
 
 def node_kernel(
@@ -402,7 +413,7 @@
     rows_grid = grid_latent.shape[1]
     rows_mesh = mesh_latent.shape[1]
     slots = senders.shape[0]
-    group, groups = lax.axis_size(GROUP), lax.axis_size("hi")
+    group, groups = lax.axis_size(GROUP), lax.axis_size(FAR)
     factor = 1.0 / math.sqrt(slots * group * groups * lax.axis_size("rep"))
     shard = lax.axis_index(SHARDS)
     scalars = jnp.stack(
@@ -516,20 +527,26 @@
         group_sum_kernel,
         "group_sum",
         [in_vmem(), anywhere()],
-        [matrix((part + extra, LANES))],
+        [matrix((groups, part // groups + extra, LANES))],
         (shares, mesh_own),
         0,
     )
-    turns = [
-        swap_pairs(packed, "hi", pairs)
-        for pairs in ([(0, 1), (2, 3)], [(0, 2), (1, 3)], [(0, 3), (1, 2)])
-    ]
+    pieces = lax.all_to_all(packed, FAR, 0, 0)
     copies, gain_grad = call(
         functools.partial(whole_sum_kernel, factor),
         "whole_sum",
-        [in_vmem()] * 4 + [anywhere()],
-        [matrix((group, part, LANES)), floats((8, width))],
-        (packed, *turns, mesh_grad),
+        [in_vmem()],
+        [matrix((groups, part // groups, LANES)), floats((8, width))],
+        (pieces,),
+        0,
+    )
+    share = lax.all_to_all(copies, FAR, 0, 0).reshape(part, LANES)
+    (copies,) = call(
+        copies_kernel,
+        "copies",
+        [in_vmem(), anywhere()],
+        [matrix((group, part, LANES))],
+        (share, mesh_grad),
         0,
     )
     total = lax.all_to_all(copies, GROUP, 0, 0)
@@ -565,8 +582,9 @@
 
 def solution(mesh):
     bands, meshes, cores = mesh.devices.shape
+    side = math.isqrt(bands) // 2
     mesh = jax.sharding.Mesh(
-        mesh.devices.reshape(bands, 4, meshes // 4, cores), ("band", "hi", "lo", "rep")
+        mesh.devices.reshape(side, 2, side, 2, meshes // 2, 2, cores), SHARDS + ("rep",)
     )
     in_specs = (
         P("rep", SHARDS, None),

time: 94.7 us -> 112 us (1.18)
  waiting for transfers between devices: 16.7 us -> 33.4 us
  blocking collectives: 21.2 us -> 13.2 us
  starting transfers between devices: 30.2 us -> 37.1 us
  Pallas kernels: 22.5 us -> 23.9 us
    all_to_all x0 -> x2, waiting for transfers between devices: none -> 22.9 us  [the longest x1 12.5 us: per_device(): share = lax.all_to_all(copies, FAR, 0, 0).reshape(part, LANES)]
    all_to_all x0 -> x2, starting transfers between devices: none -> 12.4 us  [the longest x1 8.86 us: per_device(): pieces = lax.all_to_all(packed, FAR, 0, 0)]
    all_to_all x1, blocking collectives: 21.2 us -> 13.2 us  [per_device(): total = lax.all_to_all(copies, GROUP, 0, 0)]
    ppermute x9 -> x6, waiting for transfers between devices: 5.71 us -> 0.91 us  [swap_pairs(): return lax.ppermute(value, axis, pairs + [(d, s) for s, d in pairs])]
    ppermute x9 -> x6, starting transfers between devices: 19 us -> 16 us  [swap_pairs(): return lax.ppermute(value, axis, pairs + [(d, s) for s, d in pairs])]
    all_to_all x1, starting transfers between devices: 11.1 us -> 8.81 us  [per_device(): shares = lax.all_to_all(packed, GROUP, 0, 0)]
    all_to_all x1, waiting for transfers between devices: 11 us -> 9.6 us  [per_device(): shares = lax.all_to_all(packed, GROUP, 0, 0)]
    pallas_call x8 -> x9, Pallas kernels: 18.7 us -> 20 us  [call(): pl.pallas_call(kernel, out_shape=outs, in_specs=specs, out_specs=[in_vmem...]
  transfers between devices with their start and end apart: 10 -> 9, of which waited for: 4 -> 5; matrix products, arithmetic and copies ran while one was open for 1% -> 1% of each run, Pallas kernels for 13% -> 12%
where the time goes in v9:
time: 112 us; the launch traced here: 111 us
  starting transfers between devices  37.1 us (33%)
  waiting for transfers between devices  33.4 us (30%)
  Pallas kernels  23.9 us (21%)
  blocking collectives  13.2 us (12%)
  local copies, waits for them, and re-layouts  2.09 us (2%)
  between operations  1.61 us (1%)
    pallas_call x9, Pallas kernels, call(): pl.pallas_call(kernel, out_shape=outs, in_specs=specs, out_specs=[in_vmem...  20 us
    ppermute x6, starting transfers between devices, swap_pairs(): return lax.ppermute(value, axis, pairs + [(d, s) for s, d in pairs])  16 us
    all_to_all x1, blocking collectives, per_device(): total = lax.all_to_all(copies, GROUP, 0, 0)  13.2 us
    all_to_all x1, waiting for transfers between devices, per_device(): share = lax.all_to_all(copies, FAR, 0, 0).reshape(part, LANES)  12.5 us
    all_to_all x1, waiting for transfers between devices, per_device(): pieces = lax.all_to_all(packed, FAR, 0, 0)  10.4 us
    all_to_all x1, waiting for transfers between devices, per_device(): shares = lax.all_to_all(packed, GROUP, 0, 0)  9.6 us
    all_to_all x1, starting transfers between devices, per_device(): pieces = lax.all_to_all(packed, FAR, 0, 0)  8.86 us
    all_to_all x1, starting transfers between devices, per_device(): shares = lax.all_to_all(packed, GROUP, 0, 0)  8.81 us
  transfers between devices with their start and end apart: 9, of which 5 were waited for; matrix products, arithmetic and copies ran while one was open for 1% of the time, Pallas kernels for 12%

profile of v9, /device:TPU:1, one launch (start us, length us, event | category | flops | bytes accessed | tf_op | source)
XLA Modules:
  0.0 111.4 jit_solution(9539457513663869100)
XLA Ops:
  0.6 1.0 stack.21.stack_own
  1.6 0.7 collective-permute-start.1
  2.3 5.4 %collective-permute-start = (bf16[256,512]{1,0:T(8,128)(2,1)S(1)}, bf16[256,512]{1,0:T(8,128)(2,1)S(1)}, u32[]{:S(2)}, u32[]{:S(2)}) collective-permute-start(bf16[256,512]{1,0:T(8,128)(2,1)S(1)} %stack.21.stack_own), channel_id=1, source_target_pairs={{0,2},{4,6},{8,10},{12,14},{16,18},{20,22},{24,26},{28,30},{32,34}... | collective-permute-start | bytes 786440 | tf_op jit(solution)/shard_map/ppermute | solution.py:388
  8.5 4.5 %near.1 = (f32[1024,512]{1,0:T(8,128)S(1)}, bf16[1024,512]{1,0:T(8,128)(2,1)S(1)}, bf16[1024,512]{1,0:T(8,128)(2,1)S(1)}, bf16[1536,512]{1,0:T(8,128)(2,1)S(1)}, bf16[512,512]{1,0:T(8,128)(2,1)S(1)}) custom-call(s32[5]{0:T(128)S(1)} %stack.20.scalars, s32[1,1024]{1,0:T(1,128)} %bitcast.18, bf16[512,512]{1,0:T(8,128)(2,1)} %bitcast.27, ...), custom_call_target="tpu_custom_call" | custom-call | flops 1610612736 | bytes 9965588 | tf_op jit(solution)/shard_map/near/pallas_call | solution.py:93
  13.5 5.9 %edges.1 = (bf16[1040,512]{1,0:T(8,128)(2,1)S(1)}, f32[8,512]{1,0:T(8,128)S(1)}, bf16[1024,512]{1,0:T(8,128)(2,1)S(1)}, bf16[1024,512]{1,0:T(8,128)(2,1)S(1)}, b...) custom-call(s32[5]{0:T(128)S(1)} %stack.20.scalars, s32[1,1024]{1,0:T(1,128)S(1)} %bitcast.20, ...), custom_call_target="tpu_custom_call" | custom-call | flops 3758096384 | bytes 12359700 | tf_op jit(solution)/shard_map/edges/pallas_call | solution.py:93
  19.4 1.6 %collective-permute-start.2 = (bf16[1040,512]{1,0:T(8,128)(2,1)S(1)}, bf16[1040,512]{1,0:T(8,128)(2,1)S(1)}, u32[]{:S(2)}, u32[]{:S(2)}) collective-permute-start(bf16[1040,512]{1,0:T(8,128)(2,1)S(1)} %get-tuple-element.39), channel_id=1, source_target_pairs={{0,1},{1,0},{2,3},{3,2},{4,5},{5,4},{6,7},{7,6},{8,9},{9,8},{10,11... | collective-permute-start | bytes 3194888 | tf_op jit(solution)/shard_map/ppermute | solution.py:388
  21.0 1.8 %kept.1 = f32[1024,512]{1,0:T(8,128)S(1)} custom-call(s32[5]{0:T(128)S(1)} %stack.20.scalars, bf16[1024,512]{1,0:T(8,128)(2,1)S(1)} %get-tuple-element.32.edge, bf16[1024,512]{1,0:T(8,128)(2,1)S(1)} %get-tuple-element.31.grid_picked, bf16[1024,512]{1,0:T(8,128)(2,1)S(1)} %get-tuple-element.36.mesh_picked, bf16[1024,512]{1,0:T(8,128)(2,1)S(1)} %get-tuple-element.37.hidden, ...), custom_call_target="tpu_custom_call" | custom-call | flops 1073741824 | bytes 8388628 | tf_op jit(solution)/shard_map/kept/pallas_call | solution.py:93
  23.3 1.2 %pack.1 = (bf16[8,520,128]{2,1,0:T(8,128)(2,1)}, f32[8,128]{1,0:T(8,128)S(1)}) custom-call(f32[1024,512]{1,0:T(8,128)S(1)} %kept.1, bf16[1040,512]{1,0:T(8,128)(2,1)S(1)} %collective-permute-done.2.got, f32[8,512]{1,0:T(8,128)S(1)} %get-tuple-element.40.gain_term), custom_call_target="tpu_custom_call" | custom-call | bytes 4247552 | tf_op jit(solution)/shard_map/pack/pallas_call | solution.py:93
  24.5 8.8 %all-to-all-start = ((bf16[8,520,128]{2,1,0:T(8,128)(2,1)}), bf16[8,520,128]{2,1,0:T(8,128)(2,1)S(1)}, u32[]{:S(2)}, u32[]{:S(2)}) async-start(bf16[8,520,128]{2,1,0:T(8,128)(2,1)} %get-tuple-element.47), calls=%async_computation | async-start | bytes 2129920 | tf_op jit(solution)/shard_map/all_to_all | solution.py:525
  33.3 1.4 %copy-done.5 = bf16[1536,512]{1,0:T(8,128)(2,1)S(1)} copy-done((bf16[1536,512]{1,0:T(8,128)(2,1)S(1)}, bf16[1536,512]{1,0:T(8,128)(2,1)}, u32[]{:S(2)}) %copy-start.5) | copy-done | bytes 1572888
  34.7 4.0 %nodes.1 = (bf16[1024,512]{1,0:T(8,128)(2,1)}, bf16[512,512]{1,0:T(8,128)(2,1)}, f32[128,512]{1,0:T(8,128)S(1)}, bf16[128,512]{1,0:T(8,128)(2,1)S(1)}, bf16[128,512]{1,0:T(8,128)(2,1)S(1)}) custom-call(s32[5]{0:T(128)S(1)} %stack.20.scalars, s32[1,1024]{1,0:T(1,128)S(1)} %bitcast.19, s32[1,1024]{1,0:T(1,128)S(1)} %bitcast.21, ...), custom_call_target="tpu_custom_call" | custom-call | flops 2147483648 | bytes 4730900 | tf_op jit(solution)/shard_map/nodes/pallas_call | solution.py:93
  38.7 9.6 %all-to-all-done.shares = bf16[8,520,128]{2,1,0:T(8,128)(2,1)S(1)} async-done(((bf16[8,520,128]{2,1,0:T(8,128)(2,1)}), bf16[8,520,128]{2,1,0:T(8,128)(2,1)S(1)}, u32[]{:S(2)}, u32[]{:S(2)}) %all-to-all-start) | async-done | bytes 1064992 | tf_op jit(solution)/shard_map/all_to_all | solution.py:525
  48.3 0.8 group_sum.1
  49.1 8.9 %all-to-all-start.1 = ((bf16[16,40,128]{2,1,0:T(8,128)(2,1)}), bf16[16,40,128]{2,1,0:T(8,128)(2,1)S(1)}, u32[]{:S(2)}, u32[]{:S(2)}) async-start(bf16[16,40,128]{2,1,0:T(8,128)(2,1)} %group_sum.1), calls=%async_computation.1 | async-start | bytes 327680 | tf_op jit(solution)/shard_map/all_to_all | solution.py:534
  58.0 1.9 %collective-permute-start.3 = (bf16[128,512]{1,0:T(8,128)(2,1)S(1)}, bf16[128,512]{1,0:T(8,128)(2,1)S(1)}, u32[]{:S(2)}, u32[]{:S(2)}) collective-permute-start(bf16[128,512]{1,0:T(8,128)(2,1)S(1)} %get-tuple-element.44), channel_id=1, source_target_pairs={{0,2},{4,6},{8,10},{12,14},{16,18},{20,22},{24,26},{28,30},{32,34}... | collective-permute-start | bytes 393224 | tf_op jit(solution)/shard_map/ppermute | solution.py:388
  59.8 0.7 collective-permute-start.4
  60.5 10.4 %all-to-all-done.1.pieces = bf16[16,40,128]{2,1,0:T(8,128)(2,1)S(1)} async-done(((bf16[16,40,128]{2,1,0:T(8,128)(2,1)}), bf16[16,40,128]{2,1,0:T(8,128)(2,1)S(1)}, u32[]{:S(2)}, u32[]{:S(2)}) %all-to-all-start.1) | async-done | bytes 163872 | tf_op jit(solution)/shard_map/all_to_all | solution.py:534
  70.9 0.7 whole_sum.1
  71.5 3.5 %all-to-all-start.2 = ((bf16[16,32,128]{2,1,0:T(8,128)(2,1)}), bf16[16,32,128]{2,1,0:T(8,128)(2,1)S(1)}, u32[]{:S(2)}, u32[]{:S(2)}) async-start(bf16[16,32,128]{2,1,0:T(8,128)(2,1)} %get-tuple-element.48), calls=%async_computation.2 | async-start | bytes 262144 | tf_op jit(solution)/shard_map/all_to_all | solution.py:543
  75.1 12.5 %all-to-all-done.2 = bf16[16,32,128]{2,1,0:T(8,128)(2,1)S(1)} async-done(((bf16[16,32,128]{2,1,0:T(8,128)(2,1)}), bf16[16,32,128]{2,1,0:T(8,128)(2,1)S(1)}, u32[]{:S(2)}, u32[]{:S(2)}) %all-to-all-start.2) | async-done | bytes 131104 | tf_op jit(solution)/shard_map/all_to_all | solution.py:543
  87.8 13.2 %all_to_all.20.shares = bf16[8,512,128]{2,1,0:T(8,128)(2,1)S(1)} all-to-all(bf16[8,512,128]{2,1,0:T(8,128)(2,1)S(1)} %copies.1), channel_id=1, replica_groups=mesh['x_far'=2,'x_near'=2,'y_far'=2,'y_near'=2,'z_far'=4,'z_near'=2,'rep..., dimensions={0} | all-to-all | bytes 2097152 | tf_op jit(solution)/shard_map/all_to_all | solution.py:552
  101.0 5.7 %collective-permute-start.5 = (bf16[8,512,128]{2,1,0:T(8,128)(2,1)S(1)}, bf16[8,512,128]{2,1,0:T(8,128)(2,1)S(1)}, u32[]{:S(2)}, u32[]{:S(2)}) collective-permute-start(bf16[8,512,128]{2,1,0:T(8,128)(2,1)S(1)} %all_to_all.20.shares), channel_id=1, source_target_pairs={{0,1},{1,0},{2,3},{3,2},{4,5},{5,4},{6,7},{7,6},{8,9},{9,8},{10,11... | collective-permute-start | bytes 3145736 | tf_op jit(solution)/shard_map/ppermute | solution.py:388
  107.3 1.9 %own_half.1 = (f32[1536,512]{1,0:T(8,128)}, f32[512,512]{1,0:T(8,128)}) custom-call(s32[5]{0:T(128)S(1)} %stack.20.scalars, bf16[8,512,128]{2,1,0:T(8,128)(2,1)S(1)} %all_to_all.20.shares), custom_call_target="tpu_custom_call" | custom-call | bytes 6291456 | tf_op jit(solution)/shard_map/own_half/pallas_call | solution.py:566
  109.3 1.9 %other_half.1 = (f32[1536,512]{1,0:T(8,128)}, f32[512,512]{1,0:T(8,128)}) custom-call(s32[5]{0:T(128)S(1)} %stack.20.scalars, bf16[8,512,128]{2,1,0:T(8,128)(2,1)S(1)} %collective-permute-done.5.shares, f32[1536,512]{1,0:T(8,128)} %get-tuple-element.49.first_in, f32[512,512]{1,0:T(8,128)} %get-tuple-element.50.second_in), custom_call_target="tpu_custom_call", output_to_operand_aliasing={{0}: (2, {}), {1}: (3, {})} | custom-call | bytes 6291456 | tf_op jit(solution)/shard_map/other_half/pallas_call | solution.py:567
  (21 shorter events, 1.8 us)
Async XLA Ops:
  1.6 11.4 %collective-permute-start.1 = (bf16[256,512]{1,0:T(8,128)(2,1)S(1)}, bf16[256,512]{1,0:T(8,128)(2,1)S(1)}, u32[]{:S(2)}, u32[]{:S(2)}) collective-permute-start(bf16[256,512]{1,0:T(8,128)(2,1)S(1)} %stack.21.stack_own), channel_id=1, source_target_pairs={{2,4},{6,8},{10,12},{14,16},{18,20},{22,24},{26,28},{30,32},{34,36... | collective-permute-start | bytes 786440 | tf_op jit(solution)/shard_map/ppermute | solution.py:388
  2.3 11.1 %collective-permute-start = (bf16[256,512]{1,0:T(8,128)(2,1)S(1)}, bf16[256,512]{1,0:T(8,128)(2,1)S(1)}, u32[]{:S(2)}, u32[]{:S(2)}) collective-permute-start(bf16[256,512]{1,0:T(8,128)(2,1)S(1)} %stack.21.stack_own), channel_id=1, source_target_pairs={{0,2},{4,6},{8,10},{12,14},{16,18},{20,22},{24,26},{28,30},{32,34}... | collective-permute-start | bytes 786440 | tf_op jit(solution)/shard_map/ppermute | solution.py:388
  8.5 5.0 %copy-start.2 = (s32[1024]{0:T(1024)S(1)}, s32[1024]{0:T(1024)}, u32[]{:S(2)}) copy-start(s32[1024]{0:T(1024)} %param.18) | copy-start | bytes 12292
  8.5 5.0 %copy-start.3 = (f32[512]{0:T(512)S(1)}, f32[512]{0:T(512)}, u32[]{:S(2)}) copy-start(f32[512]{0:T(512)} %param.16) | copy-start | bytes 6148
  13.0 6.4 %copy-start.4 = (bf16[1536,512]{1,0:T(8,128)(2,1)}, bf16[1536,512]{1,0:T(8,128)(2,1)S(1)}, u32[]{:S(2)}) copy-start(bf16[1536,512]{1,0:T(8,128)(2,1)S(1)} %get-tuple-element.33.w_first) | copy-start | bytes 4718596
  19.4 3.9 %collective-permute-start.2 = (bf16[1040,512]{1,0:T(8,128)(2,1)S(1)}, bf16[1040,512]{1,0:T(8,128)(2,1)S(1)}, u32[]{:S(2)}, u32[]{:S(2)}) collective-permute-start(bf16[1040,512]{1,0:T(8,128)(2,1)S(1)} %get-tuple-element.39), channel_id=1, source_target_pairs={{0,1},{1,0},{2,3},{3,2},{4,5},{5,4},{6,7},{7,6},{8,9},{9,8},{10,11... | collective-permute-start | bytes 3194888 | tf_op jit(solution)/shard_map/ppermute | solution.py:388
  24.5 8.8 %copy-start.1 = (s32[1024]{0:T(1024)S(1)}, s32[1024]{0:T(1024)}, u32[]{:S(2)}) copy-start(s32[1024]{0:T(1024)} %param.17) | copy-start | bytes 12292
  24.5 23.8 %all-to-all-start = ((bf16[8,520,128]{2,1,0:T(8,128)(2,1)}), bf16[8,520,128]{2,1,0:T(8,128)(2,1)S(1)}, u32[]{:S(2)}, u32[]{:S(2)}) async-start(bf16[8,520,128]{2,1,0:T(8,128)(2,1)} %get-tuple-element.47), calls=%async_computation | async-start | bytes 2129920 | tf_op jit(solution)/shard_map/all_to_all | solution.py:525
  33.3 1.4 %copy-start.5 = (bf16[1536,512]{1,0:T(8,128)(2,1)S(1)}, bf16[1536,512]{1,0:T(8,128)(2,1)}, u32[]{:S(2)}) copy-start(bf16[1536,512]{1,0:T(8,128)(2,1)} %copy-done.4) | copy-start | bytes 4718596
  49.1 21.8 %all-to-all-start.1 = ((bf16[16,40,128]{2,1,0:T(8,128)(2,1)}), bf16[16,40,128]{2,1,0:T(8,128)(2,1)S(1)}, u32[]{:S(2)}, u32[]{:S(2)}) async-start(bf16[16,40,128]{2,1,0:T(8,128)(2,1)} %group_sum.1), calls=%async_computation.1 | async-start | bytes 327680 | tf_op jit(solution)/shard_map/all_to_all | solution.py:534
  58.0 17.1 %collective-permute-start.3 = (bf16[128,512]{1,0:T(8,128)(2,1)S(1)}, bf16[128,512]{1,0:T(8,128)(2,1)S(1)}, u32[]{:S(2)}, u32[]{:S(2)}) collective-permute-start(bf16[128,512]{1,0:T(8,128)(2,1)S(1)} %get-tuple-element.44), channel_id=1, source_target_pairs={{0,2},{4,6},{8,10},{12,14},{16,18},{20,22},{24,26},{28,30},{32,34}... | collective-permute-start | bytes 393224 | tf_op jit(solution)/shard_map/ppermute | solution.py:388
  59.8 15.3 %collective-permute-start.4 = (bf16[128,512]{1,0:T(8,128)(2,1)S(1)}, bf16[128,512]{1,0:T(8,128)(2,1)S(1)}, u32[]{:S(2)}, u32[]{:S(2)}) collective-permute-start(bf16[128,512]{1,0:T(8,128)(2,1)S(1)} %get-tuple-element.45), channel_id=1, source_target_pairs={{2,4},{6,8},{10,12},{14,16},{18,20},{22,24},{26,28},{30,32},{34,36... | collective-permute-start | bytes 393224 | tf_op jit(solution)/shard_map/ppermute | solution.py:388
  71.5 16.1 %all-to-all-start.2 = ((bf16[16,32,128]{2,1,0:T(8,128)(2,1)}), bf16[16,32,128]{2,1,0:T(8,128)(2,1)S(1)}, u32[]{:S(2)}, u32[]{:S(2)}) async-start(bf16[16,32,128]{2,1,0:T(8,128)(2,1)} %get-tuple-element.48), calls=%async_computation.2 | async-start | bytes 262144 | tf_op jit(solution)/shard_map/all_to_all | solution.py:543
  75.1 25.9 %copy-start = (f32[128,512]{1,0:T(8,128)}, f32[128,512]{1,0:T(8,128)S(1)}, u32[]{:S(2)}) copy-start(f32[128,512]{1,0:T(8,128)S(1)} %convert_add_fusion.after) | copy-start | bytes 786436
  101.0 8.3 %collective-permute-start.5 = (bf16[8,512,128]{2,1,0:T(8,128)(2,1)S(1)}, bf16[8,512,128]{2,1,0:T(8,128)(2,1)S(1)}, u32[]{:S(2)}, u32[]{:S(2)}) collective-permute-start(bf16[8,512,128]{2,1,0:T(8,128)(2,1)S(1)} %all_to_all.20.shares), channel_id=1, source_target_pairs={{0,1},{1,0},{2,3},{3,2},{4,5},{5,4},{6,7},{7,6},{8,9},{9,8},{10,11... | collective-permute-start | bytes 3145736 | tf_op jit(solution)/shard_map/ppermute | solution.py:388

commit v10 on v8

--- a/solution.py
+++ b/solution.py
@@ -230,19 +230,27 @@
             jnp.bfloat16
         )
     gain_term[...] = jnp.broadcast_to(gain_sum, gain_term.shape)
-    sent[2 * width : 2 * width + 16, :] = jnp.concatenate(
+    sent[width : width + 16, :] = jnp.concatenate(
         [gain_rows(gain_sum, width), jnp.zeros((14, width), jnp.float32)], axis=0
     ).astype(jnp.bfloat16)
 
     @pl.when(scalars[3] == 0)
     def _():
         sent[0:width, :] = dot(mesh_picked[...], grad_pre[...], 0, 0).astype(jnp.bfloat16)
-        sent[width : 2 * width, :] = dot(hidden[...], grad_output[...], 0, 0).astype(jnp.bfloat16)
 
     @pl.when(scalars[3] != 0)
     def _():
         sent[0:width, :] = dot(edge[...], grad_pre[...], 0, 0).astype(jnp.bfloat16)
-        sent[width : 2 * width, :] = dot(grid_picked[...], grad_pre[...], 0, 0).astype(jnp.bfloat16)
+
+
+def rest_kernel(scalars, grid_picked, hidden, grad_pre, grad_output, sent):
+    @pl.when(scalars[3] == 0)
+    def _():
+        sent[...] = dot(hidden[...], grad_output[...], 0, 0).astype(jnp.bfloat16)
+
+    @pl.when(scalars[3] != 0)
+    def _():
+        sent[...] = dot(grid_picked[...], grad_pre[...], 0, 0).astype(jnp.bfloat16)
 
 
 def kept_kernel(scalars, edge, grid_picked, mesh_picked, hidden, grad_pre, grad_output, kept):
@@ -259,15 +267,17 @@
         kept[width : 2 * width, :] = dot(grid_picked[...], grad_pre[...], 0, 0)
 
 
-def pack_kernel(kept, got, gain_term, packed, done):
+def pack_kernel(kept, got, got_rest, gain_term, packed, done):
     count = packed.shape[0]
     half, width = kept.shape
     part = half // count
-    tail = got[half : half + 16, :].astype(jnp.float32)
+    tail = got[width : width + 16, :].astype(jnp.float32)
     gain = gain_rows(gain_term[0:1, :] + gain_of(tail[0:2]), LANES)
     for place in range(count):
         rows = pl.ds(place * part, part)
-        data = narrow(kept[rows, :] + got[rows, :].astype(jnp.float32))
+        first = place * part
+        other = got[rows, :] if first < width else got_rest[pl.ds(first - width, part), :]
+        data = narrow(kept[rows, :] + other.astype(jnp.float32))
         packed[place] = jnp.concatenate([data, gain], axis=0).astype(jnp.bfloat16)
     done[...] = jnp.zeros(done.shape, jnp.float32)
 
@@ -285,7 +295,7 @@
     own, near, across, far = [part[...].astype(jnp.float32) for part in (own, near, across, far)]
     total = ((own + across) + (near + far)) * factor
     data = copies.shape[1]
-    gain_grad[...] = jnp.broadcast_to(gain_of(total[data:]), gain_grad.shape)
+    gain_grad[...] = gain_of(total[data:])
     share = total[:data].astype(jnp.bfloat16)
     for place in range(copies.shape[0]):
         copies[place] = share
@@ -455,7 +465,7 @@
         "edges",
         [in_smem()] + [in_vmem()] * 10,
         [
-            matrix((2 * width + 16, width)),
+            matrix((width + 16, width)),
             floats((8, width)),
             pltpu.VMEM((slots, width), jnp.bfloat16),
         ]
@@ -476,6 +486,15 @@
         7 * unit,
     )
     got = swapped(sent)
+    (rest,) = call(
+        rest_kernel,
+        "rest",
+        [in_smem()] + [in_vmem()] * 4,
+        [matrix((width, width))],
+        (scalars, grid_picked, hidden, grad_pre, grad_output),
+        unit,
+    )
+    got_rest = swapped(rest)
     (kept,) = call(
         kept_kernel,
         "kept",
@@ -489,9 +508,9 @@
     packed, done = call(
         pack_kernel,
         "pack",
-        [in_vmem()] * 3,
+        [in_vmem()] * 4,
         [matrix((group, part + extra, LANES)), floats((8, LANES))],
-        (kept, got, gain_term),
+        (kept, got, got_rest, gain_term),
         0,
     )
     edge_grad, grid_grad, mesh_own, to_first, to_second = call(
@@ -528,7 +547,7 @@
         functools.partial(whole_sum_kernel, factor),
         "whole_sum",
         [in_vmem()] * 4 + [anywhere()],
-        [matrix((group, part, LANES)), floats((8, width))],
+        [matrix((group, part, LANES)), floats((1, width))],
         (packed, *turns, mesh_grad),
         0,
     )

time: 94.7 us -> 94 us (level)
  Pallas kernels: 22.5 us -> 23.8 us
  blocking collectives: 21.2 us -> 20.2 us
    pallas_call x8 -> x9, Pallas kernels: 18.7 us -> 20 us  [call(): pl.pallas_call(kernel, out_shape=outs, in_specs=specs, out_specs=[in_vmem...]
    all_to_all x1, blocking collectives: 21.2 us -> 20.2 us  [per_device(): total = lax.all_to_all(copies, GROUP, 0, 0)]
    ppermute x9 -> x10, starting transfers between devices: 19 us -> 19.2 us  [swap_pairs(): return lax.ppermute(value, axis, pairs + [(d, s) for s, d in pairs])]
    ppermute x9 -> x10, waiting for transfers between devices: 5.71 us -> 5.64 us  [swap_pairs(): return lax.ppermute(value, axis, pairs + [(d, s) for s, d in pairs])]
  transfers between devices with their start and end apart: 10 -> 11, of which waited for: 4 -> 5; matrix products, arithmetic and copies ran while one was open for 1% -> 0% of each run, Pallas kernels for 13% -> 15%
where the time goes in v10:
time: 94 us; the launch traced here: 93.7 us
  starting transfers between devices  30.2 us (32%)
  Pallas kernels  23.8 us (25%)
  blocking collectives  20.2 us (21%)
  waiting for transfers between devices  16.3 us (17%)
  between operations  1.61 us (2%)
  local copies, waits for them, and re-layouts  1.51 us (2%)
    all_to_all x1, blocking collectives, per_device(): total = lax.all_to_all(copies, GROUP, 0, 0)  20.2 us
    pallas_call x9, Pallas kernels, call(): pl.pallas_call(kernel, out_shape=outs, in_specs=specs, out_specs=[in_vmem...  20 us
    ppermute x10, starting transfers between devices, swap_pairs(): return lax.ppermute(value, axis, pairs + [(d, s) for s, d in pairs])  19.2 us
    all_to_all x1, starting transfers between devices, per_device(): shares = lax.all_to_all(packed, GROUP, 0, 0)  11 us
    all_to_all x1, waiting for transfers between devices, per_device(): shares = lax.all_to_all(packed, GROUP, 0, 0)  10.6 us
    ppermute x10, waiting for transfers between devices, swap_pairs(): return lax.ppermute(value, axis, pairs + [(d, s) for s, d in pairs])  5.64 us
    pallas_call x1, Pallas kernels, per_device(): halves(own_half_kernel, in_specs=[in_smem(), in_vmem()], name='own_half')  1.93 us
    pallas_call x1, Pallas kernels, per_device(): halves(other_half_kernel, in_specs=[in_smem(), in_vmem()] + [in_hbm()] *...  1.93 us
  transfers between devices with their start and end apart: 11, of which 5 were waited for; matrix products, arithmetic and copies ran while one was open for 0% of the time, Pallas kernels for 15%

profile of v10, /device:TPU:1, one launch (start us, length us, event | category | flops | bytes accessed | tf_op | source)
XLA Modules:
  0.0 93.7 jit_solution(15148430098417282690)
XLA Ops:
  0.6 1.0 %stack.21.stack_own = bf16[256,512]{1,0:T(8,128)(2,1)S(1)} custom-call(bf16[128,512]{1,0:T(8,128)(2,1)} %bitcast.21, bf16[128,512]{1,0:T(8,128)(2,1)} %bitcast.22), custom_call_target="tpu_custom_call" | custom-call | bytes 524288 | tf_op jit(solution)/shard_map/stack/pallas_call | solution.py:92
  1.6 0.7 collective-permute-start.1
  2.3 5.4 %collective-permute-start = (bf16[256,512]{1,0:T(8,128)(2,1)S(1)}, bf16[256,512]{1,0:T(8,128)(2,1)S(1)}, u32[]{:S(2)}, u32[]{:S(2)}) collective-permute-start(bf16[256,512]{1,0:T(8,128)(2,1)S(1)} %stack.21.stack_own), channel_id=1, source_target_pairs={{0,2},{4,6},{8,10},{12,14},{16,18},{20,22},{24,26},{28,30},{32,34}... | collective-permute-start | bytes 786440 | tf_op jit(solution)/shard_map/ppermute | solution.py:387
  8.5 4.5 %near.1 = (f32[1024,512]{1,0:T(8,128)S(1)}, bf16[1024,512]{1,0:T(8,128)(2,1)S(1)}, bf16[1024,512]{1,0:T(8,128)(2,1)S(1)}, bf16[1536,512]{1,0:T(8,128)(2,1)S(1)}, bf16[512,512]{1,0:T(8,128)(2,1)S(1)}) custom-call(s32[5]{0:T(128)S(1)} %stack.20.scalars, s32[1,1024]{1,0:T(1,128)} %bitcast.16, bf16[512,512]{1,0:T(8,128)(2,1)} %bitcast.24, ...), custom_call_target="tpu_custom_call" | custom-call | flops 1610612736 | bytes 9965588 | tf_op jit(solution)/shard_map/near/pallas_call | solution.py:92
  13.0 0.4 collective-permute-done.stack_first
  13.5 5.4 %edges.1 = (bf16[528,512]{1,0:T(8,128)(2,1)S(1)}, f32[8,512]{1,0:T(8,128)S(1)}, bf16[1024,512]{1,0:T(8,128)(2,1)S(1)}, bf16[1024,512]{1,0:T(8,128)(2,1)S(1)}, bf...) custom-call(s32[5]{0:T(128)S(1)} %stack.20.scalars, s32[1,1024]{1,0:T(1,128)S(1)} %bitcast.18, ...), custom_call_target="tpu_custom_call" | custom-call | flops 3758096384 | bytes 11835412 | tf_op jit(solution)/shard_map/edges/pallas_call | solution.py:92
  18.9 1.6 %collective-permute-start.2 = (bf16[528,512]{1,0:T(8,128)(2,1)S(1)}, bf16[528,512]{1,0:T(8,128)(2,1)S(1)}, u32[]{:S(2)}, u32[]{:S(2)}) collective-permute-start(bf16[528,512]{1,0:T(8,128)(2,1)S(1)} %get-tuple-element.39), channel_id=1, source_target_pairs={{0,1},{1,0},{2,3},{3,2},{4,5},{5,4},{6,7},{7,6},{8,9},{9,8},{10,11... | collective-permute-start | bytes 1622024 | tf_op jit(solution)/shard_map/ppermute | solution.py:387
  20.5 1.3 %rest.1 = bf16[512,512]{1,0:T(8,128)(2,1)S(1)} custom-call(s32[5]{0:T(128)S(1)} %stack.20.scalars, bf16[1024,512]{1,0:T(8,128)(2,1)S(1)} %get-tuple-element.31.grid_picked, bf16[1024,512]{1,0:T(8,128)(2,1)S(1)} %get-tuple-element.37.hidden, bf16[1024,512]{1,0:T(8,128)(2,1)S(1)} %get-tuple-element.35.grad_pre, bf16[1024,512]{1,0:T(8,128)(2,1)S(1)} %get-tuple-element.38.grad_output), custom_call_target="tpu_custom_call" | custom-call | flops 536870912 | bytes 4718612 | tf_op jit(solution)/shard_map/rest/pallas_call | solution.py:92
  21.9 1.8 %kept.1 = f32[1024,512]{1,0:T(8,128)S(1)} custom-call(s32[5]{0:T(128)S(1)} %stack.20.scalars, bf16[1024,512]{1,0:T(8,128)(2,1)S(1)} %get-tuple-element.32.edge, bf16[1024,512]{1,0:T(8,128)(2,1)S(1)} %get-tuple-element.31.grid_picked, bf16[1024,512]{1,0:T(8,128)(2,1)S(1)} %get-tuple-element.36.mesh_picked, bf16[1024,512]{1,0:T(8,128)(2,1)S(1)} %get-tuple-element.37.hidden, ...), custom_call_target="tpu_custom_call" | custom-call | flops 1073741824 | bytes 8388628 | tf_op jit(solution)/shard_map/kept/pallas_call | solution.py:92
  23.8 1.2 %pack.1 = (bf16[32,136,128]{2,1,0:T(8,128)(2,1)}, f32[8,128]{1,0:T(8,128)S(1)}) custom-call(f32[1024,512]{1,0:T(8,128)S(1)} %kept.1, bf16[528,512]{1,0:T(8,128)(2,1)S(1)} %collective-permute-done.2.got, bf16[512,512]{1,0:T(8,128)(2,1)S(1)} %collective-permute-done.3.got_rest, f32[8,512]{1,0:T(8,128)S(1)} %get-tuple-element.40.gain_term), custom_call_target="tpu_custom_call" | custom-call | bytes 4296704 | tf_op jit(solution)/shard_map/pack/pallas_call | solution.py:92
  25.0 11.0 %all-to-all-start = ((bf16[32,136,128]{2,1,0:T(8,128)(2,1)}), bf16[32,136,128]{2,1,0:T(8,128)(2,1)S(1)}, u32[]{:S(2)}, u32[]{:S(2)}) async-start(bf16[32,136,128]{2,1,0:T(8,128)(2,1)} %get-tuple-element.47), calls=%async_computation | async-start | bytes 2228224 | tf_op jit(solution)/shard_map/all_to_all | solution.py:533
  36.0 1.4 %copy-done.5 = bf16[1536,512]{1,0:T(8,128)(2,1)S(1)} copy-done((bf16[1536,512]{1,0:T(8,128)(2,1)S(1)}, bf16[1536,512]{1,0:T(8,128)(2,1)}, u32[]{:S(2)}) %copy-start.5) | copy-done | bytes 1572888
  37.4 4.0 %nodes.1 = (bf16[1024,512]{1,0:T(8,128)(2,1)}, bf16[512,512]{1,0:T(8,128)(2,1)}, f32[128,512]{1,0:T(8,128)S(1)}, bf16[128,512]{1,0:T(8,128)(2,1)S(1)}, bf16[128,512]{1,0:T(8,128)(2,1)S(1)}) custom-call(s32[5]{0:T(128)S(1)} %stack.20.scalars, s32[1,1024]{1,0:T(1,128)S(1)} %bitcast.17, s32[1,1024]{1,0:T(1,128)S(1)} %bitcast.19, ...), custom_call_target="tpu_custom_call" | custom-call | flops 2147483648 | bytes 4730900 | tf_op jit(solution)/shard_map/nodes/pallas_call | solution.py:92
  41.4 1.1 %collective-permute-start.4 = (bf16[128,512]{1,0:T(8,128)(2,1)S(1)}, bf16[128,512]{1,0:T(8,128)(2,1)S(1)}, u32[]{:S(2)}, u32[]{:S(2)}) collective-permute-start(bf16[128,512]{1,0:T(8,128)(2,1)S(1)} %get-tuple-element.44), channel_id=1, source_target_pairs={{0,2},{4,6},{8,10},{12,14},{16,18},{20,22},{24,26},{28,30},{32,34}... | collective-permute-start | bytes 393224 | tf_op jit(solution)/shard_map/ppermute | solution.py:387
  42.4 0.7 collective-permute-start.5
  43.1 10.6 %all-to-all-done.shares = bf16[32,136,128]{2,1,0:T(8,128)(2,1)S(1)} async-done(((bf16[32,136,128]{2,1,0:T(8,128)(2,1)}), bf16[32,136,128]{2,1,0:T(8,128)(2,1)S(1)}, u32[]{:S(2)}, u32[]{:S(2)}) %all-to-all-start) | async-done | bytes 1114144 | tf_op jit(solution)/shard_map/all_to_all | solution.py:533
  53.9 4.6 %collective-permute-start.8 = (bf16[136,128]{1,0:T(8,128)(2,1)S(1)}, bf16[136,128]{1,0:T(8,128)(2,1)S(1)}, u32[]{:S(2)}, u32[]{:S(2)}) collective-permute-start(bf16[136,128]{1,0:T(8,128)(2,1)S(1)} %group_sum.1.own), channel_id=1, source_target_pairs={{0,12},{4,8},{12,0},{8,4},{1,13},{5,9},{13,1},{9,5},{2,14},{6,10},... | collective-permute-start | bytes 104456 | tf_op jit(solution)/shard_map/ppermute | solution.py:387
  58.6 2.1 %collective-permute-start.6 = (bf16[136,128]{1,0:T(8,128)(2,1)S(1)}, bf16[136,128]{1,0:T(8,128)(2,1)S(1)}, u32[]{:S(2)}, u32[]{:S(2)}) collective-permute-start(bf16[136,128]{1,0:T(8,128)(2,1)S(1)} %group_sum.1.own), channel_id=1, source_target_pairs={{0,4},{8,12},{4,0},{12,8},{1,5},{9,13},{5,1},{13,9},{2,6},{10,14},... | collective-permute-start | bytes 104456 | tf_op jit(solution)/shard_map/ppermute | solution.py:387
  60.8 4.8 %collective-permute-done.7.across = bf16[136,128]{1,0:T(8,128)(2,1)S(1)} collective-permute-done((bf16[136,128]{1,0:T(8,128)(2,1)S(1)}, bf16[136,128]{1,0:T(8,128)(2,1)S(1)}, u32[]{:S(2)}, u32[]{:S(2)}) %collective-permute-start.7) | collective-permute-done | bytes 34848 | tf_op jit(solution)/shard_map/ppermute | solution.py:387
  65.6 0.6 whole_sum.1
  66.2 20.2 %all_to_all.10.shares = bf16[32,128,128]{2,1,0:T(8,128)(2,1)S(1)} all-to-all(bf16[32,128,128]{2,1,0:T(8,128)(2,1)S(1)} %get-tuple-element.48), channel_id=1, replica_groups=mesh['band'=16,'hi'=4,'lo'=2,'rep'=2] {'band','lo'}, dimensions={0} | all-to-all | bytes 2097152 | tf_op jit(solution)/shard_map/all_to_all | solution.py:554
  86.4 2.9 %collective-permute-start.9 = (bf16[32,128,128]{2,1,0:T(8,128)(2,1)S(1)}, bf16[32,128,128]{2,1,0:T(8,128)(2,1)S(1)}, u32[]{:S(2)}, u32[]{:S(2)}) collective-permute-start(bf16[32,128,128]{2,1,0:T(8,128)(2,1)S(1)} %all_to_all.10.shares), channel_id=1, source_target_pairs={{0,1},{1,0},{2,3},{3,2},{4,5},{5,4},{6,7},{7,6},{8,9},{9,8},{10,11... | collective-permute-start | bytes 3145736 | tf_op jit(solution)/shard_map/ppermute | solution.py:387
  89.3 1.9 %own_half.1 = (f32[1536,512]{1,0:T(8,128)}, f32[512,512]{1,0:T(8,128)}) custom-call(s32[5]{0:T(128)S(1)} %stack.20.scalars, bf16[32,128,128]{2,1,0:T(8,128)(2,1)S(1)} %all_to_all.10.shares), custom_call_target="tpu_custom_call" | custom-call | bytes 6291456 | tf_op jit(solution)/shard_map/own_half/pallas_call | solution.py:568
  91.6 1.9 %other_half.1 = (f32[1536,512]{1,0:T(8,128)}, f32[512,512]{1,0:T(8,128)}) custom-call(s32[5]{0:T(128)S(1)} %stack.20.scalars, bf16[32,128,128]{2,1,0:T(8,128)(2,1)S(1)} %collective-permute-done.9.shares, f32[1536,512]{1,0:T(8,128)} %get-tuple-element.49.first_in, f32[512,512]{1,0:T(8,128)} %get-tuple-element.50.second_in), custom_call_target="tpu_custom_call", output_to_operand_aliasing={{0}: (2, {}), {1}: (3, {})} | custom-call | bytes 6291456 | tf_op jit(solution)/shard_map/other_half/pallas_call | solution.py:569
  (24 shorter events, 0.9 us)
Async XLA Ops:
  1.6 11.4 %collective-permute-start.1 = (bf16[256,512]{1,0:T(8,128)(2,1)S(1)}, bf16[256,512]{1,0:T(8,128)(2,1)S(1)}, u32[]{:S(2)}, u32[]{:S(2)}) collective-permute-start(bf16[256,512]{1,0:T(8,128)(2,1)S(1)} %stack.21.stack_own), channel_id=1, source_target_pairs={{2,4},{6,8},{10,12},{14,16},{18,20},{22,24},{26,28},{30,32},{34,36... | collective-permute-start | bytes 786440 | tf_op jit(solution)/shard_map/ppermute | solution.py:387
  2.3 11.1 %collective-permute-start = (bf16[256,512]{1,0:T(8,128)(2,1)S(1)}, bf16[256,512]{1,0:T(8,128)(2,1)S(1)}, u32[]{:S(2)}, u32[]{:S(2)}) collective-permute-start(bf16[256,512]{1,0:T(8,128)(2,1)S(1)} %stack.21.stack_own), channel_id=1, source_target_pairs={{0,2},{4,6},{8,10},{12,14},{16,18},{20,22},{24,26},{28,30},{32,34}... | collective-permute-start | bytes 786440 | tf_op jit(solution)/shard_map/ppermute | solution.py:387
  8.5 5.0 %copy-start.2 = (s32[1024]{0:T(1024)S(1)}, s32[1024]{0:T(1024)}, u32[]{:S(2)}) copy-start(s32[1024]{0:T(1024)} %param.18) | copy-start | bytes 12292
  8.5 5.0 %copy-start.3 = (f32[512]{0:T(512)S(1)}, f32[512]{0:T(512)}, u32[]{:S(2)}) copy-start(f32[512]{0:T(512)} %param.16) | copy-start | bytes 6148
  13.0 5.9 %copy-start.4 = (bf16[1536,512]{1,0:T(8,128)(2,1)}, bf16[1536,512]{1,0:T(8,128)(2,1)S(1)}, u32[]{:S(2)}) copy-start(bf16[1536,512]{1,0:T(8,128)(2,1)S(1)} %get-tuple-element.33.w_first) | copy-start | bytes 4718596
  18.9 4.9 %collective-permute-start.2 = (bf16[528,512]{1,0:T(8,128)(2,1)S(1)}, bf16[528,512]{1,0:T(8,128)(2,1)S(1)}, u32[]{:S(2)}, u32[]{:S(2)}) collective-permute-start(bf16[528,512]{1,0:T(8,128)(2,1)S(1)} %get-tuple-element.39), channel_id=1, source_target_pairs={{0,1},{1,0},{2,3},{3,2},{4,5},{5,4},{6,7},{7,6},{8,9},{9,8},{10,11... | collective-permute-start | bytes 1622024 | tf_op jit(solution)/shard_map/ppermute | solution.py:387
  21.8 2.0 %collective-permute-start.3 = (bf16[512,512]{1,0:T(8,128)(2,1)S(1)}, bf16[512,512]{1,0:T(8,128)(2,1)S(1)}, u32[]{:S(2)}, u32[]{:S(2)}) collective-permute-start(bf16[512,512]{1,0:T(8,128)(2,1)S(1)} %rest.1), channel_id=1, source_target_pairs={{0,1},{1,0},{2,3},{3,2},{4,5},{5,4},{6,7},{7,6},{8,9},{9,8},{10,11... | collective-permute-start | bytes 1572872 | tf_op jit(solution)/shard_map/ppermute | solution.py:387
  23.8 12.2 %copy-start.1 = (s32[1024]{0:T(1024)S(1)}, s32[1024]{0:T(1024)}, u32[]{:S(2)}) copy-start(s32[1024]{0:T(1024)} %param.17) | copy-start | bytes 12292
  25.0 28.7 %all-to-all-start = ((bf16[32,136,128]{2,1,0:T(8,128)(2,1)}), bf16[32,136,128]{2,1,0:T(8,128)(2,1)S(1)}, u32[]{:S(2)}, u32[]{:S(2)}) async-start(bf16[32,136,128]{2,1,0:T(8,128)(2,1)} %get-tuple-element.47), calls=%async_computation | async-start | bytes 2228224 | tf_op jit(solution)/shard_map/all_to_all | solution.py:533
  36.0 1.4 %copy-start.5 = (bf16[1536,512]{1,0:T(8,128)(2,1)S(1)}, bf16[1536,512]{1,0:T(8,128)(2,1)}, u32[]{:S(2)}) copy-start(bf16[1536,512]{1,0:T(8,128)(2,1)} %copy-done.4) | copy-start | bytes 4718596
  41.4 19.3 %collective-permute-start.4 = (bf16[128,512]{1,0:T(8,128)(2,1)S(1)}, bf16[128,512]{1,0:T(8,128)(2,1)S(1)}, u32[]{:S(2)}, u32[]{:S(2)}) collective-permute-start(bf16[128,512]{1,0:T(8,128)(2,1)S(1)} %get-tuple-element.44), channel_id=1, source_target_pairs={{0,2},{4,6},{8,10},{12,14},{16,18},{20,22},{24,26},{28,30},{32,34}... | collective-permute-start | bytes 393224 | tf_op jit(solution)/shard_map/ppermute | solution.py:387
  42.4 18.3 %collective-permute-start.5 = (bf16[128,512]{1,0:T(8,128)(2,1)S(1)}, bf16[128,512]{1,0:T(8,128)(2,1)S(1)}, u32[]{:S(2)}, u32[]{:S(2)}) collective-permute-start(bf16[128,512]{1,0:T(8,128)(2,1)S(1)} %get-tuple-element.45), channel_id=1, source_target_pairs={{2,4},{6,8},{10,12},{14,16},{18,20},{22,24},{26,28},{30,32},{34,36... | collective-permute-start | bytes 393224 | tf_op jit(solution)/shard_map/ppermute | solution.py:387
  53.9 6.9 %collective-permute-start.8 = (bf16[136,128]{1,0:T(8,128)(2,1)S(1)}, bf16[136,128]{1,0:T(8,128)(2,1)S(1)}, u32[]{:S(2)}, u32[]{:S(2)}) collective-permute-start(bf16[136,128]{1,0:T(8,128)(2,1)S(1)} %group_sum.1.own), channel_id=1, source_target_pairs={{0,12},{4,8},{12,0},{8,4},{1,13},{5,9},{13,1},{9,5},{2,14},{6,10},... | collective-permute-start | bytes 104456 | tf_op jit(solution)/shard_map/ppermute | solution.py:387
  58.5 7.1 %collective-permute-start.7 = (bf16[136,128]{1,0:T(8,128)(2,1)S(1)}, bf16[136,128]{1,0:T(8,128)(2,1)S(1)}, u32[]{:S(2)}, u32[]{:S(2)}) collective-permute-start(bf16[136,128]{1,0:T(8,128)(2,1)S(1)} %group_sum.1.own), channel_id=1, source_target_pairs={{0,8},{4,12},{8,0},{12,4},{1,9},{5,13},{9,1},{13,5},{2,10},{6,14},... | collective-permute-start | bytes 104456 | tf_op jit(solution)/shard_map/ppermute | solution.py:387
  58.6 7.0 %collective-permute-start.6 = (bf16[136,128]{1,0:T(8,128)(2,1)S(1)}, bf16[136,128]{1,0:T(8,128)(2,1)S(1)}, u32[]{:S(2)}, u32[]{:S(2)}) collective-permute-start(bf16[136,128]{1,0:T(8,128)(2,1)S(1)} %group_sum.1.own), channel_id=1, source_target_pairs={{0,4},{8,12},{4,0},{12,8},{1,5},{9,13},{5,1},{13,9},{2,6},{10,14},... | collective-permute-start | bytes 104456 | tf_op jit(solution)/shard_map/ppermute | solution.py:387
  60.8 32.7 %copy-start = (f32[128,512]{1,0:T(8,128)}, f32[128,512]{1,0:T(8,128)S(1)}, u32[]{:S(2)}) copy-start(f32[128,512]{1,0:T(8,128)S(1)} %convert_add_fusion.after) | copy-start | bytes 786436
  86.4 5.2 %collective-permute-start.9 = (bf16[32,128,128]{2,1,0:T(8,128)(2,1)S(1)}, bf16[32,128,128]{2,1,0:T(8,128)(2,1)S(1)}, u32[]{:S(2)}, u32[]{:S(2)}) collective-permute-start(bf16[32,128,128]{2,1,0:T(8,128)(2,1)S(1)} %all_to_all.10.shares), channel_id=1, source_target_pairs={{0,1},{1,0},{2,3},{3,2},{4,5},{5,4},{6,7},{7,6},{8,9},{9,8},{10,11... | collective-permute-start | bytes 3145736 | tf_op jit(solution)/shard_map/ppermute | solution.py:387

commit v11 on v8

--- a/solution.py
+++ b/solution.py
@@ -259,7 +259,7 @@
         kept[width : 2 * width, :] = dot(grid_picked[...], grad_pre[...], 0, 0)
 
 
-def pack_kernel(kept, got, gain_term, packed, done):
+def pack_kernel(kept, got, gain_term, packed):
     count = packed.shape[0]
     half, width = kept.shape
     part = half // count
@@ -269,10 +269,9 @@
         rows = pl.ds(place * part, part)
         data = narrow(kept[rows, :] + got[rows, :].astype(jnp.float32))
         packed[place] = jnp.concatenate([data, gain], axis=0).astype(jnp.bfloat16)
-    done[...] = jnp.zeros(done.shape, jnp.float32)
-
-
-def group_sum_kernel(shares, after, packed):
+
+
+def group_sum_kernel(shares, packed):
     total = shares[0].astype(jnp.float32)
     for place in range(1, shares.shape[0]):
         total = total + shares[place].astype(jnp.float32)
@@ -486,14 +485,27 @@
     )
     part = 2 * width // group * width // LANES
     extra = 2 * width // LANES
-    packed, done = call(
+    (packed,) = call(
         pack_kernel,
         "pack",
         [in_vmem()] * 3,
-        [matrix((group, part + extra, LANES)), floats((8, LANES))],
+        [matrix((group, part + extra, LANES))],
         (kept, got, gain_term),
         0,
     )
+    shares = lax.all_to_all(packed, GROUP, 0, 0)
+    (packed,) = call(
+        group_sum_kernel,
+        "group_sum",
+        [in_vmem()],
+        [matrix((part + extra, LANES))],
+        (shares,),
+        0,
+    )
+    turns = [
+        swap_pairs(packed, "hi", pairs)
+        for pairs in ([(0, 1), (2, 3)], [(0, 2), (1, 3)], [(0, 3), (1, 2)])
+    ]
     edge_grad, grid_grad, mesh_own, to_first, to_second = call(
         node_kernel,
         "nodes",
@@ -505,31 +517,18 @@
             matrix((rows_mesh, width)),
             matrix((rows_mesh, width)),
         ],
-        (scalars, senders, receivers, grad_pre, w_first, done),
+        (scalars, senders, receivers, grad_pre, w_first, packed),
         4 * unit,
     )
     from_first = exchanged(to_first, 0).astype(jnp.float32)
     from_second = exchanged(to_second, 1).astype(jnp.float32)
     mesh_grad = mesh_own + from_first + from_second
-    shares = lax.all_to_all(packed, GROUP, 0, 0)
-    (packed,) = call(
-        group_sum_kernel,
-        "group_sum",
-        [in_vmem(), anywhere()],
-        [matrix((part + extra, LANES))],
-        (shares, mesh_own),
-        0,
-    )
-    turns = [
-        swap_pairs(packed, "hi", pairs)
-        for pairs in ([(0, 1), (2, 3)], [(0, 2), (1, 3)], [(0, 3), (1, 2)])
-    ]
     copies, gain_grad = call(
         functools.partial(whole_sum_kernel, factor),
         "whole_sum",
         [in_vmem()] * 4 + [anywhere()],
         [matrix((group, part, LANES)), floats((8, width))],
-        (packed, *turns, mesh_grad),
+        (packed, *turns, mesh_own),
         0,
     )
     total = lax.all_to_all(copies, GROUP, 0, 0)

time: 94.7 us -> 101 us (1.067)
  the two profiles are of different devices: /device:TPU:1 before, /device:TPU:2 now
where the time goes in v11:
time: 101 us
  blocking collectives  40.6 us (40%)
  starting transfers between devices  25.3 us (25%)
  Pallas kernels  21.5 us (21%)
  waiting for transfers between devices  10.3 us (10%)
  between operations  1.56 us (2%)
    ppermute x9, starting transfers between devices, swap_pairs(): return lax.ppermute(value, axis, pairs + [(d, s) for s, d in pairs])  25.3 us
    all_to_all x1, blocking collectives, per_device(): shares = lax.all_to_all(packed, GROUP, 0, 0)  22.6 us
    all_to_all x1, blocking collectives, per_device(): total = lax.all_to_all(copies, GROUP, 0, 0)  17.9 us
    pallas_call x8, Pallas kernels, call(): pl.pallas_call(kernel, out_shape=outs, in_specs=specs, out_specs=[in_vmem...  17.7 us
    ppermute x9, waiting for transfers between devices, swap_pairs(): return lax.ppermute(value, axis, pairs + [(d, s) for s, d in pairs])  10.3 us
  transfers between devices with their start and end apart: 9, of which 5 were waited for; matrix products, arithmetic and copies ran while one was open for 1% of the time, Pallas kernels for 12%

profile of v11, /device:TPU:2, one launch (start us, length us, event | category | flops | bytes accessed | tf_op | source)
XLA Modules:
  0.0 100.7 jit_solution(17215017605891190738)
XLA Ops:
  0.6 1.0 stack.21.stack_own
  1.6 10.2 %collective-permute-start.1 = (bf16[256,512]{1,0:T(8,128)(2,1)S(1)}, bf16[256,512]{1,0:T(8,128)(2,1)S(1)}, u32[]{:S(2)}, u32[]{:S(2)}) collective-permute-start(bf16[256,512]{1,0:T(8,128)(2,1)S(1)} %stack.21.stack_own), channel_id=1, source_target_pairs={{2,4},{6,8},{10,12},{14,16},{18,20},{22,24},{26,28},{30,32},{34,36... | collective-permute-start | bytes 786440 | tf_op jit(solution)/shard_map/ppermute | solution.py:376
  12.7 4.5 %near.1 = (f32[1024,512]{1,0:T(8,128)S(1)}, bf16[1024,512]{1,0:T(8,128)(2,1)S(1)}, bf16[1024,512]{1,0:T(8,128)(2,1)S(1)}, bf16[1536,512]{1,0:T(8,128)(2,1)S(1)}, bf16[512,512]{1,0:T(8,128)(2,1)S(1)}) custom-call(s32[5]{0:T(128)S(1)} %stack.20.scalars, s32[1,1024]{1,0:T(1,128)} %bitcast.16, bf16[512,512]{1,0:T(8,128)(2,1)} %bitcast.25, ...), custom_call_target="tpu_custom_call" | custom-call | flops 1610612736 | bytes 9965588 | tf_op jit(solution)/shard_map/near/pallas_call | solution.py:92
  17.2 0.9 collective-permute-done.1.stack_second
  18.1 1.6 %collective-permute-done.stack_first = bf16[256,512]{1,0:T(8,128)(2,1)S(1)} collective-permute-done((bf16[256,512]{1,0:T(8,128)(2,1)S(1)}, bf16[256,512]{1,0:T(8,128)(2,1)S(1)}, u32[]{:S(2)}, u32[]{:S(2)}) %collective-permute-start) | collective-permute-done | bytes 262176 | tf_op jit(solution)/shard_map/ppermute | solution.py:376
  19.7 5.9 %edges.1 = (bf16[1040,512]{1,0:T(8,128)(2,1)S(1)}, f32[8,512]{1,0:T(8,128)S(1)}, bf16[1024,512]{1,0:T(8,128)(2,1)S(1)}, bf16[1024,512]{1,0:T(8,128)(2,1)S(1)}, b...) custom-call(s32[5]{0:T(128)S(1)} %stack.20.scalars, s32[1,1024]{1,0:T(1,128)S(1)} %bitcast.18, ...), custom_call_target="tpu_custom_call" | custom-call | flops 3758096384 | bytes 12359700 | tf_op jit(solution)/shard_map/edges/pallas_call | solution.py:92
  25.7 1.8 %kept.1 = f32[1024,512]{1,0:T(8,128)S(1)} custom-call(s32[5]{0:T(128)S(1)} %stack.20.scalars, bf16[1024,512]{1,0:T(8,128)(2,1)S(1)} %get-tuple-element.30.edge, bf16[1024,512]{1,0:T(8,128)(2,1)S(1)} %get-tuple-element.29.grid_picked, bf16[1024,512]{1,0:T(8,128)(2,1)S(1)} %get-tuple-element.34.mesh_picked, bf16[1024,512]{1,0:T(8,128)(2,1)S(1)} %get-tuple-element.35.hidden, ...), custom_call_target="tpu_custom_call" | custom-call | flops 1073741824 | bytes 8388628 | tf_op jit(solution)/shard_map/kept/pallas_call | solution.py:92
  27.5 0.8 collective-permute-done.2.got
  28.3 0.2 pack.1
  28.5 22.6 %all_to_all.10.shares = bf16[32,136,128]{2,1,0:T(8,128)(2,1)S(1)} all-to-all(bf16[32,136,128]{2,1,0:T(8,128)(2,1)S(1)} %pack.1), channel_id=1, replica_groups=mesh['band'=16,'hi'=4,'lo'=2,'rep'=2] {'band','lo'}, dimensions={0} | all-to-all | bytes 2228224 | tf_op jit(solution)/shard_map/all_to_all | solution.py:496
  51.2 0.2 group_sum.1.after.own
  51.4 5.2 %collective-permute-start.7 = (bf16[136,128]{1,0:T(8,128)(2,1)S(1)}, bf16[136,128]{1,0:T(8,128)(2,1)S(1)}, u32[]{:S(2)}, u32[]{:S(2)}) collective-permute-start(bf16[136,128]{1,0:T(8,128)(2,1)S(1)} %group_sum.1.after.own), channel_id=1, source_target_pairs={{0,12},{4,8},{12,0},{8,4},{1,13},{5,9},{13,1},{9,5},{2,14},{6,10},... | collective-permute-start | bytes 104456 | tf_op jit(solution)/shard_map/ppermute | solution.py:376
  56.6 0.3 collective-permute-start.6
  56.9 2.1 %collective-permute-start.5 = (bf16[136,128]{1,0:T(8,128)(2,1)S(1)}, bf16[136,128]{1,0:T(8,128)(2,1)S(1)}, u32[]{:S(2)}, u32[]{:S(2)}) collective-permute-start(bf16[136,128]{1,0:T(8,128)(2,1)S(1)} %group_sum.1.after.own), channel_id=1, source_target_pairs={{0,4},{8,12},{4,0},{12,8},{1,5},{9,13},{5,1},{13,9},{2,6},{10,14},... | collective-permute-start | bytes 104456 | tf_op jit(solution)/shard_map/ppermute | solution.py:376
  59.0 4.0 %nodes.1 = (bf16[1024,512]{1,0:T(8,128)(2,1)}, bf16[512,512]{1,0:T(8,128)(2,1)}, f32[128,512]{1,0:T(8,128)S(1)}, bf16[128,512]{1,0:T(8,128)(2,1)S(1)}, bf16[128,512]{1,0:T(8,128)(2,1)S(1)}) custom-call(s32[5]{0:T(128)S(1)} %stack.20.scalars, s32[1,1024]{1,0:T(1,128)S(1)} %bitcast.17, s32[1,1024]{1,0:T(1,128)S(1)} %bitcast.19, ...), custom_call_target="tpu_custom_call" | custom-call | flops 2147483648 | bytes 4761620 | tf_op jit(solution)/shard_map/nodes/pallas_call | solution.py:92
  63.0 1.6 %collective-permute-done.6.across = bf16[136,128]{1,0:T(8,128)(2,1)S(1)} collective-permute-done((bf16[136,128]{1,0:T(8,128)(2,1)S(1)}, bf16[136,128]{1,0:T(8,128)(2,1)S(1)}, u32[]{:S(2)}, u32[]{:S(2)}) %collective-permute-start.6) | collective-permute-done | bytes 34848 | tf_op jit(solution)/shard_map/ppermute | solution.py:376
  64.7 17.9 %all_to_all.11.shares = bf16[32,128,128]{2,1,0:T(8,128)(2,1)S(1)} all-to-all(bf16[32,128,128]{2,1,0:T(8,128)(2,1)S(1)} %get-tuple-element.44), channel_id=1, replica_groups=mesh['band'=16,'hi'=4,'lo'=2,'rep'=2] {'band','lo'}, dimensions={0} | all-to-all | bytes 2097152 | tf_op jit(solution)/shard_map/all_to_all | solution.py:534
  82.6 1.6 %collective-permute-start.3 = (bf16[128,512]{1,0:T(8,128)(2,1)S(1)}, bf16[128,512]{1,0:T(8,128)(2,1)S(1)}, u32[]{:S(2)}, u32[]{:S(2)}) collective-permute-start(bf16[128,512]{1,0:T(8,128)(2,1)S(1)} %get-tuple-element.41), channel_id=1, source_target_pairs={{0,2},{4,6},{8,10},{12,14},{16,18},{20,22},{24,26},{28,30},{32,34}... | collective-permute-start | bytes 393224 | tf_op jit(solution)/shard_map/ppermute | solution.py:376
  84.2 5.7 %collective-permute-start.4 = (bf16[128,512]{1,0:T(8,128)(2,1)S(1)}, bf16[128,512]{1,0:T(8,128)(2,1)S(1)}, u32[]{:S(2)}, u32[]{:S(2)}) collective-permute-start(bf16[128,512]{1,0:T(8,128)(2,1)S(1)} %get-tuple-element.42), channel_id=1, source_target_pairs={{2,4},{6,8},{10,12},{14,16},{18,20},{22,24},{26,28},{30,32},{34,36... | collective-permute-start | bytes 393224 | tf_op jit(solution)/shard_map/ppermute | solution.py:376
  90.0 0.6 slice.3
  90.5 5.4 %collective-permute-done.4 = bf16[128,512]{1,0:T(8,128)(2,1)S(1)} collective-permute-done((bf16[128,512]{1,0:T(8,128)(2,1)S(1)}, bf16[128,512]{1,0:T(8,128)(2,1)S(1)}, u32[]{:S(2)}, u32[]{:S(2)}) %collective-permute-start.4) | collective-permute-done | bytes 131104 | tf_op jit(solution)/shard_map/ppermute | solution.py:376
  95.9 0.8 add_bitcast_fusion
  96.7 1.9 %own_half.1 = (f32[1536,512]{1,0:T(8,128)}, f32[512,512]{1,0:T(8,128)}) custom-call(s32[5]{0:T(128)S(1)} %stack.20.scalars, bf16[32,128,128]{2,1,0:T(8,128)(2,1)S(1)} %all_to_all.11.shares), custom_call_target="tpu_custom_call" | custom-call | bytes 6291456 | tf_op jit(solution)/shard_map/own_half/pallas_call | solution.py:548
  98.7 1.9 %other_half.1 = (f32[1536,512]{1,0:T(8,128)}, f32[512,512]{1,0:T(8,128)}) custom-call(s32[5]{0:T(128)S(1)} %stack.20.scalars, bf16[32,128,128]{2,1,0:T(8,128)(2,1)S(1)} %collective-permute-done.8.shares, f32[1536,512]{1,0:T(8,128)} %get-tuple-element.45.first_in, f32[512,512]{1,0:T(8,128)} %get-tuple-element.46.second_in), custom_call_target="tpu_custom_call", output_to_operand_aliasing={{0}: (2, {}), {1}: (3, {})} | custom-call | bytes 6291456 | tf_op jit(solution)/shard_map/other_half/pallas_call | solution.py:549
  (15 shorter events, 0.4 us)
Async XLA Ops:
  1.6 16.5 %collective-permute-start.1 = (bf16[256,512]{1,0:T(8,128)(2,1)S(1)}, bf16[256,512]{1,0:T(8,128)(2,1)S(1)}, u32[]{:S(2)}, u32[]{:S(2)}) collective-permute-start(bf16[256,512]{1,0:T(8,128)(2,1)S(1)} %stack.21.stack_own), channel_id=1, source_target_pairs={{2,4},{6,8},{10,12},{14,16},{18,20},{22,24},{26,28},{30,32},{34,36... | collective-permute-start | bytes 786440 | tf_op jit(solution)/shard_map/ppermute | solution.py:376
  11.8 7.9 %collective-permute-start = (bf16[256,512]{1,0:T(8,128)(2,1)S(1)}, bf16[256,512]{1,0:T(8,128)(2,1)S(1)}, u32[]{:S(2)}, u32[]{:S(2)}) collective-permute-start(bf16[256,512]{1,0:T(8,128)(2,1)S(1)} %stack.21.stack_own), channel_id=1, source_target_pairs={{0,2},{4,6},{8,10},{12,14},{16,18},{20,22},{24,26},{28,30},{32,34}... | collective-permute-start | bytes 786440 | tf_op jit(solution)/shard_map/ppermute | solution.py:376
  12.7 7.0 %copy-start.1 = (s32[1024]{0:T(1024)S(1)}, s32[1024]{0:T(1024)}, u32[]{:S(2)}) copy-start(s32[1024]{0:T(1024)} %param.18) | copy-start | bytes 12292
  12.7 7.0 %copy-start.2 = (f32[512]{0:T(512)S(1)}, f32[512]{0:T(512)}, u32[]{:S(2)}) copy-start(f32[512]{0:T(512)} %param.16) | copy-start | bytes 6148
  25.6 2.8 %collective-permute-start.2 = (bf16[1040,512]{1,0:T(8,128)(2,1)S(1)}, bf16[1040,512]{1,0:T(8,128)(2,1)S(1)}, u32[]{:S(2)}, u32[]{:S(2)}) collective-permute-start(bf16[1040,512]{1,0:T(8,128)(2,1)S(1)} %get-tuple-element.37), channel_id=1, source_target_pairs={{0,1},{1,0},{2,3},{3,2},{4,5},{5,4},{6,7},{7,6},{8,9},{9,8},{10,11... | collective-permute-start | bytes 3194888 | tf_op jit(solution)/shard_map/ppermute | solution.py:376
  28.5 30.5 %copy-start = (s32[1024]{0:T(1024)S(1)}, s32[1024]{0:T(1024)}, u32[]{:S(2)}) copy-start(s32[1024]{0:T(1024)} %param.17) | copy-start | bytes 12292
  51.4 11.7 %collective-permute-start.7 = (bf16[136,128]{1,0:T(8,128)(2,1)S(1)}, bf16[136,128]{1,0:T(8,128)(2,1)S(1)}, u32[]{:S(2)}, u32[]{:S(2)}) collective-permute-start(bf16[136,128]{1,0:T(8,128)(2,1)S(1)} %group_sum.1.after.own), channel_id=1, source_target_pairs={{0,12},{4,8},{12,0},{8,4},{1,13},{5,9},{13,1},{9,5},{2,14},{6,10},... | collective-permute-start | bytes 104456 | tf_op jit(solution)/shard_map/ppermute | solution.py:376
  56.6 8.0 %collective-permute-start.6 = (bf16[136,128]{1,0:T(8,128)(2,1)S(1)}, bf16[136,128]{1,0:T(8,128)(2,1)S(1)}, u32[]{:S(2)}, u32[]{:S(2)}) collective-permute-start(bf16[136,128]{1,0:T(8,128)(2,1)S(1)} %group_sum.1.after.own), channel_id=1, source_target_pairs={{0,8},{4,12},{8,0},{12,4},{1,9},{5,13},{9,1},{13,5},{2,10},{6,14},... | collective-permute-start | bytes 104456 | tf_op jit(solution)/shard_map/ppermute | solution.py:376
  56.9 7.7 %collective-permute-start.5 = (bf16[136,128]{1,0:T(8,128)(2,1)S(1)}, bf16[136,128]{1,0:T(8,128)(2,1)S(1)}, u32[]{:S(2)}, u32[]{:S(2)}) collective-permute-start(bf16[136,128]{1,0:T(8,128)(2,1)S(1)} %group_sum.1.after.own), channel_id=1, source_target_pairs={{0,4},{8,12},{4,0},{12,8},{1,5},{9,13},{5,1},{13,9},{2,6},{10,14},... | collective-permute-start | bytes 104456 | tf_op jit(solution)/shard_map/ppermute | solution.py:376
  82.6 16.0 %collective-permute-start.8 = (bf16[32,128,128]{2,1,0:T(8,128)(2,1)S(1)}, bf16[32,128,128]{2,1,0:T(8,128)(2,1)S(1)}, u32[]{:S(2)}, u32[]{:S(2)}) collective-permute-start(bf16[32,128,128]{2,1,0:T(8,128)(2,1)S(1)} %all_to_all.11.shares), channel_id=1, source_target_pairs={{0,1},{1,0},{2,3},{3,2},{4,5},{5,4},{6,7},{7,6},{8,9},{9,8},{10,11... | collective-permute-start | bytes 3145736 | tf_op jit(solution)/shard_map/ppermute | solution.py:376
  82.6 7.9 %collective-permute-start.3 = (bf16[128,512]{1,0:T(8,128)(2,1)S(1)}, bf16[128,512]{1,0:T(8,128)(2,1)S(1)}, u32[]{:S(2)}, u32[]{:S(2)}) collective-permute-start(bf16[128,512]{1,0:T(8,128)(2,1)S(1)} %get-tuple-element.41), channel_id=1, source_target_pairs={{0,2},{4,6},{8,10},{12,14},{16,18},{20,22},{24,26},{28,30},{32,34}... | collective-permute-start | bytes 393224 | tf_op jit(solution)/shard_map/ppermute | solution.py:376
  84.2 11.7 %collective-permute-start.4 = (bf16[128,512]{1,0:T(8,128)(2,1)S(1)}, bf16[128,512]{1,0:T(8,128)(2,1)S(1)}, u32[]{:S(2)}, u32[]{:S(2)}) collective-permute-start(bf16[128,512]{1,0:T(8,128)(2,1)S(1)} %get-tuple-element.42), channel_id=1, source_target_pairs={{2,4},{6,8},{10,12},{14,16},{18,20},{22,24},{26,28},{30,32},{34,36... | collective-permute-start | bytes 393224 | tf_op jit(solution)/shard_map/ppermute | solution.py:376

commit v12 on v8

--- a/solution.py
+++ b/solution.py
@@ -281,8 +281,8 @@
     packed[...] = jnp.concatenate([total[:data], gain], axis=0).astype(jnp.bfloat16)
 
 
-def whole_sum_kernel(factor, own, near, across, far, after, copies, gain_grad):
-    own, near, across, far = [part[...].astype(jnp.float32) for part in (own, near, across, far)]
+def whole_sum_kernel(factor, own, near, far, across, after, copies, gain_grad):
+    own, near, far, across = [part[...].astype(jnp.float32) for part in (own, near, far, across)]
     total = ((own + across) + (near + far)) * factor
     data = copies.shape[1]
     gain_grad[...] = jnp.broadcast_to(gain_of(total[data:]), gain_grad.shape)
@@ -522,7 +522,7 @@
     )
     turns = [
         swap_pairs(packed, "hi", pairs)
-        for pairs in ([(0, 1), (2, 3)], [(0, 2), (1, 3)], [(0, 3), (1, 2)])
+        for pairs in ([(0, 1), (2, 3)], [(0, 3), (1, 2)], [(0, 2), (1, 3)])
     ]
     copies, gain_grad = call(
         functools.partial(whole_sum_kernel, factor),

time: 94.7 us -> 91.9 us (0.970)
  waiting for transfers between devices: 16.7 us -> 13.8 us
    ppermute x9, waiting for transfers between devices: 5.71 us -> 2.81 us  [swap_pairs(): return lax.ppermute(value, axis, pairs + [(d, s) for s, d in pairs])]
  transfers between devices with their start and end apart: 10 -> 10, of which waited for: 4 -> 6; matrix products, arithmetic and copies ran while one was open for 1% -> 1% of each run, Pallas kernels for 13% -> 14%
where the time goes in v12:
time: 91.9 us; the launch traced here: 91.6 us
  starting transfers between devices  30.1 us (33%)
  Pallas kernels  22.5 us (24%)
  blocking collectives  21.4 us (23%)
  waiting for transfers between devices  13.8 us (15%)
  local copies, waits for them, and re-layouts  2.09 us (2%)
  between operations  1.6 us (2%)
    all_to_all x1, blocking collectives, per_device(): total = lax.all_to_all(copies, GROUP, 0, 0)  21.4 us
    ppermute x9, starting transfers between devices, swap_pairs(): return lax.ppermute(value, axis, pairs + [(d, s) for s, d in pairs])  19 us
    pallas_call x8, Pallas kernels, call(): pl.pallas_call(kernel, out_shape=outs, in_specs=specs, out_specs=[in_vmem...  18.7 us
    all_to_all x1, starting transfers between devices, per_device(): shares = lax.all_to_all(packed, GROUP, 0, 0)  11.1 us
    all_to_all x1, waiting for transfers between devices, per_device(): shares = lax.all_to_all(packed, GROUP, 0, 0)  11 us
    ppermute x9, waiting for transfers between devices, swap_pairs(): return lax.ppermute(value, axis, pairs + [(d, s) for s, d in pairs])  2.81 us
    pallas_call x1, Pallas kernels, per_device(): halves(other_half_kernel, in_specs=[in_smem(), in_vmem()] + [in_hbm()] *...  1.94 us
    pallas_call x1, Pallas kernels, per_device(): halves(own_half_kernel, in_specs=[in_smem(), in_vmem()], name='own_half')  1.93 us
  transfers between devices with their start and end apart: 10, of which 6 were waited for; matrix products, arithmetic and copies ran while one was open for 1% of the time, Pallas kernels for 14%

profile of v12, /device:TPU:1, one launch (start us, length us, event | category | flops | bytes accessed | tf_op | source)
XLA Modules:
  0.0 91.6 jit_solution(10406793550824018568)
XLA Ops:
  0.6 1.0 %stack.21.stack_own = bf16[256,512]{1,0:T(8,128)(2,1)S(1)} custom-call(bf16[128,512]{1,0:T(8,128)(2,1)} %bitcast.21, bf16[128,512]{1,0:T(8,128)(2,1)} %bitcast.22), custom_call_target="tpu_custom_call" | custom-call | bytes 524288 | tf_op jit(solution)/shard_map/stack/pallas_call | solution.py:92
  1.6 0.7 collective-permute-start.1
  2.3 5.4 %collective-permute-start = (bf16[256,512]{1,0:T(8,128)(2,1)S(1)}, bf16[256,512]{1,0:T(8,128)(2,1)S(1)}, u32[]{:S(2)}, u32[]{:S(2)}) collective-permute-start(bf16[256,512]{1,0:T(8,128)(2,1)S(1)} %stack.21.stack_own), channel_id=1, source_target_pairs={{0,2},{4,6},{8,10},{12,14},{16,18},{20,22},{24,26},{28,30},{32,34}... | collective-permute-start | bytes 786440 | tf_op jit(solution)/shard_map/ppermute | solution.py:377
  8.5 4.5 %near.1 = (f32[1024,512]{1,0:T(8,128)S(1)}, bf16[1024,512]{1,0:T(8,128)(2,1)S(1)}, bf16[1024,512]{1,0:T(8,128)(2,1)S(1)}, bf16[1536,512]{1,0:T(8,128)(2,1)S(1)}, bf16[512,512]{1,0:T(8,128)(2,1)S(1)}) custom-call(s32[5]{0:T(128)S(1)} %stack.20.scalars, s32[1,1024]{1,0:T(1,128)} %bitcast.16, bf16[512,512]{1,0:T(8,128)(2,1)} %bitcast.25, ...), custom_call_target="tpu_custom_call" | custom-call | flops 1610612736 | bytes 9965588 | tf_op jit(solution)/shard_map/near/pallas_call | solution.py:92
  13.5 5.9 %edges.1 = (bf16[1040,512]{1,0:T(8,128)(2,1)S(1)}, f32[8,512]{1,0:T(8,128)S(1)}, bf16[1024,512]{1,0:T(8,128)(2,1)S(1)}, bf16[1024,512]{1,0:T(8,128)(2,1)S(1)}, b...) custom-call(s32[5]{0:T(128)S(1)} %stack.20.scalars, s32[1,1024]{1,0:T(1,128)S(1)} %bitcast.18, ...), custom_call_target="tpu_custom_call" | custom-call | flops 3758096384 | bytes 12359700 | tf_op jit(solution)/shard_map/edges/pallas_call | solution.py:92
  19.4 1.6 %collective-permute-start.2 = (bf16[1040,512]{1,0:T(8,128)(2,1)S(1)}, bf16[1040,512]{1,0:T(8,128)(2,1)S(1)}, u32[]{:S(2)}, u32[]{:S(2)}) collective-permute-start(bf16[1040,512]{1,0:T(8,128)(2,1)S(1)} %get-tuple-element.39), channel_id=1, source_target_pairs={{0,1},{1,0},{2,3},{3,2},{4,5},{5,4},{6,7},{7,6},{8,9},{9,8},{10,11... | collective-permute-start | bytes 3194888 | tf_op jit(solution)/shard_map/ppermute | solution.py:377
  21.0 1.8 %kept.1 = f32[1024,512]{1,0:T(8,128)S(1)} custom-call(s32[5]{0:T(128)S(1)} %stack.20.scalars, bf16[1024,512]{1,0:T(8,128)(2,1)S(1)} %get-tuple-element.32.edge, bf16[1024,512]{1,0:T(8,128)(2,1)S(1)} %get-tuple-element.31.grid_picked, bf16[1024,512]{1,0:T(8,128)(2,1)S(1)} %get-tuple-element.36.mesh_picked, bf16[1024,512]{1,0:T(8,128)(2,1)S(1)} %get-tuple-element.37.hidden, ...), custom_call_target="tpu_custom_call" | custom-call | flops 1073741824 | bytes 8388628 | tf_op jit(solution)/shard_map/kept/pallas_call | solution.py:92
  22.8 0.5 collective-permute-done.2.got
  23.3 1.2 %pack.1 = (bf16[32,136,128]{2,1,0:T(8,128)(2,1)}, f32[8,128]{1,0:T(8,128)S(1)}) custom-call(f32[1024,512]{1,0:T(8,128)S(1)} %kept.1, bf16[1040,512]{1,0:T(8,128)(2,1)S(1)} %collective-permute-done.2.got, f32[8,512]{1,0:T(8,128)S(1)} %get-tuple-element.40.gain_term), custom_call_target="tpu_custom_call" | custom-call | bytes 4296704 | tf_op jit(solution)/shard_map/pack/pallas_call | solution.py:92
  24.5 11.1 %all-to-all-start = ((bf16[32,136,128]{2,1,0:T(8,128)(2,1)}), bf16[32,136,128]{2,1,0:T(8,128)(2,1)S(1)}, u32[]{:S(2)}, u32[]{:S(2)}) async-start(bf16[32,136,128]{2,1,0:T(8,128)(2,1)} %get-tuple-element.47), calls=%async_computation | async-start | bytes 2228224 | tf_op jit(solution)/shard_map/all_to_all | solution.py:514
  35.7 1.4 %copy-done.5 = bf16[1536,512]{1,0:T(8,128)(2,1)S(1)} copy-done((bf16[1536,512]{1,0:T(8,128)(2,1)S(1)}, bf16[1536,512]{1,0:T(8,128)(2,1)}, u32[]{:S(2)}) %copy-start.5) | copy-done | bytes 1572888
  37.1 4.0 %nodes.1 = (bf16[1024,512]{1,0:T(8,128)(2,1)}, bf16[512,512]{1,0:T(8,128)(2,1)}, f32[128,512]{1,0:T(8,128)S(1)}, bf16[128,512]{1,0:T(8,128)(2,1)S(1)}, bf16[128,512]{1,0:T(8,128)(2,1)S(1)}) custom-call(s32[5]{0:T(128)S(1)} %stack.20.scalars, s32[1,1024]{1,0:T(1,128)S(1)} %bitcast.17, s32[1,1024]{1,0:T(1,128)S(1)} %bitcast.19, ...), custom_call_target="tpu_custom_call" | custom-call | flops 2147483648 | bytes 4730900 | tf_op jit(solution)/shard_map/nodes/pallas_call | solution.py:92
  41.0 1.1 %collective-permute-start.3 = (bf16[128,512]{1,0:T(8,128)(2,1)S(1)}, bf16[128,512]{1,0:T(8,128)(2,1)S(1)}, u32[]{:S(2)}, u32[]{:S(2)}) collective-permute-start(bf16[128,512]{1,0:T(8,128)(2,1)S(1)} %get-tuple-element.44), channel_id=1, source_target_pairs={{0,2},{4,6},{8,10},{12,14},{16,18},{20,22},{24,26},{28,30},{32,34}... | collective-permute-start | bytes 393224 | tf_op jit(solution)/shard_map/ppermute | solution.py:377
  42.1 0.7 collective-permute-start.4
  42.8 11.0 %all-to-all-done.shares = bf16[32,136,128]{2,1,0:T(8,128)(2,1)S(1)} async-done(((bf16[32,136,128]{2,1,0:T(8,128)(2,1)}), bf16[32,136,128]{2,1,0:T(8,128)(2,1)S(1)}, u32[]{:S(2)}, u32[]{:S(2)}) %all-to-all-start) | async-done | bytes 1114144 | tf_op jit(solution)/shard_map/all_to_all | solution.py:514
  53.9 2.1 %collective-permute-start.7 = (bf16[136,128]{1,0:T(8,128)(2,1)S(1)}, bf16[136,128]{1,0:T(8,128)(2,1)S(1)}, u32[]{:S(2)}, u32[]{:S(2)}) collective-permute-start(bf16[136,128]{1,0:T(8,128)(2,1)S(1)} %group_sum.1.own), channel_id=1, source_target_pairs={{0,8},{4,12},{8,0},{12,4},{1,9},{5,13},{9,1},{13,5},{2,10},{6,14},... | collective-permute-start | bytes 104456 | tf_op jit(solution)/shard_map/ppermute | solution.py:377
  56.0 2.4 %collective-permute-start.6 = (bf16[136,128]{1,0:T(8,128)(2,1)S(1)}, bf16[136,128]{1,0:T(8,128)(2,1)S(1)}, u32[]{:S(2)}, u32[]{:S(2)}) collective-permute-start(bf16[136,128]{1,0:T(8,128)(2,1)S(1)} %group_sum.1.own), channel_id=1, source_target_pairs={{0,12},{4,8},{12,0},{8,4},{1,13},{5,9},{13,1},{9,5},{2,14},{6,10},... | collective-permute-start | bytes 104456 | tf_op jit(solution)/shard_map/ppermute | solution.py:377
  58.4 2.0 %collective-permute-start.5 = (bf16[136,128]{1,0:T(8,128)(2,1)S(1)}, bf16[136,128]{1,0:T(8,128)(2,1)S(1)}, u32[]{:S(2)}, u32[]{:S(2)}) collective-permute-start(bf16[136,128]{1,0:T(8,128)(2,1)S(1)} %group_sum.1.own), channel_id=1, source_target_pairs={{0,4},{8,12},{4,0},{12,8},{1,5},{9,13},{5,1},{13,9},{2,6},{10,14},... | collective-permute-start | bytes 104456 | tf_op jit(solution)/shard_map/ppermute | solution.py:377
  61.0 1.3 %collective-permute-done.5.near = bf16[136,128]{1,0:T(8,128)(2,1)S(1)} collective-permute-done((bf16[136,128]{1,0:T(8,128)(2,1)S(1)}, bf16[136,128]{1,0:T(8,128)(2,1)S(1)}, u32[]{:S(2)}, u32[]{:S(2)}) %collective-permute-start.5) | collective-permute-done | bytes 34848 | tf_op jit(solution)/shard_map/ppermute | solution.py:377
  62.4 21.4 %all_to_all.10.shares = bf16[32,128,128]{2,1,0:T(8,128)(2,1)S(1)} all-to-all(bf16[32,128,128]{2,1,0:T(8,128)(2,1)S(1)} %get-tuple-element.48), channel_id=1, replica_groups=mesh['band'=16,'hi'=4,'lo'=2,'rep'=2] {'band','lo'}, dimensions={0} | all-to-all | bytes 2097152 | tf_op jit(solution)/shard_map/all_to_all | solution.py:535
  83.8 3.1 %collective-permute-start.8 = (bf16[32,128,128]{2,1,0:T(8,128)(2,1)S(1)}, bf16[32,128,128]{2,1,0:T(8,128)(2,1)S(1)}, u32[]{:S(2)}, u32[]{:S(2)}) collective-permute-start(bf16[32,128,128]{2,1,0:T(8,128)(2,1)S(1)} %all_to_all.10.shares), channel_id=1, source_target_pairs={{0,1},{1,0},{2,3},{3,2},{4,5},{5,4},{6,7},{7,6},{8,9},{9,8},{10,11... | collective-permute-start | bytes 3145736 | tf_op jit(solution)/shard_map/ppermute | solution.py:377
  86.9 0.6 slice.3
  87.5 1.9 %own_half.1 = (f32[1536,512]{1,0:T(8,128)}, f32[512,512]{1,0:T(8,128)}) custom-call(s32[5]{0:T(128)S(1)} %stack.20.scalars, bf16[32,128,128]{2,1,0:T(8,128)(2,1)S(1)} %all_to_all.10.shares), custom_call_target="tpu_custom_call" | custom-call | bytes 6291456 | tf_op jit(solution)/shard_map/own_half/pallas_call | solution.py:549
  89.5 1.9 %other_half.1 = (f32[1536,512]{1,0:T(8,128)}, f32[512,512]{1,0:T(8,128)}) custom-call(s32[5]{0:T(128)S(1)} %stack.20.scalars, bf16[32,128,128]{2,1,0:T(8,128)(2,1)S(1)} %collective-permute-done.8.shares, f32[1536,512]{1,0:T(8,128)} %get-tuple-element.49.first_in, f32[512,512]{1,0:T(8,128)} %get-tuple-element.50.second_in), custom_call_target="tpu_custom_call", output_to_operand_aliasing={{0}: (2, {}), {1}: (3, {})} | custom-call | bytes 6291456 | tf_op jit(solution)/shard_map/other_half/pallas_call | solution.py:550
  (22 shorter events, 1.5 us)
Async XLA Ops:
  1.6 11.4 %collective-permute-start.1 = (bf16[256,512]{1,0:T(8,128)(2,1)S(1)}, bf16[256,512]{1,0:T(8,128)(2,1)S(1)}, u32[]{:S(2)}, u32[]{:S(2)}) collective-permute-start(bf16[256,512]{1,0:T(8,128)(2,1)S(1)} %stack.21.stack_own), channel_id=1, source_target_pairs={{2,4},{6,8},{10,12},{14,16},{18,20},{22,24},{26,28},{30,32},{34,36... | collective-permute-start | bytes 786440 | tf_op jit(solution)/shard_map/ppermute | solution.py:377
  2.3 11.1 %collective-permute-start = (bf16[256,512]{1,0:T(8,128)(2,1)S(1)}, bf16[256,512]{1,0:T(8,128)(2,1)S(1)}, u32[]{:S(2)}, u32[]{:S(2)}) collective-permute-start(bf16[256,512]{1,0:T(8,128)(2,1)S(1)} %stack.21.stack_own), channel_id=1, source_target_pairs={{0,2},{4,6},{8,10},{12,14},{16,18},{20,22},{24,26},{28,30},{32,34}... | collective-permute-start | bytes 786440 | tf_op jit(solution)/shard_map/ppermute | solution.py:377
  8.5 5.0 %copy-start.2 = (s32[1024]{0:T(1024)S(1)}, s32[1024]{0:T(1024)}, u32[]{:S(2)}) copy-start(s32[1024]{0:T(1024)} %param.18) | copy-start | bytes 12292
  8.5 5.0 %copy-start.3 = (f32[512]{0:T(512)S(1)}, f32[512]{0:T(512)}, u32[]{:S(2)}) copy-start(f32[512]{0:T(512)} %param.16) | copy-start | bytes 6148
  13.0 6.4 %copy-start.4 = (bf16[1536,512]{1,0:T(8,128)(2,1)}, bf16[1536,512]{1,0:T(8,128)(2,1)S(1)}, u32[]{:S(2)}) copy-start(bf16[1536,512]{1,0:T(8,128)(2,1)S(1)} %get-tuple-element.33.w_first) | copy-start | bytes 4718596
  19.4 3.9 %collective-permute-start.2 = (bf16[1040,512]{1,0:T(8,128)(2,1)S(1)}, bf16[1040,512]{1,0:T(8,128)(2,1)S(1)}, u32[]{:S(2)}, u32[]{:S(2)}) collective-permute-start(bf16[1040,512]{1,0:T(8,128)(2,1)S(1)} %get-tuple-element.39), channel_id=1, source_target_pairs={{0,1},{1,0},{2,3},{3,2},{4,5},{5,4},{6,7},{7,6},{8,9},{9,8},{10,11... | collective-permute-start | bytes 3194888 | tf_op jit(solution)/shard_map/ppermute | solution.py:377
  24.5 11.1 %copy-start.1 = (s32[1024]{0:T(1024)S(1)}, s32[1024]{0:T(1024)}, u32[]{:S(2)}) copy-start(s32[1024]{0:T(1024)} %param.17) | copy-start | bytes 12292
  24.5 29.2 %all-to-all-start = ((bf16[32,136,128]{2,1,0:T(8,128)(2,1)}), bf16[32,136,128]{2,1,0:T(8,128)(2,1)S(1)}, u32[]{:S(2)}, u32[]{:S(2)}) async-start(bf16[32,136,128]{2,1,0:T(8,128)(2,1)} %get-tuple-element.47), calls=%async_computation | async-start | bytes 2228224 | tf_op jit(solution)/shard_map/all_to_all | solution.py:514
  35.7 1.4 %copy-start.5 = (bf16[1536,512]{1,0:T(8,128)(2,1)S(1)}, bf16[1536,512]{1,0:T(8,128)(2,1)}, u32[]{:S(2)}) copy-start(bf16[1536,512]{1,0:T(8,128)(2,1)} %copy-done.4) | copy-start | bytes 4718596
  41.0 19.3 %collective-permute-start.3 = (bf16[128,512]{1,0:T(8,128)(2,1)S(1)}, bf16[128,512]{1,0:T(8,128)(2,1)S(1)}, u32[]{:S(2)}, u32[]{:S(2)}) collective-permute-start(bf16[128,512]{1,0:T(8,128)(2,1)S(1)} %get-tuple-element.44), channel_id=1, source_target_pairs={{0,2},{4,6},{8,10},{12,14},{16,18},{20,22},{24,26},{28,30},{32,34}... | collective-permute-start | bytes 393224 | tf_op jit(solution)/shard_map/ppermute | solution.py:377
  42.1 18.3 %collective-permute-start.4 = (bf16[128,512]{1,0:T(8,128)(2,1)S(1)}, bf16[128,512]{1,0:T(8,128)(2,1)S(1)}, u32[]{:S(2)}, u32[]{:S(2)}) collective-permute-start(bf16[128,512]{1,0:T(8,128)(2,1)S(1)} %get-tuple-element.45), channel_id=1, source_target_pairs={{2,4},{6,8},{10,12},{14,16},{18,20},{22,24},{26,28},{30,32},{34,36... | collective-permute-start | bytes 393224 | tf_op jit(solution)/shard_map/ppermute | solution.py:377
  53.9 6.8 %collective-permute-start.7 = (bf16[136,128]{1,0:T(8,128)(2,1)S(1)}, bf16[136,128]{1,0:T(8,128)(2,1)S(1)}, u32[]{:S(2)}, u32[]{:S(2)}) collective-permute-start(bf16[136,128]{1,0:T(8,128)(2,1)S(1)} %group_sum.1.own), channel_id=1, source_target_pairs={{0,8},{4,12},{8,0},{12,4},{1,9},{5,13},{9,1},{13,5},{2,10},{6,14},... | collective-permute-start | bytes 104456 | tf_op jit(solution)/shard_map/ppermute | solution.py:377
  56.0 5.1 %collective-permute-start.6 = (bf16[136,128]{1,0:T(8,128)(2,1)S(1)}, bf16[136,128]{1,0:T(8,128)(2,1)S(1)}, u32[]{:S(2)}, u32[]{:S(2)}) collective-permute-start(bf16[136,128]{1,0:T(8,128)(2,1)S(1)} %group_sum.1.own), channel_id=1, source_target_pairs={{0,12},{4,8},{12,0},{8,4},{1,13},{5,9},{13,1},{9,5},{2,14},{6,10},... | collective-permute-start | bytes 104456 | tf_op jit(solution)/shard_map/ppermute | solution.py:377
  58.4 4.0 %collective-permute-start.5 = (bf16[136,128]{1,0:T(8,128)(2,1)S(1)}, bf16[136,128]{1,0:T(8,128)(2,1)S(1)}, u32[]{:S(2)}, u32[]{:S(2)}) collective-permute-start(bf16[136,128]{1,0:T(8,128)(2,1)S(1)} %group_sum.1.own), channel_id=1, source_target_pairs={{0,4},{8,12},{4,0},{12,8},{1,5},{9,13},{5,1},{13,9},{2,6},{10,14},... | collective-permute-start | bytes 104456 | tf_op jit(solution)/shard_map/ppermute | solution.py:377
  60.4 29.0 %copy-start = (f32[128,512]{1,0:T(8,128)}, f32[128,512]{1,0:T(8,128)S(1)}, u32[]{:S(2)}) copy-start(f32[128,512]{1,0:T(8,128)S(1)} %convert_add_fusion.after) | copy-start | bytes 786436
  83.8 5.6 %collective-permute-start.8 = (bf16[32,128,128]{2,1,0:T(8,128)(2,1)S(1)}, bf16[32,128,128]{2,1,0:T(8,128)(2,1)S(1)}, u32[]{:S(2)}, u32[]{:S(2)}) collective-permute-start(bf16[32,128,128]{2,1,0:T(8,128)(2,1)S(1)} %all_to_all.10.shares), channel_id=1, source_target_pairs={{0,1},{1,0},{2,3},{3,2},{4,5},{5,4},{6,7},{7,6},{8,9},{9,8},{10,11... | collective-permute-start | bytes 3145736 | tf_op jit(solution)/shard_map/ppermute | solution.py:377
